TPU v7x, 256 devices: a whole 4x4x8 slice. The times are simulated.
256 devices in a mesh: group: 8 (over x, z_lo), view: 8 (over z_hi, core), tok: 4 (over y).
Axes of the slice: x: 4, y: 4, z: 8 (z_hi: 4, z_lo: 2; z = z_hi * 2 + z_lo), core: 2. Of those that a mesh axis runs over, the one named last changes fastest.
Arguments:
- tokens: bfloat16 [65536, 768], P(('group', 'view', 'tok')), may hold values from -6 to 6
- self_gain: float32 [768], replicated, may hold values from 0.5 to 1.5
- self_shift: float32 [768], replicated, may hold values from -3 to 3
- query_gain: float32 [768], replicated, may hold values from 0.5 to 1.5
- query_shift: float32 [768], replicated, may hold values from -3 to 3
- memory_gain: float32 [768], replicated, may hold values from 0.5 to 1.5
- memory_shift: float32 [768], replicated, may hold values from -3 to 3
- self_query: bfloat16 [768, 768], replicated
- self_key: bfloat16 [768, 768], replicated
- self_value: bfloat16 [768, 768], replicated, may hold values from -0.21875 to 0.21875
- self_output: bfloat16 [768, 768], replicated, may hold values from -0.21875 to 0.21875
- cross_query: bfloat16 [768, 768], replicated
- cross_key: bfloat16 [768, 768], replicated
- cross_value: bfloat16 [768, 768], replicated, may hold values from -0.21875 to 0.21875
- cross_output: bfloat16 [768, 768], replicated, may hold values from -0.21875 to 0.21875
- partner: int32 [64], replicated, may hold values from 0 to 63, as said below
- camera_rows: int32 [8, 16], replicated, may hold values from 0 to 8191, as said below
Outputs:
- mixed: float32 [65536, 768], P(('group', 'view', 'tok'))
Inputs may be any that keep to these rules, and one draw needn't show every extreme that they name: partner[i] is never i. `camera_rows`: the c-th row number of a group lies in c * 512 to (c + 1) * 512 - 1.
All inputs are finite; a program needn't handle non-finite values.
Results may differ from a plain program's by a relative error of at most 0.0065.
The roundings to bfloat16 on the way count: a program that leaves them out, or rounds other values in their place, can miss the bound.
Values may be sent and summed in bfloat16 or wider, within the bound.
No kernel may reach another device: no remote copies, remote signals or barrier semaphores. Data moves between devices by JAX's collectives and lax.ppermute only.
A program may use at most 128 MiB of HBM per device.

v0:
```python
import jax
import jax.numpy as jnp
from jax import lax
from jax.sharding import PartitionSpec as P

HEADS = 12
HDIM = 64


def normalize(values, gain, shift):
    wide = values.astype(jnp.float32)
    center = jnp.mean(wide, axis=-1, keepdims=True)
    spread = jnp.mean((wide - center) ** 2, axis=-1, keepdims=True)
    return ((wide - center) * lax.rsqrt(spread + 1e-06) * gain + shift).astype(jnp.bfloat16)


def project(left, weight):
    return jnp.dot(left, weight, preferred_element_type=jnp.float32).astype(jnp.bfloat16)


def attend(queries, keys, values):
    qh = queries.reshape(queries.shape[0], HEADS, HDIM)
    kh = keys.reshape(keys.shape[0], HEADS, HDIM)
    vh = values.reshape(values.shape[0], HEADS, HDIM)
    scores = jnp.einsum("qhd,khd->hqk", qh, kh, preferred_element_type=jnp.float32)
    scores = scores / jnp.sqrt(jnp.float32(HDIM))
    weights = jax.nn.softmax(scores, axis=-1).astype(jnp.bfloat16)
    context = jnp.einsum("hqk,khd->qhd", weights, vh, preferred_element_type=jnp.float32)
    return context.reshape(queries.shape[0], HEADS * HDIM)


def route_keys(keys, values, partner):
    count = lax.axis_size(("group", "view"))
    rows = keys.shape[0]
    width = keys.shape[1]
    shaped = (
        keys.reshape(count, rows // count, width),
        values.reshape(count, rows // count, width),
    )
    first_k, first_v = (
        lax.all_to_all(shaped[0], ("group", "view"), split_axis=0, concat_axis=0, tiled=True),
        lax.all_to_all(shaped[1], ("group", "view"), split_axis=0, concat_axis=0, tiled=True),
    )
    onward_k = jnp.take(first_k, partner, axis=0)
    onward_v = jnp.take(first_v, partner, axis=0)
    final_k, final_v = (
        lax.all_to_all(onward_k, ("group", "view"), split_axis=0, concat_axis=0, tiled=True),
        lax.all_to_all(onward_v, ("group", "view"), split_axis=0, concat_axis=0, tiled=True),
    )
    return (final_k.reshape(rows, width), final_v.reshape(rows, width))


def local(
    tokens,
    self_gain,
    self_shift,
    query_gain,
    query_shift,
    memory_gain,
    memory_shift,
    self_query,
    self_key,
    self_value,
    self_output,
    cross_query,
    cross_key,
    cross_value,
    cross_output,
    partner,
    camera_rows,
):
    rows = tokens.shape[0]
    hidden = normalize(tokens, self_gain, self_shift)
    sq = project(hidden, self_query)
    sk = project(hidden, self_key)
    sv = project(hidden, self_value)
    view_k, view_v = (
        lax.all_gather(sk, "tok", axis=0, tiled=True),
        lax.all_gather(sv, "tok", axis=0, tiled=True),
    )
    self_ctx = attend(sq, view_k, view_v).astype(jnp.bfloat16)
    memory = normalize(tokens, memory_gain, memory_shift)
    own_k = project(memory, cross_key)
    own_v = project(memory, cross_value)
    part_k, part_v = route_keys(own_k, own_v, partner)
    whole_k, whole_v = (
        lax.all_gather(part_k, "tok", axis=0, tiled=True),
        lax.all_gather(part_v, "tok", axis=0, tiled=True),
    )
    my_group = lax.axis_index("group")
    within = lax.axis_index(("view", "tok"))
    row_ids = within * rows + jnp.arange(rows, dtype=jnp.int32)
    my_cams = lax.dynamic_index_in_dim(camera_rows, my_group, 0, keepdims=False)
    selector = (my_cams[:, None] == row_ids[None, :]).astype(jnp.bfloat16)
    picked = jnp.dot(selector, tokens, preferred_element_type=jnp.float32)
    group_cams = lax.psum(picked.astype(jnp.bfloat16), ("view", "tok"))
    cams = lax.all_gather(group_cams, "group", axis=0, tiled=True)
    cam_memory = normalize(cams, memory_gain, memory_shift)
    camk = project(cam_memory, cross_key)
    camv = project(cam_memory, cross_value)
    cq = project(normalize(tokens, query_gain, query_shift), cross_query)
    cross_ctx = (attend(cq, whole_k, whole_v) + attend(cq, camk, camv)).astype(jnp.bfloat16)
    self_term = jnp.dot(self_ctx, self_output, preferred_element_type=jnp.float32)
    cross_term = jnp.dot(cross_ctx, cross_output, preferred_element_type=jnp.float32)
    return tokens.astype(jnp.float32) + self_term + cross_term


def solution(mesh):
    placed = (
        P(("group", "view", "tok"), None),
        P(),
        P(),
        P(),
        P(),
        P(),
        P(),
        P(),
        P(),
        P(),
        P(),
        P(),
        P(),
        P(),
        P(),
        P(),
        P(),
    )
    return jax.shard_map(
        local,
        mesh=mesh,
        in_specs=placed,
        out_specs=P(("group", "view", "tok"), None),
        check_vma=False,
    )
```

profile of v0, /device:TPU:2, one launch (start us, length us, event | category | flops | bytes accessed | tf_op | source)
XLA Modules:
  0.0 329.9 jit_solution(9722589945073748899)
XLA Ops:
  6.5 1.2 convert_reduce_fusion
  7.8 1.2 fusion.32
  9.1 2.8 convolution_convert_fusion.3
  11.9 1.9 convolution_convert_fusion.2
  13.8 0.8 reshape.93
  14.7 12.0 %all-to-all-start = ((bf16[64,4,768]{2,1,0:T(4,128)(2,1)}), bf16[64,4,768]{2,1,0:T(4,128)(2,1)S(1)}, u32[]{:S(2)}, u32[]{:S(2)}) async-start(bf16[64,4,768]{2,1,0:T(4,128)(2,1)} %reshape.93), calls=%async_computation | async-start | bytes 786432 | tf_op jit(solution)/shard_map/all_to_all | solution.py:42
  26.8 1.3 convolution_convert_fusion.5
  29.6 12.2 %all-to-all-done = bf16[64,4,768]{2,1,0:T(4,128)(2,1)S(1)} async-done(((bf16[64,4,768]{2,1,0:T(4,128)(2,1)}), bf16[64,4,768]{2,1,0:T(4,128)(2,1)S(1)}, u32[]{:S(2)}, u32[]{:S(2)}) %all-to-all-start) | async-done | bytes 393248 | tf_op jit(solution)/shard_map/all_to_all | solution.py:42
  41.8 5.7 %all-to-all-start.2 = ((bf16[64,4,768]{2,1,0:T(4,128)(2,1)}), bf16[64,4,768]{2,1,0:T(4,128)(2,1)S(1)}, u32[]{:S(2)}, u32[]{:S(2)}) async-start(bf16[64,4,768]{2,1,0:T(4,128)(2,1)} %reshape.97), calls=%async_computation.2 | async-start | bytes 786432 | tf_op jit(solution)/shard_map/all_to_all | solution.py:41
  47.6 0.9 gather_fusion
  48.6 14.1 %all-to-all-done.2 = bf16[64,4,768]{2,1,0:T(4,128)(2,1)S(1)} async-done(((bf16[64,4,768]{2,1,0:T(4,128)(2,1)}), bf16[64,4,768]{2,1,0:T(4,128)(2,1)S(1)}, u32[]{:S(2)}, u32[]{:S(2)}) %all-to-all-start.2) | async-done | bytes 393248 | tf_op jit(solution)/shard_map/all_to_all | solution.py:41
  62.6 0.9 gather_fusion.1
  63.5 1.2 broadcast_select_fusion
  64.7 20.7 %all_to_all.20 = bf16[64,4,768]{2,1,0:T(4,128)(2,1)S(1)} all-to-all(bf16[64,4,768]{2,1,0:T(4,128)(2,1)S(1)} %get-tuple-element.6), channel_id=1, replica_groups=mesh['group'=8,'view'=8,'tok'=4] {'group','view'}, dimensions={0} | all-to-all | bytes 786432 | tf_op jit(solution)/shard_map/all_to_all | solution.py:47
  85.6 0.9 copy.33
  88.2 141.2 %psum.7 = bf16[16,768]{1,0:T(8,128)(2,1)S(1)} all-reduce(bf16[16,768]{1,0:T(8,128)(2,1)S(1)} %convolution_convert_fusion.8), channel_id=1, replica_groups=mesh['group'=8,'view'=8,'tok'=4] {'view','tok'}, use_global_device_ids=true, to_apply=%region_6.0 | all-reduce | flops 12288 | bytes 49152 | tf_op jit(solution)/shard_map/psum | solution.py:96
  229.4 27.9 %all_gather.19 = bf16[128,768]{1,0:T(8,128)(2,1)S(1)} all-gather(bf16[16,768]{1,0:T(8,128)(2,1)S(1)} %psum.7), channel_id=1, replica_groups=mesh['group'=8,'view'=8,'tok'=4] {'group'}, dimensions={0}, use_global_device_ids=true | all-gather | bytes 221184 | tf_op jit(solution)/shard_map/all_gather | solution.py:97
  258.3 8.8 %all-to-all-start.1 = ((bf16[64,4,768]{2,1,0:T(4,128)(2,1)}), bf16[64,4,768]{2,1,0:T(4,128)(2,1)S(1)}, u32[]{:S(2)}, u32[]{:S(2)}) async-start(bf16[64,4,768]{2,1,0:T(4,128)(2,1)} %get-tuple-element.7), calls=%async_computation.1 | async-start | bytes 786432 | tf_op jit(solution)/shard_map/all_to_all | solution.py:48
  267.2 1.6 convolution_convert_fusion.7
  269.7 1.8 convolution_convert_fusion.4
  271.5 0.9 copy.29
  272.4 2.4 fusion.60
  274.8 7.4 %all-to-all-done.1 = bf16[64,4,768]{2,1,0:T(4,128)(2,1)S(1)} async-done(((bf16[64,4,768]{2,1,0:T(4,128)(2,1)}), bf16[64,4,768]{2,1,0:T(4,128)(2,1)S(1)}, u32[]{:S(2)}, u32[]{:S(2)}) %all-to-all-start.1) | async-done | bytes 393248 | tf_op jit(solution)/shard_map/all_to_all | solution.py:48
  282.3 0.9 copy.31
  283.3 1.9 copy.30
  285.2 10.0 %fusion.58 = (f32[12,256]{1,0:T(8,128)}, f32[12,256,1024]{2,1,0:T(8,128)}) fusion(bf16[256,12,64]{0,2,1:T(8,128)(2,1)} %bitcast.47, bf16[1024,12,64]{0,2,1:T(8,128)(2,1)S(1)} %bitcast.42), kind=kOutput, calls=%fused_computation.81 | convolution fusion | flops 412091392 | bytes 14561280 | tf_op jit(solution)/shard_map/sub | solution.py:27
  295.2 1.7 copy.28
  296.9 7.0 %fusion.19 = bf16[12,64,256]{2,1,0:T(8,128)(2,1)S(1)} fusion(bf16[1024,12,64]{0,2,1:T(8,128)(2,1)S(1)} %bitcast.43, f32[12,256,1024]{2,1,0:T(8,128)} %get-tuple-element.9, f32[12,256]{1,0:T(8,128)} %get-tuple-element.8), kind=kOutput, calls=%fused_computation.26 | convolution fusion | flops 409141248 | bytes 14561280 | tf_op jit(solution)/shard_map/hqk,khd->qhd/dot_general | solution.py:28
  304.4 9.8 %fusion.59 = (f32[12,256]{1,0:T(8,128)S(1)}, f32[12,256,1024]{2,1,0:T(8,128)}) fusion(bf16[256,12,64]{0,2,1:T(8,128)(2,1)S(1)} %bitcast.46, bf16[1024,12,64]{0,2,1:T(8,128)(2,1)} %bitcast.51), kind=kOutput, calls=%fused_computation.82 | convolution fusion | flops 412091392 | bytes 14561280 | tf_op jit(solution)/shard_map/sub | solution.py:27
  314.2 6.5 %fusion.12 = f32[12,64,256]{2,1,0:T(8,128)S(1)} fusion(bf16[1024,12,64]{0,2,1:T(8,128)(2,1)} %bitcast.52, f32[12,256,1024]{2,1,0:T(8,128)} %get-tuple-element.11, f32[12,256]{1,0:T(8,128)S(1)} %get-tuple-element.10), kind=kOutput, calls=%fused_computation.16 | convolution fusion | flops 408944640 | bytes 14954496 | tf_op jit(solution)/shard_map/hqk,khd->qhd/dot_general | solution.py:28
  321.0 1.0 copy-done.2
  322.0 1.4 convolution_add_fusion.1
  (74 shorter events, 6.1 us)
Async XLA Ops:
  6.5 21.6 %copy-start = (bf16[768,768]{1,0:T(8,128)(2,1)S(1)}, bf16[768,768]{1,0:T(8,128)(2,1)}, u32[]{:S(2)}) copy-start(bf16[768,768]{1,0:T(8,128)(2,1)} %param.31) | copy-start | bytes 3538948
  6.5 276.8 %all-gather.7.cloned.1.call-start = ((), (), s32[]{:S(2)}) async-start(), calls=%async_computation.5 | async-start | bytes 1966080 | tf_op jit(solution)/shard_map/all_gather | solution.py:78
  9.0 2.8 copy-start.1
  9.0 2.8 copy-start.9
  9.0 2.8 copy-start.11
  11.9 14.9 %copy-start.5 = (bf16[768,768]{1,0:T(8,128)(2,1)S(1)}, bf16[768,768]{1,0:T(8,128)(2,1)}, u32[]{:S(2)}) copy-start(bf16[768,768]{1,0:T(8,128)(2,1)} %param.28) | copy-start | bytes 3538948
  11.9 14.9 %copy-start.13 = (f32[768]{0:T(1024)S(1)}, f32[768]{0:T(1024)}, u32[]{:S(2)}) copy-start(f32[768]{0:T(1024)} %param.21) | copy-start | bytes 9220
  11.9 14.9 %copy-start.15 = (f32[768]{0:T(1024)S(1)}, f32[768]{0:T(1024)}, u32[]{:S(2)}) copy-start(f32[768]{0:T(1024)} %param.20) | copy-start | bytes 9220
  14.7 27.1 %all-to-all-start = ((bf16[64,4,768]{2,1,0:T(4,128)(2,1)}), bf16[64,4,768]{2,1,0:T(4,128)(2,1)S(1)}, u32[]{:S(2)}, u32[]{:S(2)}) async-start(bf16[64,4,768]{2,1,0:T(4,128)(2,1)} %reshape.93), calls=%async_computation | async-start | bytes 786432 | tf_op jit(solution)/shard_map/all_to_all | solution.py:42
  26.7 268.5 %all-gather.5.cloned.1.call-start = ((), (), s32[]{:S(2)}) async-start(), calls=%async_computation.4 | async-start | bytes 1966080 | tf_op jit(solution)/shard_map/all_gather | solution.py:79
  28.1 19.4 %copy-start.17 = (s32[64]{0:T(128)S(1)}, s32[64]{0:T(128)}, u32[]{:S(2)}) copy-start(s32[64]{0:T(128)} %param.34) | copy-start | bytes 772
  41.8 20.8 %all-to-all-start.2 = ((bf16[64,4,768]{2,1,0:T(4,128)(2,1)}), bf16[64,4,768]{2,1,0:T(4,128)(2,1)S(1)}, u32[]{:S(2)}, u32[]{:S(2)}) async-start(bf16[64,4,768]{2,1,0:T(4,128)(2,1)} %reshape.97), calls=%async_computation.2 | async-start | bytes 786432 | tf_op jit(solution)/shard_map/all_to_all | solution.py:41
  47.5 256.9 %all-gather.11.cloned.1.call-start = ((), (), s32[]{:S(2)}) async-start(), calls=%async_computation.7 | async-start | bytes 1966080 | tf_op jit(solution)/shard_map/all_gather | solution.py:87
  64.7 21.8 %copy-start.6 = (bf16[768,768]{1,0:T(8,128)(2,1)S(1)}, bf16[768,768]{1,0:T(8,128)(2,1)}, u32[]{:S(2)}) copy-start(bf16[768,768]{1,0:T(8,128)(2,1)} %param.30) | copy-start | bytes 3538948
  64.7 21.8 %copy-start.7 = (f32[768]{0:T(1024)S(1)}, f32[768]{0:T(1024)}, u32[]{:S(2)}) copy-start(f32[768]{0:T(1024)} %param.23) | copy-start | bytes 9220
  64.7 21.8 %copy-start.8 = (f32[768]{0:T(1024)S(1)}, f32[768]{0:T(1024)}, u32[]{:S(2)}) copy-start(f32[768]{0:T(1024)} %param.22) | copy-start | bytes 9220
  87.1 170.6 %copy-start.10 = (f32[768]{0:T(1024)S(1)}, f32[768]{0:T(1024)}, u32[]{:S(2)}) copy-start(f32[768]{0:T(1024)} %param.25) | copy-start | bytes 9220
  87.1 170.6 %copy-start.12 = (f32[768]{0:T(1024)S(1)}, f32[768]{0:T(1024)}, u32[]{:S(2)}) copy-start(f32[768]{0:T(1024)} %param.24) | copy-start | bytes 9220
  258.1 11.5 %copy-start.14 = (f32[768]{0:T(1024)S(1)}, f32[768]{0:T(1024)}, u32[]{:S(2)}) copy-start(f32[768]{0:T(1024)} %param.21) | copy-start | bytes 9220
  258.1 11.5 %copy-start.16 = (f32[768]{0:T(1024)S(1)}, f32[768]{0:T(1024)}, u32[]{:S(2)}) copy-start(f32[768]{0:T(1024)} %param.20) | copy-start | bytes 9220
  258.3 23.9 %all-to-all-start.1 = ((bf16[64,4,768]{2,1,0:T(4,128)(2,1)}), bf16[64,4,768]{2,1,0:T(4,128)(2,1)S(1)}, u32[]{:S(2)}, u32[]{:S(2)}) async-start(bf16[64,4,768]{2,1,0:T(4,128)(2,1)} %get-tuple-element.7), calls=%async_computation.1 | async-start | bytes 786432 | tf_op jit(solution)/shard_map/all_to_all | solution.py:48
  267.1 47.1 %all-gather.9.cloned.1.call-start = ((), (), s32[]{:S(2)}) async-start(), calls=%async_computation.6 | async-start | bytes 1966080 | tf_op jit(solution)/shard_map/all_gather | solution.py:88
  296.9 7.0 %copy-start.3 = (bf16[768,768]{1,0:T(8,128)(2,1)S(1)}, bf16[768,768]{1,0:T(8,128)(2,1)}, u32[]{:S(2)}) copy-start(bf16[768,768]{1,0:T(8,128)(2,1)} %param.29) | copy-start | bytes 3538948
  314.2 6.5 %copy-start.4 = (bf16[128,768]{0,1:T(8,128)(2,1)S(1)}, bf16[128,768]{0,1:T(8,128)(2,1)}, u32[]{:S(2)}) copy-start(bf16[128,768]{0,1:T(8,128)(2,1)} %copy.34) | copy-start | bytes 589828
  314.2 6.5 %copy-start.18 = (f32[12,256,128]{1,2,0:T(8,128)S(1)}, f32[12,256,128]{1,2,0:T(8,128)}, u32[]{:S(2)}) copy-start(f32[12,256,128]{1,2,0:T(8,128)} %get-tuple-element.13) | copy-start | bytes 4718596
  314.2 6.5 %copy-start.19 = (f32[12,256]{1,0:T(8,128)S(1)}, f32[12,256]{1,0:T(8,128)}, u32[]{:S(2)}) copy-start(f32[12,256]{1,0:T(8,128)} %get-tuple-element.12) | copy-start | bytes 36868
  320.7 1.3 copy-start.2
Sparse Core Ops, SparseCore 0:
  12.0 32.0 all-gather.6
  45.9 29.1 all-gather.4
  86.6 29.7 all-gather.10
  283.4 26.7 all-gather.8
where the time goes:
time: 332 us; the launch traced here: 330 us
  blocking collectives  190 us (57%)
  matrix products  48.9 us (15%)
  waiting for transfers between devices  33.8 us (10%)
  starting transfers between devices  26.7 us (8%)
  between operations  13.6 us (4%)
  local copies, waits for them, and re-layouts  13 us (4%)
  other arithmetic  4 us (1%)
    psum x1, blocking collectives, local(): group_cams = lax.psum(picked.astype(jnp.bfloat16), ('view', 'tok'))  141 us
    all_gather x1, blocking collectives, local(): cams = lax.all_gather(group_cams, 'group', axis=0, tiled=True)  27.9 us
    sub x3, matrix products, attend(): weights = jax.nn.softmax(scores, axis=-1).astype(jnp.bfloat16)  22.1 us
    all_to_all x1, blocking collectives, route_keys(): lax.all_to_all(onward_k, ('group', 'view'), split_axis=0, concat_axis=0,...  20.7 us
    all_to_all x1, waiting for transfers between devices, route_keys(): lax.all_to_all(shaped[0], ('group', 'view'), split_axis=0, concat_axis=0,...  14.1 us
    dot_general x3, matrix products, attend(): jnp.einsum('hqk,khd->qhd', weights, vh, preferred_element_type=jnp.float32)  13.7 us
    all_to_all x1, waiting for transfers between devices, route_keys(): lax.all_to_all(shaped[1], ('group', 'view'), split_axis=0, concat_axis=0,...  12.2 us
    all_to_all x1, starting transfers between devices, route_keys(): lax.all_to_all(shaped[1], ('group', 'view'), split_axis=0, concat_axis=0,...  12 us
  transfers between devices with their start and end apart: 7, of which 3 were waited for; matrix products, arithmetic and copies ran while one was open for 16% of the time, Pallas kernels for 0%

commit v1 on v0

v1 whole, which is shorter than its diff:
```python
import functools

import jax
import jax.numpy as jnp
from jax import lax
from jax.experimental import pallas as pl
from jax.experimental.pallas import tpu as pltpu
from jax.sharding import Mesh, PartitionSpec as P

D = 768
HDIM = 64
COLS = 256
STEPS = D // COLS
ROUTE = ("core", "zh", "zl", "x")
ROWS = 256
PIECES = 64
VIEW = 1024


def norm(wide, gain, shift):
    center = jnp.mean(wide, axis=-1, keepdims=True)
    spread = jnp.mean((wide - center) ** 2, axis=-1, keepdims=True)
    return ((wide - center) * lax.rsqrt(spread + 1e-06) * gain + shift).astype(jnp.bfloat16)


def mm(left, right):
    return lax.dot_general(left, right, (((1,), (0,)), ((), ())), preferred_element_type=jnp.float32)


def mm_nt(left, right):
    return lax.dot_general(left, right, (((1,), (1,)), ((), ())), preferred_element_type=jnp.float32)


def attend(q, k, v):
    lane = lax.broadcasted_iota(jnp.int32, q.shape, 1) // HDIM
    out = None
    for head in range(COLS // HDIM):
        mine = lane == head
        s = mm_nt(jnp.where(mine, q, jnp.zeros_like(q)), k)
        p = jnp.exp(s - jnp.max(s, axis=-1, keepdims=True))
        total = jnp.sum(p, axis=-1, keepdims=True)
        c = mm(p.astype(jnp.bfloat16), v) / total
        out = c if out is None else jnp.where(mine, c, out)
    return out


def unpack(ref):
    wide = ref[...].astype(jnp.float32).reshape(PIECES // 2, 2, 8, D // 2)
    return jnp.concatenate(
        [wide[:, 0].reshape(ROWS, D // 2), wide[:, 1].reshape(ROWS, D // 2)], axis=1
    )


def pack_kernel(pos, cams, x_ref, o_ref):
    group, view, tok = pos[0], pos[1], pos[2]
    row = cams[group, 2 * view + tok // 2] - (view * VIEW + tok * ROWS)
    x = x_ref[...]
    pick = (lax.broadcasted_iota(jnp.int32, (8, ROWS), 1) == row).astype(jnp.bfloat16)
    cam = mm(pick, x)
    sub = lax.broadcasted_iota(jnp.int32, (8, 128), 0)
    extra = jnp.zeros((8, 128), jnp.float32)
    for r in range(D // 128):
        extra = jnp.where(sub == r, cam[:, 128 * r : 128 * (r + 1)], extra)
    wide = x.astype(jnp.float32)
    left = wide[:, : D // 2].reshape(PIECES // 2, 1, 8, D // 2)
    right = wide[:, D // 2 :].reshape(PIECES // 2, 1, 8, D // 2)
    both = jnp.concatenate([left, right], axis=1).reshape(PIECES, 8, D // 2)
    o_ref[:, :, : D // 2] = both.astype(jnp.bfloat16)
    o_ref[:, :, D // 2 :] = jnp.broadcast_to(extra[None], (PIECES, 8, 128)).astype(jnp.bfloat16)


def select_kernel(partner, r_ref, o_ref, c_ref):
    for slot in range(PIECES):
        core, zh, zl, x = slot // 32, slot // 8 % 4, slot // 4 % 2, slot % 4
        p = partner[((x * 2 + zl) * 4 + zh) * 2 + core]
        src = (p % 2) * 32 + (p // 2 % 4) * 8 + (p // 8 % 2) * 4 + p // 16
        o_ref[slot] = r_ref[src, :, : D // 2]
    c_ref[...] = r_ref[:, :, D // 2 :]


def self_kernel(x0, x1, x2, x3, gain, shift, wq, wk, wv, wo, o_ref, h_ref):
    step = pl.program_id(0)

    @pl.when(step == 0)
    def _():
        for i, ref in enumerate((x0, x1, x2, x3)):
            h_ref[i * ROWS : (i + 1) * ROWS] = norm(ref[...].astype(jnp.float32), gain[...], shift[...])
        o_ref[...] = x0[...].astype(jnp.float32)

    h = h_ref[...]
    k = mm(h, wk[...]).astype(jnp.bfloat16)
    v = mm(h, wv[...]).astype(jnp.bfloat16)
    q = mm(h[:ROWS], wq[...]).astype(jnp.bfloat16) * jnp.bfloat16(0.125)
    o_ref[...] += mm(attend(q, k, v).astype(jnp.bfloat16), wo[...])


def prep_kernel(x0, cams, qgain, qshift, mgain, mshift, wq, wk, wv, q_ref, c_ref, h_ref, m_ref):
    step = pl.program_id(0)

    @pl.when(step == 0)
    def _():
        h_ref[...] = norm(x0[...].astype(jnp.float32), qgain[...], qshift[...])
        m_ref[...] = norm(cams[...].astype(jnp.float32), mgain[...], mshift[...])

    m = m_ref[...]
    k = mm(m, wk[...]).astype(jnp.bfloat16)
    v = mm(m, wv[...]).astype(jnp.bfloat16)
    q = mm(h_ref[...], wq[...]).astype(jnp.bfloat16) * jnp.bfloat16(0.125)
    q_ref[...] = q
    c_ref[...] = attend(q, k, v)


def cross_kernel(y0, y1, y2, y3, gain, shift, wk, wv, wo, q_ref, c_ref, b_ref, o_ref, m_ref):
    step = pl.program_id(0)

    @pl.when(step == 0)
    def _():
        for i, ref in enumerate((y0, y1, y2, y3)):
            m_ref[i * ROWS : (i + 1) * ROWS] = norm(unpack(ref), gain[...], shift[...])
        o_ref[...] = b_ref[...]

    m = m_ref[...]
    k = mm(m, wk[...]).astype(jnp.bfloat16)
    v = mm(m, wv[...]).astype(jnp.bfloat16)
    ctx = attend(q_ref[...], k, v) + c_ref[...]
    o_ref[...] += mm(ctx.astype(jnp.bfloat16), wo[...])


def full(shape):
    return pl.BlockSpec(shape, lambda i: (0,) * len(shape))


WCOL = pl.BlockSpec((D, COLS), lambda i: (0, i))
WROW = pl.BlockSpec((COLS, D), lambda i: (i, 0))
XCOL = pl.BlockSpec((ROWS, COLS), lambda i: (0, i))
VEC = full((1, D))
X = full((ROWS, D))
PIECE = full((PIECES, 8, D // 2))
PARAMS = pltpu.CompilerParams(
    dimension_semantics=("arbitrary",), vmem_limit_bytes=32 * 1024 * 1024
)


def cost(keys, rows_kv):
    return pl.CostEstimate(
        flops=2 * D * D * (2 * rows_kv + 2 * ROWS) + 16 * ROWS * keys * D,
        bytes_accessed=8 * D * D,
        transcendentals=ROWS * keys * 12,
    )


def call_self(x0, x1, x2, x3, *rest):
    return pl.pallas_call(
        self_kernel,
        grid=(STEPS,),
        in_specs=[X] * 4 + [VEC] * 2 + [WCOL] * 3 + [WROW],
        out_specs=X,
        out_shape=jax.ShapeDtypeStruct((ROWS, D), jnp.float32),
        scratch_shapes=[pltpu.VMEM((VIEW, D), jnp.bfloat16)],
        compiler_params=PARAMS,
        cost_estimate=cost(VIEW, VIEW),
        name="self_attention",
    )(x0, x1, x2, x3, *rest)


def call_prep(x0, cams, *rest):
    return pl.pallas_call(
        prep_kernel,
        grid=(STEPS,),
        in_specs=[X, full((128, D))] + [VEC] * 4 + [WCOL] * 3,
        out_specs=[XCOL, XCOL],
        out_shape=[
            jax.ShapeDtypeStruct((ROWS, D), jnp.bfloat16),
            jax.ShapeDtypeStruct((ROWS, D), jnp.float32),
        ],
        scratch_shapes=[pltpu.VMEM((ROWS, D), jnp.bfloat16), pltpu.VMEM((128, D), jnp.bfloat16)],
        compiler_params=PARAMS,
        cost_estimate=cost(128, 128),
        name="camera_attention",
    )(x0, cams, *rest)


def call_cross(y0, y1, y2, y3, *rest):
    return pl.pallas_call(
        cross_kernel,
        grid=(STEPS,),
        in_specs=[PIECE] * 4 + [VEC] * 2 + [WCOL] * 2 + [WROW, XCOL, XCOL, X],
        out_specs=X,
        out_shape=jax.ShapeDtypeStruct((ROWS, D), jnp.float32),
        scratch_shapes=[pltpu.VMEM((VIEW, D), jnp.bfloat16)],
        compiler_params=PARAMS,
        cost_estimate=cost(VIEW, VIEW),
        name="cross_attention",
    )(y0, y1, y2, y3, *rest)


def call_pack(pos, camera_rows, tokens):
    return pl.pallas_call(
        pack_kernel,
        grid_spec=pltpu.PrefetchScalarGridSpec(
            num_scalar_prefetch=2,
            grid=(1,),
            in_specs=[pl.BlockSpec((ROWS, D), lambda i, *_: (0, 0))],
            out_specs=pl.BlockSpec((PIECES, 8, 512), lambda i, *_: (0, 0, 0)),
        ),
        out_shape=jax.ShapeDtypeStruct((PIECES, 8, 512), jnp.bfloat16),
        name="pack_pieces",
    )(pos, camera_rows, tokens)


def call_select(partner, first):
    return pl.pallas_call(
        select_kernel,
        grid_spec=pltpu.PrefetchScalarGridSpec(
            num_scalar_prefetch=1,
            grid=(1,),
            in_specs=[pl.BlockSpec((PIECES, 8, 512), lambda i, *_: (0, 0, 0))],
            out_specs=[
                pl.BlockSpec((PIECES, 8, 384), lambda i, *_: (0, 0, 0)),
                pl.BlockSpec((PIECES, 8, 128), lambda i, *_: (0, 0, 0)),
            ],
        ),
        out_shape=[
            jax.ShapeDtypeStruct((PIECES, 8, 384), jnp.bfloat16),
            jax.ShapeDtypeStruct((PIECES, 8, 128), jnp.bfloat16),
        ],
        name="select_pieces",
    )(partner, first)


def around(value):
    return [
        lax.ppermute(value, "tok", [(i, (i + s) % 4) for i in range(4)]) for s in (1, 3, 2)
    ]


def local(
    tokens,
    self_gain,
    self_shift,
    query_gain,
    query_shift,
    memory_gain,
    memory_shift,
    self_query,
    self_key,
    self_value,
    self_output,
    cross_query,
    cross_key,
    cross_value,
    cross_output,
    partner,
    camera_rows,
):
    row = lambda v: v.reshape(1, D)
    group = lax.axis_index(("x", "zl"))
    view = lax.axis_index(("zh", "core"))
    tok = lax.axis_index("tok")
    pos = jnp.stack([group, view, tok]).astype(jnp.int32)

    packed = call_pack(pos, camera_rows, tokens)
    first = lax.all_to_all(packed, ROUTE, split_axis=0, concat_axis=0, tiled=True)
    onward, cam_own = call_select(partner, first)
    mine = lax.all_to_all(onward, ROUTE, split_axis=0, concat_axis=0, tiled=True)

    others = around(tokens)
    base = call_self(
        tokens, *others, row(self_gain), row(self_shift), self_query, self_key, self_value, self_output
    )

    cam_parts = [cam_own] + around(cam_own)
    halves = [tok // 2] + [((tok - s) % 4) // 2 for s in (1, 3, 2)]
    cams = jnp.concatenate(
        [
            sum(jnp.where(h == want, c, jnp.zeros_like(c)) for h, c in zip(halves, cam_parts))
            for want in (0, 1)
        ],
        axis=0,
    )
    cams = cams[:, :6].reshape(128, D)
    cq, cam_ctx = call_prep(
        tokens,
        cams,
        row(query_gain),
        row(query_shift),
        row(memory_gain),
        row(memory_shift),
        cross_query,
        cross_key,
        cross_value,
    )
    theirs = around(mine)
    return call_cross(
        mine,
        *theirs,
        row(memory_gain),
        row(memory_shift),
        cross_key,
        cross_value,
        cross_output,
        cq,
        cam_ctx,
        base,
    )


def solution(mesh):
    split = Mesh(mesh.devices.reshape(4, 2, 4, 2, 4), ("x", "zl", "zh", "core", "tok"))
    rows = P(("x", "zl", "zh", "core", "tok"), None)
    return jax.shard_map(
        local, mesh=split, in_specs=(rows,) + (P(),) * 16, out_specs=rows, check_vma=False
    )
```

time: 332 us -> 96.6 us (0.29)
  blocking collectives: 190 us -> 0 us
  matrix products: 48.9 us -> 0 us
  Pallas kernels: 0 us -> 33.1 us
  waiting for transfers between devices: 33.8 us -> 16.8 us
  between operations: 13.6 us -> 0.4 us
  starting transfers between devices: 26.7 us -> 33.7 us
  local copies, waits for them, and re-layouts: 13 us -> 8.74 us
    psum x1 -> x0, blocking collectives: 141 us -> none  [local(): group_cams = lax.psum(picked.astype(jnp.bfloat16), ('view', 'tok'))]
    pallas_call x0 -> x5, Pallas kernels: none -> 33.1 us  [the longest x1 11.8 us: call_self(): pl.pallas_call(self_kernel, grid=(STEPS,), in_specs=[X] * 4 + [VEC] * 2 +...]
    all_gather x1 -> x0, blocking collectives: 27.9 us -> none  [local(): cams = lax.all_gather(group_cams, 'group', axis=0, tiled=True)]
    dot_general x14 -> x0, matrix products: 26.8 us -> none  [the longest x3 13.7 us: attend(): jnp.einsum('hqk,khd->qhd', weights, vh, preferred_element_type=jnp.float32)]
    all_to_all x3 -> x2, waiting for transfers between devices: 33.7 us -> 10.5 us  [the longest x1 10.5 us: local(): lax.all_to_all(packed, ROUTE, split_axis=0, concat_axis=0, tiled=True)]
    sub x3 -> x0, matrix products: 22.1 us -> none  [attend(): weights = jax.nn.softmax(scores, axis=-1).astype(jnp.bfloat16)]
    all_to_all x1 -> x0, blocking collectives: 20.7 us -> none  [route_keys(): lax.all_to_all(onward_k, ('group', 'view'), split_axis=0, concat_axis=0,...]
    ppermute x0 -> x9, starting transfers between devices: none -> 14 us  [around(): lax.ppermute(value, 'tok', [(i, (i + s) % 4) for i in range(4)])]
  transfers between devices with their start and end apart: 7 -> 11, of which waited for: 3 -> 3; matrix products, arithmetic and copies ran while one was open for 16% -> 3% of each run, Pallas kernels for 0% -> 21%
where the time goes in v1:
time: 96.6 us; the launch traced here: 95.2 us
  starting transfers between devices  33.7 us (35%)
  Pallas kernels  33.1 us (34%)
  waiting for transfers between devices  16.8 us (17%)
  local copies, waits for them, and re-layouts  8.74 us (9%)
  other arithmetic  2.46 us (3%)
    ppermute x9, starting transfers between devices, around(): lax.ppermute(value, 'tok', [(i, (i + s) % 4) for i in range(4)])  14 us
    all_to_all x1, starting transfers between devices, local(): lax.all_to_all(packed, ROUTE, split_axis=0, concat_axis=0, tiled=True)  12.2 us
    pallas_call x1, Pallas kernels, call_self(): pl.pallas_call(self_kernel, grid=(STEPS,), in_specs=[X] * 4 + [VEC] * 2 +...  11.8 us
    pallas_call x1, Pallas kernels, call_cross(): pl.pallas_call(cross_kernel, grid=(STEPS,), in_specs=[PIECE] * 4 + [VEC]...  10.8 us
    all_to_all x1, waiting for transfers between devices, local(): lax.all_to_all(packed, ROUTE, split_axis=0, concat_axis=0, tiled=True)  10.5 us
    all_to_all x1, starting transfers between devices, local(): lax.all_to_all(onward, ROUTE, split_axis=0, concat_axis=0, tiled=True)  7.55 us
    unnamed x40, local copies, waits for them, and re-layouts  7.43 us
    ppermute x9, waiting for transfers between devices, around(): lax.ppermute(value, 'tok', [(i, (i + s) % 4) for i in range(4)])  6.33 us
  transfers between devices with their start and end apart: 11, of which 3 were waited for; matrix products, arithmetic and copies ran while one was open for 3% of the time, Pallas kernels for 21%

profile of v1, /device:TPU:2, one launch (start us, length us, event | category | flops | bytes accessed | tf_op | source)
XLA Modules:
  0.0 95.2 jit_solution(2210199543754721888)
XLA Ops:
  0.0 0.7 pad_add_fusion.pos
  0.7 2.7 %pack_pieces.1 = bf16[64,8,512]{2,1,0:T(8,128)(2,1)} custom-call(s32[3]{0:T(128)} %pad_add_fusion.pos, s32[8,16]{1,0:T(8,128)} %cams.1, bf16[256,768]{1,0:T(8,128)(2,1)} %x0.3), custom_call_target="tpu_custom_call" | custom-call | tf_op jit(solution)/shard_map/pack_pieces/pallas_call | solution.py:198
  3.4 0.0 copy-start.19
  3.4 0.0 copy-start.1
  3.4 12.2 %all-to-all-start = ((bf16[64,8,512]{2,1,0:T(8,128)(2,1)}), bf16[64,8,512]{2,1,0:T(8,128)(2,1)S(1)}, u32[]{:S(2)}, u32[]{:S(2)}) async-start(bf16[64,8,512]{2,1,0:T(8,128)(2,1)} %pack_pieces.1), calls=%async_computation | async-start | bytes 1048576 | tf_op jit(solution)/shard_map/all_to_all | solution.py:263
  15.6 3.1 %collective-permute-start.7 = (bf16[256,768]{1,0:T(8,128)(2,1)S(1)}, bf16[256,768]{1,0:T(8,128)(2,1)}, u32[]{:S(2)}, u32[]{:S(2)}) collective-permute-start(bf16[256,768]{1,0:T(8,128)(2,1)S(1)} %copy-done), channel_id=1, source_target_pairs={{0,3},{1,0},{2,1},{3,2},{4,7},{5,4},{6,5},{7,6},{8,11},{9,8},{10,9... | collective-permute-start | bytes 1179656 | tf_op jit(solution)/shard_map/ppermute | solution.py:233
  18.7 2.2 %collective-permute-start.8 = (bf16[256,768]{1,0:T(8,128)(2,1)S(1)}, bf16[256,768]{1,0:T(8,128)(2,1)}, u32[]{:S(2)}, u32[]{:S(2)}) collective-permute-start(bf16[256,768]{1,0:T(8,128)(2,1)S(1)} %copy-done), channel_id=1, source_target_pairs={{0,2},{1,3},{2,0},{3,1},{4,6},{5,7},{6,4},{7,5},{8,10},{9,11},{10,... | collective-permute-start | bytes 1179656 | tf_op jit(solution)/shard_map/ppermute | solution.py:233
  20.9 10.5 %all-to-all-done.r_ref = bf16[64,8,512]{2,1,0:T(8,128)(2,1)S(1)} async-done(((bf16[64,8,512]{2,1,0:T(8,128)(2,1)}), bf16[64,8,512]{2,1,0:T(8,128)(2,1)S(1)}, u32[]{:S(2)}, u32[]{:S(2)}) %all-to-all-start) | async-done | bytes 524320 | tf_op jit(solution)/shard_map/all_to_all | solution.py:263
  31.4 0.8 copy-done.11
  32.2 3.5 %select_pieces.1 = (bf16[64,8,384]{2,1,0:T(8,128)(2,1)}, bf16[64,8,128]{2,1,0:T(8,128)(2,1)}) custom-call(s32[64]{0:T(128)} %partner.1, bf16[64,8,512]{2,1,0:T(8,128)(2,1)} %copy-done.11), custom_call_target="tpu_custom_call" | custom-call | tf_op jit(solution)/shard_map/select_pieces/pallas_call | solution.py:212
  35.7 7.5 %all-to-all-start.1 = ((bf16[64,8,384]{2,1,0:T(8,128)(2,1)}), bf16[64,8,384]{2,1,0:T(8,128)(2,1)S(1)}, u32[]{:S(2)}, u32[]{:S(2)}) async-start(bf16[64,8,384]{2,1,0:T(8,128)(2,1)} %get-tuple-element.9), calls=%async_computation.1 | async-start | bytes 786432 | tf_op jit(solution)/shard_map/all_to_all | solution.py:265
  43.5 3.3 %collective-permute-start.5 = (bf16[64,8,128]{2,1,0:T(8,128)(2,1)}, bf16[64,8,128]{2,1,0:T(8,128)(2,1)}, u32[]{:S(2)}, u32[]{:S(2)}) collective-permute-start(bf16[64,8,128]{2,1,0:T(8,128)(2,1)} %get-tuple-element.10), channel_id=1, source_target_pairs={{0,2},{1,3},{2,0},{3,1},{4,6},{5,7},{6,4},{7,5},{8,10},{9,11},{10,... | collective-permute-start | bytes 393224 | tf_op jit(solution)/shard_map/ppermute | solution.py:233
  46.8 1.1 %collective-permute-start.4 = (bf16[64,8,128]{2,1,0:T(8,128)(2,1)}, bf16[64,8,128]{2,1,0:T(8,128)(2,1)S(1)}, u32[]{:S(2)}, u32[]{:S(2)}) collective-permute-start(bf16[64,8,128]{2,1,0:T(8,128)(2,1)} %get-tuple-element.10), channel_id=1, source_target_pairs={{0,3},{1,0},{2,1},{3,2},{4,7},{5,4},{6,5},{7,6},{8,11},{9,8},{10,9... | collective-permute-start | bytes 393224 | tf_op jit(solution)/shard_map/ppermute | solution.py:233
  47.9 1.0 %collective-permute-start.3 = (bf16[64,8,128]{2,1,0:T(8,128)(2,1)}, bf16[64,8,128]{2,1,0:T(8,128)(2,1)}, u32[]{:S(2)}, u32[]{:S(2)}) collective-permute-start(bf16[64,8,128]{2,1,0:T(8,128)(2,1)} %get-tuple-element.10), channel_id=1, source_target_pairs={{0,1},{1,2},{2,3},{3,0},{4,5},{5,6},{6,7},{7,4},{8,9},{9,10},{10,1... | collective-permute-start | bytes 393224 | tf_op jit(solution)/shard_map/ppermute | solution.py:233
  48.8 0.0 copy-start.3
  48.9 1.3 %copy-done.3 = bf16[768,768]{1,0:T(8,128)(2,1)S(1)} copy-done((bf16[768,768]{1,0:T(8,128)(2,1)S(1)}, bf16[768,768]{1,0:T(8,128)(2,1)}, u32[]{:S(2)}) %copy-start.3) | copy-done | bytes 1179672
  50.1 1.3 %copy-done.4 = bf16[768,768]{1,0:T(8,128)(2,1)S(1)} copy-done((bf16[768,768]{1,0:T(8,128)(2,1)S(1)}, bf16[768,768]{1,0:T(8,128)(2,1)}, u32[]{:S(2)}) %copy-start.4) | copy-done | bytes 1179672
  51.4 11.8 %self_attention.1.b_ref = f32[256,768]{1,0:T(8,128)S(1)} custom-call(bf16[256,768]{1,0:T(8,128)(2,1)S(1)} %copy-done, bf16[256,768]{1,0:T(8,128)(2,1)} %collective-permute-done.6.x1, bf16[256,768]{1,0:T(8,128)(2,1)} %collective-permute-done.7.x2, bf16[256,768]{1,0:T(8,128)(2,1)} %collective-permute-done.8.x3, f32[1,768]{1,0:T(1,128)S(1)} %reshape.28.gain, ...), custom_call_target="tpu_custom_call" | custom-call | flops 6241124352 | bytes 4718592 | tf_op jit(solution)/shard_map/self_attention/pallas_call | solution.py:153
  63.2 0.9 copy-done.9
  64.1 0.7 collective-permute-start.2
  64.8 2.6 %collective-permute-start.1 = (bf16[64,8,384]{2,1,0:T(8,128)(2,1)S(1)}, bf16[64,8,384]{2,1,0:T(8,128)(2,1)S(1)}, u32[]{:S(2)}, u32[]{:S(2)}) collective-permute-start(bf16[64,8,384]{2,1,0:T(8,128)(2,1)S(1)} %all-to-all-done.1.y0), channel_id=1, source_target_pairs={{0,3},{1,0},{2,1},{3,2},{4,7},{5,4},{6,5},{7,6},{8,11},{9,8},{10,9... | collective-permute-start | bytes 1179656 | tf_op jit(solution)/shard_map/ppermute | solution.py:233
  67.4 0.6 copy-done.13
  68.1 1.1 %select_add_fusion.1 = (bf16[64,8,128]{2,1,0:T(8,128)(2,1)S(1)}, bf16[64,8,128]{2,1,0:T(8,128)(2,1)S(1)}) fusion(bf16[64,8,128]{2,1,0:T(8,128)(2,1)} %collective-permute-done.5, bf16[64,8,128]{2,1,0:T(8,128)(2,1)} %copy-done.13, bf16[64,8,128]{2,1,0:T(8,128)(2,1)} %collective-permute-done.3, bf16[64,8,128]{2,1,0:T(8,128)(2,1)S(1)} %copy-done.12, pred[]{:T(512)S(6)} %eq.31, ...), kind=kLoop, calls=%fused_computation.2 | loop fusion | flops 917504 | bytes 786440 | tf_op jit(solution)/shard_map/add | solution.py:276
  69.2 0.7 pad_maximum_fusion
  69.9 1.1 %copy.18 = bf16[128,6,128]{0,2,1:T(8,128)(2,1)S(1)} copy(bf16[128,6,128]{2,1,0:T(8,128)(2,1)} %pad_maximum_fusion) | data formatting | bytes 393216 | tf_op jit(solution)/shard_map/slice | solution.py:281
  71.0 0.1 copy.19.cams
  71.2 1.3 %copy-done.6 = bf16[768,768]{1,0:T(8,128)(2,1)S(1)} copy-done((bf16[768,768]{1,0:T(8,128)(2,1)S(1)}, bf16[768,768]{1,0:T(8,128)(2,1)}, u32[]{:S(2)}) %copy-start.6) | copy-done | bytes 1179672
  72.5 1.3 %copy-done.7 = bf16[768,768]{1,0:T(8,128)(2,1)S(1)} copy-done((bf16[768,768]{1,0:T(8,128)(2,1)S(1)}, bf16[768,768]{1,0:T(8,128)(2,1)}, u32[]{:S(2)}) %copy-start.7) | copy-done | bytes 1179672
  73.7 4.3 %camera_attention.1 = (bf16[256,768]{1,0:T(8,128)(2,1)S(1)}, f32[256,768]{1,0:T(8,128)S(1)}) custom-call(bf16[256,768]{1,0:T(8,128)(2,1)S(1)} %copy-done, bf16[128,768]{1,0:T(8,128)(2,1)S(1)} %copy.19.cams, f32[1,768]{1,0:T(1,128)S(1)} %reshape.26.qgain, f32[1,768]{1,0:T(1,128)S(1)} %reshape.27.qshift, f32[1,768]{1,0:T(1,128)S(1)} %reshape.23.mgain.gain, ...), custom_call_target="tpu_custom_call" | custom-call | flops 1308622848 | bytes 4718592 | tf_op jit(solution)/shard_map/camera_attention/pallas_call | solution.py:167
  78.1 5.9 %collective-permute-done.1.y2 = bf16[64,8,384]{2,1,0:T(8,128)(2,1)S(1)} collective-permute-done((bf16[64,8,384]{2,1,0:T(8,128)(2,1)S(1)}, bf16[64,8,384]{2,1,0:T(8,128)(2,1)S(1)}, u32[]{:S(2)}, u32[]{:S(2)}) %collective-permute-start.1) | collective-permute-done | bytes 393248 | tf_op jit(solution)/shard_map/ppermute | solution.py:233
  84.0 0.4 collective-permute-done.y1
  84.4 10.8 %cross_attention.1 = f32[256,768]{1,0:T(8,128)} custom-call(bf16[64,8,384]{2,1,0:T(8,128)(2,1)S(1)} %all-to-all-done.1.y0, bf16[64,8,384]{2,1,0:T(8,128)(2,1)S(1)} %collective-permute-done.y1, bf16[64,8,384]{2,1,0:T(8,128)(2,1)S(1)} %collective-permute-done.1.y2, bf16[64,8,384]{2,1,0:T(8,128)(2,1)S(1)} %collective-permute-done.2.y3, ...), custom_call_target="tpu_custom_call" | custom-call | flops 6241124352 | bytes 4718592 | tf_op jit(solution)/shard_map/cross_attention/pallas_call | solution.py:184
  (46 shorter events, 0.1 us)
Async XLA Ops:
  0.0 15.6 %copy-start = (bf16[256,768]{1,0:T(8,128)(2,1)S(1)}, bf16[256,768]{1,0:T(8,128)(2,1)}, u32[]{:S(2)}) copy-start(bf16[256,768]{1,0:T(8,128)(2,1)} %x0.3) | copy-start | bytes 1179652
  3.4 40.0 %copy-start.14 = (f32[768]{0:T(1024)S(1)}, f32[768]{0:T(1024)}, u32[]{:S(2)}) copy-start(f32[768]{0:T(1024)} %param.22) | copy-start | bytes 9220
  3.4 40.0 %copy-start.15 = (f32[768]{0:T(1024)S(1)}, f32[768]{0:T(1024)}, u32[]{:S(2)}) copy-start(f32[768]{0:T(1024)} %param.23) | copy-start | bytes 9220
  3.4 40.0 %copy-start.16 = (f32[768]{0:T(1024)S(1)}, f32[768]{0:T(1024)}, u32[]{:S(2)}) copy-start(f32[768]{0:T(1024)} %param.18) | copy-start | bytes 9220
  3.4 40.1 %copy-start.17 = (f32[768]{0:T(1024)S(1)}, f32[768]{0:T(1024)}, u32[]{:S(2)}) copy-start(f32[768]{0:T(1024)} %param.19) | copy-start | bytes 9220
  3.4 40.1 %copy-start.18 = (f32[768]{0:T(1024)S(1)}, f32[768]{0:T(1024)}, u32[]{:S(2)}) copy-start(f32[768]{0:T(1024)} %param.20) | copy-start | bytes 9220
  3.4 40.1 %copy-start.19 = (f32[768]{0:T(1024)S(1)}, f32[768]{0:T(1024)}, u32[]{:S(2)}) copy-start(f32[768]{0:T(1024)} %param.21) | copy-start | bytes 9220
  3.4 45.4 %copy-start.1 = (bf16[768,768]{1,0:T(8,128)(2,1)S(1)}, bf16[768,768]{1,0:T(8,128)(2,1)}, u32[]{:S(2)}) copy-start(bf16[768,768]{1,0:T(8,128)(2,1)} %wq.3) | copy-start | bytes 3538948
  3.4 45.4 %copy-start.2 = (bf16[768,768]{1,0:T(8,128)(2,1)S(1)}, bf16[768,768]{1,0:T(8,128)(2,1)}, u32[]{:S(2)}) copy-start(bf16[768,768]{1,0:T(8,128)(2,1)} %wk.4) | copy-start | bytes 3538948
  3.4 28.0 %all-to-all-start = ((bf16[64,8,512]{2,1,0:T(8,128)(2,1)}), bf16[64,8,512]{2,1,0:T(8,128)(2,1)S(1)}, u32[]{:S(2)}, u32[]{:S(2)}) async-start(bf16[64,8,512]{2,1,0:T(8,128)(2,1)} %pack_pieces.1), calls=%async_computation | async-start | bytes 1048576 | tf_op jit(solution)/shard_map/all_to_all | solution.py:263
  15.6 32.2 %collective-permute-start.7 = (bf16[256,768]{1,0:T(8,128)(2,1)S(1)}, bf16[256,768]{1,0:T(8,128)(2,1)}, u32[]{:S(2)}, u32[]{:S(2)}) collective-permute-start(bf16[256,768]{1,0:T(8,128)(2,1)S(1)} %copy-done), channel_id=1, source_target_pairs={{0,3},{1,0},{2,1},{3,2},{4,7},{5,4},{6,5},{7,6},{8,11},{9,8},{10,9... | collective-permute-start | bytes 1179656 | tf_op jit(solution)/shard_map/ppermute | solution.py:233
  18.7 30.1 %collective-permute-start.6 = (bf16[256,768]{1,0:T(8,128)(2,1)S(1)}, bf16[256,768]{1,0:T(8,128)(2,1)}, u32[]{:S(2)}, u32[]{:S(2)}) collective-permute-start(bf16[256,768]{1,0:T(8,128)(2,1)S(1)} %copy-done), channel_id=1, source_target_pairs={{0,1},{1,2},{2,3},{3,0},{4,5},{5,6},{6,7},{7,4},{8,9},{9,10},{10,1... | collective-permute-start | bytes 1179656 | tf_op jit(solution)/shard_map/ppermute | solution.py:233
  18.7 30.1 %collective-permute-start.8 = (bf16[256,768]{1,0:T(8,128)(2,1)S(1)}, bf16[256,768]{1,0:T(8,128)(2,1)}, u32[]{:S(2)}, u32[]{:S(2)}) collective-permute-start(bf16[256,768]{1,0:T(8,128)(2,1)S(1)} %copy-done), channel_id=1, source_target_pairs={{0,2},{1,3},{2,0},{3,1},{4,6},{5,7},{6,4},{7,5},{8,10},{9,11},{10,... | collective-permute-start | bytes 1179656 | tf_op jit(solution)/shard_map/ppermute | solution.py:233
  31.4 0.8 copy-start.11
  35.7 28.4 %all-to-all-start.1 = ((bf16[64,8,384]{2,1,0:T(8,128)(2,1)}), bf16[64,8,384]{2,1,0:T(8,128)(2,1)S(1)}, u32[]{:S(2)}, u32[]{:S(2)}) async-start(bf16[64,8,384]{2,1,0:T(8,128)(2,1)} %get-tuple-element.9), calls=%async_computation.1 | async-start | bytes 786432 | tf_op jit(solution)/shard_map/all_to_all | solution.py:265
  43.5 23.9 %collective-permute-start.5 = (bf16[64,8,128]{2,1,0:T(8,128)(2,1)}, bf16[64,8,128]{2,1,0:T(8,128)(2,1)}, u32[]{:S(2)}, u32[]{:S(2)}) collective-permute-start(bf16[64,8,128]{2,1,0:T(8,128)(2,1)} %get-tuple-element.10), channel_id=1, source_target_pairs={{0,2},{1,3},{2,0},{3,1},{4,6},{5,7},{6,4},{7,5},{8,10},{9,11},{10,... | collective-permute-start | bytes 393224 | tf_op jit(solution)/shard_map/ppermute | solution.py:233
  46.8 20.6 %collective-permute-start.4 = (bf16[64,8,128]{2,1,0:T(8,128)(2,1)}, bf16[64,8,128]{2,1,0:T(8,128)(2,1)S(1)}, u32[]{:S(2)}, u32[]{:S(2)}) collective-permute-start(bf16[64,8,128]{2,1,0:T(8,128)(2,1)} %get-tuple-element.10), channel_id=1, source_target_pairs={{0,3},{1,0},{2,1},{3,2},{4,7},{5,4},{6,5},{7,6},{8,11},{9,8},{10,9... | collective-permute-start | bytes 393224 | tf_op jit(solution)/shard_map/ppermute | solution.py:233
  47.9 20.2 %collective-permute-start.3 = (bf16[64,8,128]{2,1,0:T(8,128)(2,1)}, bf16[64,8,128]{2,1,0:T(8,128)(2,1)}, u32[]{:S(2)}, u32[]{:S(2)}) collective-permute-start(bf16[64,8,128]{2,1,0:T(8,128)(2,1)} %get-tuple-element.10), channel_id=1, source_target_pairs={{0,1},{1,2},{2,3},{3,0},{4,5},{5,6},{6,7},{7,4},{8,9},{9,10},{10,1... | collective-permute-start | bytes 393224 | tf_op jit(solution)/shard_map/ppermute | solution.py:233
  48.8 1.3 %copy-start.3 = (bf16[768,768]{1,0:T(8,128)(2,1)S(1)}, bf16[768,768]{1,0:T(8,128)(2,1)}, u32[]{:S(2)}) copy-start(bf16[768,768]{1,0:T(8,128)(2,1)} %wv.4) | copy-start | bytes 3538948
  50.1 1.3 %copy-start.4 = (bf16[768,768]{1,0:T(8,128)(2,1)S(1)}, bf16[768,768]{1,0:T(8,128)(2,1)}, u32[]{:S(2)}) copy-start(bf16[768,768]{1,0:T(8,128)(2,1)} %wo.2) | copy-start | bytes 3538948
  51.4 16.7 %copy-start.12 = (bf16[64,8,128]{2,1,0:T(8,128)(2,1)S(1)}, bf16[64,8,128]{2,1,0:T(8,128)(2,1)}, u32[]{:S(2)}) copy-start(bf16[64,8,128]{2,1,0:T(8,128)(2,1)} %get-tuple-element.10) | copy-start | bytes 393220
  63.2 0.9 copy-start.9
  64.1 7.1 %copy-start.5 = (bf16[768,768]{1,0:T(8,128)(2,1)S(1)}, bf16[768,768]{1,0:T(8,128)(2,1)}, u32[]{:S(2)}) copy-start(bf16[768,768]{1,0:T(8,128)(2,1)} %wq.2) | copy-start | bytes 3538948
  64.1 14.0 %collective-permute-start.2 = (bf16[64,8,384]{2,1,0:T(8,128)(2,1)S(1)}, bf16[64,8,384]{2,1,0:T(8,128)(2,1)S(1)}, u32[]{:S(2)}, u32[]{:S(2)}) collective-permute-start(bf16[64,8,384]{2,1,0:T(8,128)(2,1)S(1)} %all-to-all-done.1.y0), channel_id=1, source_target_pairs={{0,2},{1,3},{2,0},{3,1},{4,6},{5,7},{6,4},{7,5},{8,10},{9,11},{10,... | collective-permute-start | bytes 1179656 | tf_op jit(solution)/shard_map/ppermute | solution.py:233
  64.8 19.2 %collective-permute-start.1 = (bf16[64,8,384]{2,1,0:T(8,128)(2,1)S(1)}, bf16[64,8,384]{2,1,0:T(8,128)(2,1)S(1)}, u32[]{:S(2)}, u32[]{:S(2)}) collective-permute-start(bf16[64,8,384]{2,1,0:T(8,128)(2,1)S(1)} %all-to-all-done.1.y0), channel_id=1, source_target_pairs={{0,3},{1,0},{2,1},{3,2},{4,7},{5,4},{6,5},{7,6},{8,11},{9,8},{10,9... | collective-permute-start | bytes 1179656 | tf_op jit(solution)/shard_map/ppermute | solution.py:233
  67.4 17.0 %collective-permute-start = (bf16[64,8,384]{2,1,0:T(8,128)(2,1)S(1)}, bf16[64,8,384]{2,1,0:T(8,128)(2,1)S(1)}, u32[]{:S(2)}, u32[]{:S(2)}) collective-permute-start(bf16[64,8,384]{2,1,0:T(8,128)(2,1)S(1)} %all-to-all-done.1.y0), channel_id=1, source_target_pairs={{0,1},{1,2},{2,3},{3,0},{4,5},{5,6},{6,7},{7,4},{8,9},{9,10},{10,1... | collective-permute-start | bytes 1179656 | tf_op jit(solution)/shard_map/ppermute | solution.py:233
  67.4 0.6 copy-start.13
  71.2 1.3 %copy-start.6 = (bf16[768,768]{1,0:T(8,128)(2,1)S(1)}, bf16[768,768]{1,0:T(8,128)(2,1)}, u32[]{:S(2)}) copy-start(bf16[768,768]{1,0:T(8,128)(2,1)} %wk.5) | copy-start | bytes 3538948
  72.5 1.3 %copy-start.7 = (bf16[768,768]{1,0:T(8,128)(2,1)S(1)}, bf16[768,768]{1,0:T(8,128)(2,1)}, u32[]{:S(2)}) copy-start(bf16[768,768]{1,0:T(8,128)(2,1)} %wv.5) | copy-start | bytes 3538948
  73.7 10.7 %copy-start.8 = (bf16[768,768]{1,0:T(8,128)(2,1)S(1)}, bf16[768,768]{1,0:T(8,128)(2,1)}, u32[]{:S(2)}) copy-start(bf16[768,768]{1,0:T(8,128)(2,1)} %wo.3) | copy-start | bytes 3538948
  73.7 10.7 %copy-start.10 = (f32[256,768]{1,0:T(8,128)S(1)}, f32[256,768]{1,0:T(8,128)}, u32[]{:S(2)}) copy-start(f32[256,768]{1,0:T(8,128)} %copy-done.9) | copy-start | bytes 2359300

commit v2 on v0

v2 whole, which is shorter than its diff:
```python
import jax
import jax.numpy as jnp
from jax import lax
from jax.experimental import pallas as pl
from jax.experimental.pallas import tpu as pltpu
from jax.sharding import Mesh, PartitionSpec as P

D = 768
HDIM = 64
COLS = 256
STEPS = D // COLS
HEADS = COLS // HDIM
ROUTE = ("core", "zh", "zl", "x")
ROWS = 256
PIECES = 64
VIEW = 1024
BF = jnp.bfloat16


def norm(wide, gain, shift):
    center = jnp.mean(wide, axis=-1, keepdims=True)
    spread = jnp.mean((wide - center) ** 2, axis=-1, keepdims=True)
    return ((wide - center) * lax.rsqrt(spread + 1e-06) * gain + shift).astype(BF)


def mm(left, right):
    return lax.dot_general(left, right, (((1,), (0,)), ((), ())), preferred_element_type=jnp.float32)


def mm_nt(left, right):
    return lax.dot_general(left, right, (((1,), (1,)), ((), ())), preferred_element_type=jnp.float32)


def heads(q, k, v):
    lane = lax.broadcasted_iota(jnp.int32, q.shape, 1) // HDIM
    score = lambda head: mm_nt(jnp.where(lane == head, q, jnp.zeros_like(q)), k)
    ahead = score(0)
    for head in range(HEADS):
        s = ahead
        if head + 1 < HEADS:
            ahead = score(head + 1)
        top = jnp.max(s, axis=-1, keepdims=True)
        p = jnp.exp(s - top)
        yield lane == head, top, jnp.sum(p, axis=-1, keepdims=True), mm(p.astype(BF), v)


def attend(q, k, v):
    out = None
    for mine, _, total, c in heads(q, k, v):
        c = c / total
        out = c if out is None else jnp.where(mine, c, out)
    return out


def heads_t(q, k, vt):
    lane = lax.broadcasted_iota(jnp.int32, q.shape, 1) // HDIM
    score = lambda head: mm_nt(k, jnp.where(lane == head, q, jnp.zeros_like(q)))
    ahead = score(0)
    for head in range(HEADS):
        s = ahead
        if head + 1 < HEADS:
            ahead = score(head + 1)
        top = jnp.max(s, axis=0, keepdims=True)
        p = jnp.exp(s - top)
        c = mm(vt[HDIM * head : HDIM * (head + 1)], p.astype(BF))
        yield slice(HDIM * head, HDIM * (head + 1)), head, top, jnp.sum(p, axis=0, keepdims=True), c


def mm_tn(left, right):
    return lax.dot_general(left, right, (((0,), (0,)), ((), ())), preferred_element_type=jnp.float32)


def project(refs, w, out):
    for i, ref in enumerate(refs):
        out[i * ROWS : (i + 1) * ROWS] = mm(ref[...], w).astype(BF)


def pack_kernel(cams, x_ref, gain, shift, o_ref):
    group = lax.axis_index(("x", "zl"))
    view = lax.axis_index(("zh", "core"))
    tok = lax.axis_index("tok")
    row = cams[group, 2 * view + tok // 2] - (view * VIEW + tok * ROWS)
    m = norm(x_ref[...].astype(jnp.float32), gain[...][None], shift[...][None])
    pick = (lax.broadcasted_iota(jnp.int32, (8, ROWS), 1) == row).astype(BF)
    cam = mm(pick, m)
    sub = lax.broadcasted_iota(jnp.int32, (8, 128), 0)
    extra = jnp.zeros((8, 128), jnp.float32)
    for c in range(D // 128):
        extra = jnp.where(sub == c, cam[:, 128 * c : 128 * (c + 1)], extra)
        tiles = m[:, 128 * c : 128 * (c + 1)].astype(jnp.float32).reshape(ROWS // 8, 8, 128)
        o_ref[:, c // 3, c % 3] = tiles.astype(BF)
    spread = jnp.broadcast_to(extra[None], (ROWS // 8, 8, 128)).astype(BF)
    o_ref[:, 0, 3] = spread
    o_ref[:, 1, 3] = spread


def norm_kernel(x_ref, gain, shift, o_ref):
    o_ref[...] = norm(x_ref[...].astype(jnp.float32), gain[...][None], shift[...][None])


def query_kernel(x_ref, h_ref, gain, shift, wc, ws, c_ref, s_ref, n_ref):
    @pl.when(pl.program_id(0) == 0)
    def _():
        n_ref[...] = norm(x_ref[...].astype(jnp.float32), gain[...][None], shift[...][None])

    c_ref[...] = mm(n_ref[...], wc[...]).astype(BF) * BF(0.125)
    s_ref[...] = mm(h_ref[...], ws[...]).astype(BF) * BF(0.125)


def self_kernel(*refs):
    sources, o_ref, held, k_ref, v_ref, c_ref, sems = refs[:9], refs[9], refs[10:19], *refs[19:23]
    copies = [
        pltpu.make_async_copy(src, dst, sems.at[i])
        for i, (src, dst) in enumerate(zip(sources, held))
    ]
    for copy in copies:
        copy.start()
    (h0, wk, h1, h2, h3, wv, q_ref, x_ref, wo) = held
    copies[0].wait()
    copies[1].wait()
    for i, h in enumerate((h0, h1, h2, h3)):
        if i:
            copies[i + 1].wait()
        k_ref[i * ROWS : (i + 1) * ROWS] = mm(h[...], wk[...]).astype(BF)
    copies[5].wait()
    for i, h in enumerate((h0, h1, h2, h3)):
        v_ref[i * ROWS : (i + 1) * ROWS] = mm(h[...], wv[...]).astype(BF)
    copies[6].wait()
    for step in range(STEPS):
        at = slice(step * COLS, (step + 1) * COLS)
        c_ref[:, at] = attend(q_ref[:, at], k_ref[:, at], v_ref[:, at]).astype(BF)
    copies[7].wait()
    copies[8].wait()
    o_ref[...] = x_ref[...].astype(jnp.float32) + mm(c_ref[...], wo[...])


def camera_kernel(p0, p1, p2, p3, q_ref, wk, wv, c_ref, m_ref):
    @pl.when(pl.program_id(0) == 0)
    def _():
        tok = lax.axis_index("tok")
        parts = [ref[...].astype(jnp.float32) for ref in (p0, p1, p2, p3)]
        for half in (0, 1):
            total = jnp.zeros((PIECES, 8, 128), jnp.float32)
            for shift, part in zip((0, 1, 3, 2), parts):
                total += jnp.where((tok + 4 - shift) % 4 // 2 == half, part, 0.0)
            for c in range(D // 128):
                m_ref[PIECES * half : PIECES * (half + 1), 128 * c : 128 * (c + 1)] = total[
                    :, c, :
                ].astype(BF)

    m = m_ref[...]
    k = mm(m, wk[...]).astype(BF)
    v = mm(m, wv[...]).astype(BF)
    for at, _, _, total, c in heads_t(q_ref[...], k, jnp.transpose(v)):
        c_ref[at] = c * (1.0 / total)


def early_kernel(m0, m1, m2, q_ref, wk, wv, c_ref, t_ref, l_ref, k_ref, v_ref):
    project((m0, m1, m2), wk[...], k_ref)
    project((m0, m1, m2), wv[...], v_ref)
    for at, head, top, total, c in heads_t(q_ref[...], k_ref[...], jnp.transpose(v_ref[...])):
        c_ref[at] = c
        t_ref[head : head + 1] = top
        l_ref[head : head + 1] = total


def late_kernel(ma, mb, q_ref, wk, wv, wo, c_ref, t_ref, l_ref, cam_ref, b_ref, o_ref):
    @pl.when(pl.program_id(0) == 0)
    def _():
        o_ref[...] = b_ref[...]

    m = jnp.concatenate([ma[...], mb[...]], axis=0)
    k = mm(m, wk[...]).astype(BF)
    v = mm(m, wv[...]).astype(BF)
    ctx = []
    for at, head, top, total, c in heads_t(q_ref[...], k, jnp.transpose(v)):
        top0 = t_ref[head : head + 1]
        best = jnp.maximum(top, top0)
        w0 = jnp.exp(top0 - best)
        w1 = jnp.exp(top - best)
        down = 1.0 / (w0 * l_ref[head : head + 1] + w1 * total)
        ctx.append(c_ref[at] * (w0 * down) + c * (w1 * down) + cam_ref[at])
    o_ref[...] += mm_tn(jnp.concatenate(ctx, axis=0).astype(BF), wo[...])


def full(shape):
    return pl.BlockSpec(shape, lambda i: (0,) * len(shape))


WCOL = pl.BlockSpec((D, COLS), lambda i: (0, i))
WROW = pl.BlockSpec((COLS, D), lambda i: (i, 0))
XCOL = pl.BlockSpec((ROWS, COLS), lambda i: (0, i))
CTX = pl.BlockSpec((COLS, ROWS), lambda i: (i, 0))
STAT = pl.BlockSpec((8, ROWS), lambda i: (i, 0))
VEC = full((D,))
X = full((ROWS, D))
HALF = full((ROWS // 2, D))
CAMS = full((PIECES, 8, 128))


def shape(*dims, dtype=BF):
    return jax.ShapeDtypeStruct(dims, dtype)


def call(name, kernel, ins, outs, out_shape, scratch=(), steps=STEPS, work=0, limit=32):
    return pl.pallas_call(
        kernel,
        grid=(steps,),
        in_specs=ins,
        out_specs=outs,
        out_shape=out_shape,
        scratch_shapes=list(scratch),
        compiler_params=pltpu.CompilerParams(
            dimension_semantics=("arbitrary",), vmem_limit_bytes=limit * 1024 * 1024
        ),
        cost_estimate=pl.CostEstimate(
            flops=work, bytes_accessed=2 * D * D * 2, transcendentals=0
        ),
        name=name,
    )


def call_pack(camera_rows, tokens, gain, shift):
    return pl.pallas_call(
        pack_kernel,
        grid_spec=pltpu.PrefetchScalarGridSpec(
            num_scalar_prefetch=1,
            grid=(1,),
            in_specs=[
                pl.BlockSpec((ROWS, D), lambda i, *_: (0, 0)),
                pl.BlockSpec((D,), lambda i, *_: (0,)),
                pl.BlockSpec((D,), lambda i, *_: (0,)),
            ],
            out_specs=pl.BlockSpec((ROWS // 8, 2, 4, 8, 128), lambda i, *_: (0, 0, 0, 0, 0)),
        ),
        out_shape=shape(ROWS // 8, 2, 4, 8, 128),
        name="memory_norm",
    )(camera_rows, tokens, gain, shift)


def call_self(*operands):
    return pl.pallas_call(
        self_kernel,
        in_specs=[pl.BlockSpec(memory_space=pl.ANY)] * 9,
        out_specs=pl.BlockSpec(memory_space=pltpu.VMEM),
        out_shape=shape(ROWS, D, dtype=jnp.float32),
        scratch_shapes=[pltpu.VMEM(v.shape, BF) for v in operands]
        + [pltpu.VMEM((VIEW, D), BF)] * 2
        + [pltpu.VMEM((ROWS, D), BF), pltpu.SemaphoreType.DMA((9,))],
        compiler_params=pltpu.CompilerParams(vmem_limit_bytes=60 * 1024 * 1024),
        cost_estimate=pl.CostEstimate(
            flops=4 * VIEW * D * D + 16 * ROWS * VIEW * D,
            bytes_accessed=10 * D * D,
            transcendentals=0,
        ),
        name="self_attention",
    )(*operands)


def to_tiles(x):
    return x.reshape(32, 8, 6, 128).transpose(0, 2, 1, 3).reshape(PIECES, 24, 128)


def from_tiles(pieces):
    return pieces.reshape(32, 6, 8, 128).transpose(0, 2, 1, 3).reshape(ROWS, D)


def turn(shift):
    return [(i, (i + shift) % 4) for i in range(4)]


def around(value):
    return [lax.ppermute(value, "tok", turn(shift)) for shift in (1, 3, 2)]


def local(
    tokens,
    self_gain,
    self_shift,
    query_gain,
    query_shift,
    memory_gain,
    memory_shift,
    self_query,
    self_key,
    self_value,
    self_output,
    cross_query,
    cross_key,
    cross_value,
    cross_output,
    partner,
    camera_rows,
):
    packed = call_pack(camera_rows, tokens, memory_gain, memory_shift).reshape(PIECES, 32, 128)
    first = lax.all_to_all(packed, ROUTE, split_axis=0, concat_axis=0, tiled=True)
    wanted = partner.reshape(4, 2, 4, 2).transpose(3, 2, 1, 0).reshape(PIECES)
    place = (wanted % 2) * 32 + (wanted // 2 % 4) * 8 + (wanted // 8 % 2) * 4 + wanted // 16
    place = (place[:, None] * 4 + jnp.arange(3)[None, :]).reshape(PIECES * 3)
    onward = first.reshape(PIECES * 4, 8, 128).at[place].get(mode="promise_in_bounds")
    onward = onward.reshape(PIECES, 24, 128)
    cam_own = first[:, 24:]

    hidden = call("self_norm", norm_kernel, [X, VEC, VEC], X, shape(ROWS, D), steps=1)(
        tokens, self_gain, self_shift
    )
    others = around(hidden)
    cq, sq = call(
        "queries",
        query_kernel,
        [X, X, VEC, VEC, WCOL, WCOL],
        [XCOL, XCOL],
        [shape(ROWS, D), shape(ROWS, D)],
        [pltpu.VMEM((ROWS, D), BF)],
        work=4 * ROWS * D * D,
    )(tokens, hidden, query_gain, query_shift, cross_query, self_query)
    sq, onward = lax.optimization_barrier((sq, onward))
    base = call_self(hidden, self_key, *others, self_value, sq, tokens, self_output)

    mine = lax.all_to_all(onward, ROUTE, split_axis=0, concat_axis=0, tiled=True)
    cam_parts = [cam_own] + around(cam_own)
    mine, base, cq, *cam_parts = lax.optimization_barrier((mine, base, cq, *cam_parts))
    mine = from_tiles(mine)
    near_a = lax.ppermute(mine, "tok", turn(1))
    near_b = lax.ppermute(mine, "tok", turn(3))
    far_a = lax.ppermute(near_a[: ROWS // 2], "tok", turn(1))
    far_b = lax.ppermute(near_b[ROWS // 2 :], "tok", turn(3))
    cam_ctx = call(
        "camera_attention",
        camera_kernel,
        [CAMS] * 4 + [XCOL, WCOL, WCOL],
        CTX,
        shape(D, ROWS, dtype=jnp.float32),
        [pltpu.VMEM((2 * PIECES, D), BF)],
        work=4 * 128 * D * D + 16 * ROWS * 128 * D,
    )(*cam_parts, cq, cross_key, cross_value)
    ctx, tops, sums = call(
        "cross_early",
        early_kernel,
        [X] * 3 + [XCOL, WCOL, WCOL],
        [CTX, STAT, STAT],
        [shape(n, ROWS, dtype=jnp.float32) for n in (D, 8 * STEPS, 8 * STEPS)],
        [pltpu.VMEM((3 * ROWS, COLS), BF)] * 2,
        work=12 * ROWS * D * D + 48 * ROWS * ROWS * D,
    )(mine, near_a, near_b, cq, cross_key, cross_value)
    return call(
        "cross_late",
        late_kernel,
        [HALF, HALF, XCOL, WCOL, WCOL, WROW, CTX, STAT, STAT, CTX, X],
        X,
        shape(ROWS, D, dtype=jnp.float32),
        work=4 * ROWS * D * D + 16 * ROWS * ROWS * D,
    )(far_a, far_b, cq, cross_key, cross_value, cross_output, ctx, tops, sums, cam_ctx, base)


def solution(mesh):
    split = Mesh(mesh.devices.reshape(4, 2, 4, 2, 4), ("x", "zl", "zh", "core", "tok"))
    rows = P(("x", "zl", "zh", "core", "tok"), None)
    return jax.shard_map(
        local, mesh=split, in_specs=(rows,) + (P(),) * 16, out_specs=rows, check_vma=False
    )
```

time: 332 us -> 86.7 us (0.26)
  blocking collectives: 190 us -> 0 us
  matrix products: 48.9 us -> 0 us
  Pallas kernels: 0 us -> 31.8 us
  waiting for transfers between devices: 33.8 us -> 11 us
  between operations: 13.6 us -> 0.32 us
  starting transfers between devices: 26.7 us -> 36.8 us
  local copies, waits for them, and re-layouts: 13 us -> 6.32 us
  other arithmetic: 4 us -> 0.11 us
    psum x1 -> x0, blocking collectives: 141 us -> none  [local(): group_cams = lax.psum(picked.astype(jnp.bfloat16), ('view', 'tok'))]
    pallas_call x0 -> x7, Pallas kernels: none -> 31.8 us  [the longest x1 11.1 us: call_self(): pl.pallas_call(self_kernel, in_specs=[pl.BlockSpec(memory_space=pl.ANY)]...]
    all_gather x1 -> x0, blocking collectives: 27.9 us -> none  [local(): cams = lax.all_gather(group_cams, 'group', axis=0, tiled=True)]
    dot_general x14 -> x0, matrix products: 26.8 us -> none  [the longest x3 13.7 us: attend(): jnp.einsum('hqk,khd->qhd', weights, vh, preferred_element_type=jnp.float32)]
    all_to_all x3 -> x2, waiting for transfers between devices: 33.7 us -> 6.9 us  [the longest x1 6.89 us: local(): lax.all_to_all(packed, ROUTE, split_axis=0, concat_axis=0, tiled=True)]
    sub x3 -> x0, matrix products: 22.1 us -> none  [attend(): weights = jax.nn.softmax(scores, axis=-1).astype(jnp.bfloat16)]
    all_to_all x1 -> x0, blocking collectives: 20.7 us -> none  [route_keys(): lax.all_to_all(onward_k, ('group', 'view'), split_axis=0, concat_axis=0,...]
    ppermute x0 -> x10, starting transfers between devices: none -> 16.7 us  [the longest x6 10.6 us: around(): return [lax.ppermute(value, 'tok', turn(shift)) for shift in (1, 3, 2)]]
  transfers between devices with their start and end apart: 7 -> 12, of which waited for: 3 -> 2; matrix products, arithmetic and copies ran while one was open for 16% -> 5% of each run, Pallas kernels for 0% -> 28%
where the time goes in v2:
time: 86.7 us; the launch traced here: 86.3 us
  starting transfers between devices  36.8 us (42%)
  Pallas kernels  31.8 us (37%)
  waiting for transfers between devices  11 us (13%)
  local copies, waits for them, and re-layouts  6.32 us (7%)
    all_to_all x1, starting transfers between devices, local(): lax.all_to_all(packed, ROUTE, split_axis=0, concat_axis=0, tiled=True)  12.3 us
    pallas_call x1, Pallas kernels, call_self(): pl.pallas_call(self_kernel, in_specs=[pl.BlockSpec(memory_space=pl.ANY)]...  11.1 us
    ppermute x6, starting transfers between devices, around(): return [lax.ppermute(value, 'tok', turn(shift)) for shift in (1, 3, 2)]  10.6 us
    all_to_all x1, starting transfers between devices, local(): lax.all_to_all(onward, ROUTE, split_axis=0, concat_axis=0, tiled=True)  7.71 us
    pallas_call x1, Pallas kernels, local(): call('cross_early', early_kernel, [X] * 3 + [XCOL, WCOL, WCOL], [CTX, STA...  7.41 us
    all_to_all x1, waiting for transfers between devices, local(): lax.all_to_all(packed, ROUTE, split_axis=0, concat_axis=0, tiled=True)  6.89 us
    pallas_call x1, Pallas kernels, local(): call('cross_late', late_kernel, [HALF, HALF, XCOL, WCOL, WCOL, WROW, CTX,...  4.72 us
    ppermute x1, waiting for transfers between devices, local(): near_b = lax.ppermute(mine, 'tok', turn(3))  4.11 us
  transfers between devices with their start and end apart: 12, of which 2 were waited for; matrix products, arithmetic and copies ran while one was open for 5% of the time, Pallas kernels for 28%

profile of v2, /device:TPU:2, one launch (start us, length us, event | category | flops | bytes accessed | tf_op | source)
XLA Modules:
  0.0 86.3 jit_solution(5049908429044066726)
XLA Ops:
  0.0 3.1 %memory_norm.1 = bf16[32,2,4,8,128]{4,3,2,1,0:T(8,128)(2,1)} custom-call(s32[8,16]{1,0:T(8,128)} %cams.1, bf16[256,768]{1,0:T(8,128)(2,1)} %refs_7_.1, f32[768]{0:T(1024)} %gain.5, f32[768]{0:T(1024)} %shift.5), custom_call_target="tpu_custom_call" | custom-call | tf_op jit(solution)/shard_map/memory_norm/pallas_call | solution.py:224
  3.2 12.3 %all-to-all-start = ((bf16[64,32,128]{2,1,0:T(8,128)(2,1)}), bf16[64,32,128]{2,1,0:T(8,128)(2,1)}, u32[]{:S(2)}, u32[]{:S(2)}) async-start(bf16[64,32,128]{2,1,0:T(8,128)(2,1)} %bitcast.10), calls=%async_computation | async-start | bytes 1048576 | tf_op jit(solution)/shard_map/all_to_all | solution.py:296
  15.6 0.3 self_norm.1.h_ref.refs_0_
  15.9 3.3 %collective-permute-start.2 = (bf16[256,768]{1,0:T(8,128)(2,1)S(1)}, bf16[256,768]{1,0:T(8,128)(2,1)}, u32[]{:S(2)}, u32[]{:S(2)}) collective-permute-start(bf16[256,768]{1,0:T(8,128)(2,1)S(1)} %self_norm.1.h_ref.refs_0_), channel_id=1, source_target_pairs={{0,2},{1,3},{2,0},{3,1},{4,6},{5,7},{6,4},{7,5},{8,10},{9,11},{10,... | collective-permute-start | bytes 1179656 | tf_op jit(solution)/shard_map/ppermute | solution.py:273
  19.2 1.1 %collective-permute-start.1 = (bf16[256,768]{1,0:T(8,128)(2,1)S(1)}, bf16[256,768]{1,0:T(8,128)(2,1)}, u32[]{:S(2)}, u32[]{:S(2)}) collective-permute-start(bf16[256,768]{1,0:T(8,128)(2,1)S(1)} %self_norm.1.h_ref.refs_0_), channel_id=1, source_target_pairs={{0,3},{1,0},{2,1},{3,2},{4,7},{5,4},{6,5},{7,6},{8,11},{9,8},{10,9... | collective-permute-start | bytes 1179656 | tf_op jit(solution)/shard_map/ppermute | solution.py:273
  20.2 1.0 %collective-permute-start = (bf16[256,768]{1,0:T(8,128)(2,1)S(1)}, bf16[256,768]{1,0:T(8,128)(2,1)}, u32[]{:S(2)}, u32[]{:S(2)}) collective-permute-start(bf16[256,768]{1,0:T(8,128)(2,1)S(1)} %self_norm.1.h_ref.refs_0_), channel_id=1, source_target_pairs={{0,1},{1,2},{2,3},{3,0},{4,5},{5,6},{6,7},{7,4},{8,9},{9,10},{10,1... | collective-permute-start | bytes 1179656 | tf_op jit(solution)/shard_map/ppermute | solution.py:273
  21.2 0.1 reshape.151
  21.3 0.1 copy.19
  21.5 0.1 reshape.152
  21.6 0.1 iota_add_fusion
  21.7 0.1 add.108
  21.9 1.7 %queries.1 = (bf16[256,768]{1,0:T(8,128)(2,1)S(1)}, bf16[256,768]{1,0:T(8,128)(2,1)S(1)}) custom-call(bf16[256,768]{1,0:T(8,128)(2,1)S(1)} %copy-done.2, bf16[256,768]{1,0:T(8,128)(2,1)S(1)} %self_norm.1.h_ref.refs_0_, f32[768]{0:T(1024)S(1)} %copy-done.12, f32[768]{0:T(1024)S(1)} %copy-done.13, bf16[768,768]{1,0:T(8,128)(2,1)S(1)} %copy-done.4, ...), custom_call_target="tpu_custom_call" | custom-call | flops 603979776 | bytes 2359296 | tf_op jit(solution)/shard_map/queries/pallas_call | solution.py:308
  23.6 0.7 copy-done.14
  24.4 6.9 %all-to-all-done = bf16[64,32,128]{2,1,0:T(8,128)(2,1)} async-done(((bf16[64,32,128]{2,1,0:T(8,128)(2,1)}), bf16[64,32,128]{2,1,0:T(8,128)(2,1)}, u32[]{:S(2)}, u32[]{:S(2)}) %all-to-all-start) | async-done | bytes 524320 | tf_op jit(solution)/shard_map/all_to_all | solution.py:296
  31.3 2.5 %gather_fusion = bf16[192,8,128]{2,1,0:T(8,128)(2,1)} fusion(bf16[256,8,128]{2,1,0:T(8,128)(2,1)} %bitcast.1, s32[1024]{0:T(1024)S(1)} %pad_clamp_fusion), kind=kCustom, calls=%fused_computation | custom fusion | bytes 787200 | tf_op jit(solution)/shard_map/gather | solution.py:300
  33.8 7.7 %all-to-all-start.1 = ((bf16[64,24,128]{2,1,0:T(8,128)(2,1)}), bf16[64,24,128]{2,1,0:T(8,128)(2,1)}, u32[]{:S(2)}, u32[]{:S(2)}) async-start(bf16[64,24,128]{2,1,0:T(8,128)(2,1)} %bitcast.4), calls=%async_computation.1 | async-start | bytes 786432 | tf_op jit(solution)/shard_map/all_to_all | solution.py:320
  41.5 0.9 %slice.14.p0 = bf16[64,8,128]{2,1,0:T(8,128)(2,1)S(1)} slice(bf16[64,32,128]{2,1,0:T(8,128)(2,1)} %all-to-all-done), slice={[0:64], [24:32], [0:128]} | slice | bytes 262144 | tf_op jit(solution)/shard_map/slice | solution.py:302
  42.4 0.0 copy-start
  42.5 0.0 copy-start.1
  42.5 3.3 %collective-permute-start.5 = (bf16[64,8,128]{2,1,0:T(8,128)(2,1)S(1)}, bf16[64,8,128]{2,1,0:T(8,128)(2,1)S(1)}, u32[]{:S(2)}, u32[]{:S(2)}) collective-permute-start(bf16[64,8,128]{2,1,0:T(8,128)(2,1)S(1)} %slice.14.p0), channel_id=1, source_target_pairs={{0,2},{1,3},{2,0},{3,1},{4,6},{5,7},{6,4},{7,5},{8,10},{9,11},{10,... | collective-permute-start | bytes 393224 | tf_op jit(solution)/shard_map/ppermute | solution.py:273
  45.7 1.1 %collective-permute-start.4 = (bf16[64,8,128]{2,1,0:T(8,128)(2,1)S(1)}, bf16[64,8,128]{2,1,0:T(8,128)(2,1)S(1)}, u32[]{:S(2)}, u32[]{:S(2)}) collective-permute-start(bf16[64,8,128]{2,1,0:T(8,128)(2,1)S(1)} %slice.14.p0), channel_id=1, source_target_pairs={{0,3},{1,0},{2,1},{3,2},{4,7},{5,4},{6,5},{7,6},{8,11},{9,8},{10,9... | collective-permute-start | bytes 393224 | tf_op jit(solution)/shard_map/ppermute | solution.py:273
  46.8 1.0 %collective-permute-start.3 = (bf16[64,8,128]{2,1,0:T(8,128)(2,1)S(1)}, bf16[64,8,128]{2,1,0:T(8,128)(2,1)S(1)}, u32[]{:S(2)}, u32[]{:S(2)}) collective-permute-start(bf16[64,8,128]{2,1,0:T(8,128)(2,1)S(1)} %slice.14.p0), channel_id=1, source_target_pairs={{0,1},{1,2},{2,3},{3,0},{4,5},{5,6},{6,7},{7,4},{8,9},{9,10},{10,1... | collective-permute-start | bytes 393224 | tf_op jit(solution)/shard_map/ppermute | solution.py:273
  47.8 11.1 %self_attention.1.b_ref = f32[256,768]{1,0:T(8,128)} custom-call(bf16[256,768]{1,0:T(8,128)(2,1)} %copy-done.3, bf16[768,768]{1,0:T(8,128)(2,1)} %refs_1_.1, bf16[256,768]{1,0:T(8,128)(2,1)} %collective-permute-done.refs_2_, bf16[256,768]{1,0:T(8,128)(2,1)} %collective-permute-done.1.refs_3_, bf16[256,768]{1,0:T(8,128)(2,1)} %collective-permute-done.2.refs_4_, ...), custom_call_target="tpu_custom_call" | custom-call | flops 5637144576 | bytes 5898240 | tf_op jit(solution)/shard_map/self_attention/pallas_call | solution.py:242
  58.9 0.6 copy-done.8
  59.6 2.3 %collective-permute-start.8 = (bf16[256,768]{1,0:T(8,128)(2,1)}, bf16[256,768]{1,0:T(8,128)(2,1)S(1)}, u32[]{:S(2)}, u32[]{:S(2)}) collective-permute-start(bf16[256,768]{1,0:T(8,128)(2,1)} %bitcast.7.m0), channel_id=1, source_target_pairs={{0,3},{1,0},{2,1},{3,2},{4,7},{5,4},{6,5},{7,6},{8,11},{9,8},{10,9... | collective-permute-start | bytes 1179656 | tf_op jit(solution)/shard_map/ppermute | solution.py:325
  61.9 0.9 %copy-done.9 = bf16[64,8,128]{2,1,0:T(8,128)(2,1)S(1)} copy-done((bf16[64,8,128]{2,1,0:T(8,128)(2,1)S(1)}, bf16[64,8,128]{2,1,0:T(8,128)(2,1)}, u32[]{:S(2)}) %copy-start.9) | copy-done | bytes 131096
  62.8 3.3 %camera_attention.1.cam_ref = f32[768,256]{1,0:T(8,128)S(1)} custom-call(bf16[64,8,128]{2,1,0:T(8,128)(2,1)S(1)} %slice.14.p0, bf16[64,8,128]{2,1,0:T(8,128)(2,1)S(1)} %copy-done.9, bf16[64,8,128]{2,1,0:T(8,128)(2,1)S(1)} %collective-permute-done.4.p2, bf16[64,8,128]{2,1,0:T(8,128)(2,1)S(1)} %collective-permute-done.5.p3, ...), custom_call_target="tpu_custom_call" | custom-call | flops 704643072 | bytes 2359296 | tf_op jit(solution)/shard_map/camera_attention/pallas_call | solution.py:328
  66.1 4.1 %collective-permute-done.8.m2 = bf16[256,768]{1,0:T(8,128)(2,1)S(1)} collective-permute-done((bf16[256,768]{1,0:T(8,128)(2,1)}, bf16[256,768]{1,0:T(8,128)(2,1)S(1)}, u32[]{:S(2)}, u32[]{:S(2)}) %collective-permute-start.8) | collective-permute-done | bytes 393248 | tf_op jit(solution)/shard_map/ppermute | solution.py:325
  70.2 3.6 %collective-permute-start.9 = (bf16[128,768]{1,0:T(8,128)(2,1)S(1)}, bf16[128,768]{1,0:T(8,128)(2,1)S(1)}, u32[]{:S(2)}, u32[]{:S(2)}) collective-permute-start(bf16[128,768]{1,0:T(8,128)(2,1)S(1)} %slice.16), channel_id=1, source_target_pairs={{0,3},{1,0},{2,1},{3,2},{4,7},{5,4},{6,5},{7,6},{8,11},{9,8},{10,9... | collective-permute-start | bytes 589832 | tf_op jit(solution)/shard_map/ppermute | solution.py:327
  73.8 0.3 collective-permute-start.7
  74.1 7.4 %cross_early.1 = (f32[768,256]{1,0:T(8,128)S(1)}, f32[24,256]{1,0:T(8,128)S(1)}, f32[24,256]{1,0:T(8,128)S(1)}) custom-call(bf16[256,768]{1,0:T(8,128)(2,1)} %bitcast.7.m0, bf16[256,768]{1,0:T(8,128)(2,1)S(1)} %collective-permute-done.6.m1, bf16[256,768]{1,0:T(8,128)(2,1)S(1)} %collective-permute-done.8.m2, bf16[256,768]{1,0:T(8,128)(2,1)S(1)} %get-tuple-element.24.q_ref, ...), custom_call_target="tpu_custom_call" | custom-call | flops 4227858432 | bytes 2359296 | tf_op jit(solution)/shard_map/cross_early/pallas_call | solution.py:337
  81.6 4.7 %cross_late.1 = f32[256,768]{1,0:T(8,128)} custom-call(bf16[128,768]{1,0:T(8,128)(2,1)S(1)} %collective-permute-done.7.ma, bf16[128,768]{1,0:T(8,128)(2,1)S(1)} %collective-permute-done.9.mb, bf16[256,768]{1,0:T(8,128)(2,1)S(1)} %get-tuple-element.24.q_ref, bf16[768,768]{1,0:T(8,128)(2,1)S(1)} %copy-done, bf16[768,768]{1,0:T(8,128)(2,1)S(1)} %copy-done.1, ...), custom_call_target="tpu_custom_call" | custom-call | flops 1409286144 | bytes 2359296 | tf_op jit(solution)/shard_map/cross_late/pallas_call | solution.py:346
  (43 shorter events, 0.1 us)
Async XLA Ops:
  0.0 15.5 %copy-start.2 = (bf16[256,768]{1,0:T(8,128)(2,1)S(1)}, bf16[256,768]{1,0:T(8,128)(2,1)}, u32[]{:S(2)}) copy-start(bf16[256,768]{1,0:T(8,128)(2,1)} %refs_7_.1) | copy-start | bytes 1179652
  0.0 15.5 %copy-start.11 = (f32[768]{0:T(1024)S(1)}, f32[768]{0:T(1024)}, u32[]{:S(2)}) copy-start(f32[768]{0:T(1024)} %shift.3) | copy-start | bytes 9220
  0.0 15.5 %copy-start.10 = (f32[768]{0:T(1024)S(1)}, f32[768]{0:T(1024)}, u32[]{:S(2)}) copy-start(f32[768]{0:T(1024)} %gain.3) | copy-start | bytes 9220
  0.0 21.2 %copy-start.15 = (s32[64]{0:T(128)S(1)}, s32[64]{0:T(128)}, u32[]{:S(2)}) copy-start(s32[64]{0:T(128)} %param.32) | copy-start | bytes 772
  0.0 21.8 %copy-start.5 = (bf16[768,768]{1,0:T(8,128)(2,1)S(1)}, bf16[768,768]{1,0:T(8,128)(2,1)}, u32[]{:S(2)}) copy-start(bf16[768,768]{1,0:T(8,128)(2,1)} %ws.1) | copy-start | bytes 3538948
  3.2 18.7 %copy-start.4 = (bf16[768,768]{1,0:T(8,128)(2,1)S(1)}, bf16[768,768]{1,0:T(8,128)(2,1)}, u32[]{:S(2)}) copy-start(bf16[768,768]{1,0:T(8,128)(2,1)} %wc.1) | copy-start | bytes 3538948
  3.2 18.7 %copy-start.12 = (f32[768]{0:T(1024)S(1)}, f32[768]{0:T(1024)}, u32[]{:S(2)}) copy-start(f32[768]{0:T(1024)} %gain.4) | copy-start | bytes 9220
  3.2 18.7 %copy-start.13 = (f32[768]{0:T(1024)S(1)}, f32[768]{0:T(1024)}, u32[]{:S(2)}) copy-start(f32[768]{0:T(1024)} %shift.4) | copy-start | bytes 9220
  3.2 28.1 %all-to-all-start = ((bf16[64,32,128]{2,1,0:T(8,128)(2,1)}), bf16[64,32,128]{2,1,0:T(8,128)(2,1)}, u32[]{:S(2)}, u32[]{:S(2)}) async-start(bf16[64,32,128]{2,1,0:T(8,128)(2,1)} %bitcast.10), calls=%async_computation | async-start | bytes 1048576 | tf_op jit(solution)/shard_map/all_to_all | solution.py:296
  15.9 7.7 %copy-start.3 = (bf16[256,768]{1,0:T(8,128)(2,1)}, bf16[256,768]{1,0:T(8,128)(2,1)S(1)}, u32[]{:S(2)}) copy-start(bf16[256,768]{1,0:T(8,128)(2,1)S(1)} %self_norm.1.h_ref.refs_0_) | copy-start | bytes 1179652
  15.9 30.9 %collective-permute-start.2 = (bf16[256,768]{1,0:T(8,128)(2,1)S(1)}, bf16[256,768]{1,0:T(8,128)(2,1)}, u32[]{:S(2)}, u32[]{:S(2)}) collective-permute-start(bf16[256,768]{1,0:T(8,128)(2,1)S(1)} %self_norm.1.h_ref.refs_0_), channel_id=1, source_target_pairs={{0,2},{1,3},{2,0},{3,1},{4,6},{5,7},{6,4},{7,5},{8,10},{9,11},{10,... | collective-permute-start | bytes 1179656 | tf_op jit(solution)/shard_map/ppermute | solution.py:273
  19.2 28.6 %collective-permute-start.1 = (bf16[256,768]{1,0:T(8,128)(2,1)S(1)}, bf16[256,768]{1,0:T(8,128)(2,1)}, u32[]{:S(2)}, u32[]{:S(2)}) collective-permute-start(bf16[256,768]{1,0:T(8,128)(2,1)S(1)} %self_norm.1.h_ref.refs_0_), channel_id=1, source_target_pairs={{0,3},{1,0},{2,1},{3,2},{4,7},{5,4},{6,5},{7,6},{8,11},{9,8},{10,9... | collective-permute-start | bytes 1179656 | tf_op jit(solution)/shard_map/ppermute | solution.py:273
  20.2 27.6 %collective-permute-start = (bf16[256,768]{1,0:T(8,128)(2,1)S(1)}, bf16[256,768]{1,0:T(8,128)(2,1)}, u32[]{:S(2)}, u32[]{:S(2)}) collective-permute-start(bf16[256,768]{1,0:T(8,128)(2,1)S(1)} %self_norm.1.h_ref.refs_0_), channel_id=1, source_target_pairs={{0,1},{1,2},{2,3},{3,0},{4,5},{5,6},{6,7},{7,4},{8,9},{9,10},{10,1... | collective-permute-start | bytes 1179656 | tf_op jit(solution)/shard_map/ppermute | solution.py:273
  23.6 0.7 copy-start.14
  33.8 25.8 %all-to-all-start.1 = ((bf16[64,24,128]{2,1,0:T(8,128)(2,1)}), bf16[64,24,128]{2,1,0:T(8,128)(2,1)}, u32[]{:S(2)}, u32[]{:S(2)}) async-start(bf16[64,24,128]{2,1,0:T(8,128)(2,1)} %bitcast.4), calls=%async_computation.1 | async-start | bytes 786432 | tf_op jit(solution)/shard_map/all_to_all | solution.py:320
  42.4 19.4 %copy-start = (bf16[768,768]{1,0:T(8,128)(2,1)S(1)}, bf16[768,768]{1,0:T(8,128)(2,1)}, u32[]{:S(2)}) copy-start(bf16[768,768]{1,0:T(8,128)(2,1)} %wk.5) | copy-start | bytes 3538948
  42.5 19.4 %copy-start.1 = (bf16[768,768]{1,0:T(8,128)(2,1)S(1)}, bf16[768,768]{1,0:T(8,128)(2,1)}, u32[]{:S(2)}) copy-start(bf16[768,768]{1,0:T(8,128)(2,1)} %wv.5) | copy-start | bytes 3538948
  42.5 16.4 %collective-permute-start.5 = (bf16[64,8,128]{2,1,0:T(8,128)(2,1)S(1)}, bf16[64,8,128]{2,1,0:T(8,128)(2,1)S(1)}, u32[]{:S(2)}, u32[]{:S(2)}) collective-permute-start(bf16[64,8,128]{2,1,0:T(8,128)(2,1)S(1)} %slice.14.p0), channel_id=1, source_target_pairs={{0,2},{1,3},{2,0},{3,1},{4,6},{5,7},{6,4},{7,5},{8,10},{9,11},{10,... | collective-permute-start | bytes 393224 | tf_op jit(solution)/shard_map/ppermute | solution.py:273
  45.7 13.2 %collective-permute-start.4 = (bf16[64,8,128]{2,1,0:T(8,128)(2,1)S(1)}, bf16[64,8,128]{2,1,0:T(8,128)(2,1)S(1)}, u32[]{:S(2)}, u32[]{:S(2)}) collective-permute-start(bf16[64,8,128]{2,1,0:T(8,128)(2,1)S(1)} %slice.14.p0), channel_id=1, source_target_pairs={{0,3},{1,0},{2,1},{3,2},{4,7},{5,4},{6,5},{7,6},{8,11},{9,8},{10,9... | collective-permute-start | bytes 393224 | tf_op jit(solution)/shard_map/ppermute | solution.py:273
  46.8 12.1 %collective-permute-start.3 = (bf16[64,8,128]{2,1,0:T(8,128)(2,1)S(1)}, bf16[64,8,128]{2,1,0:T(8,128)(2,1)S(1)}, u32[]{:S(2)}, u32[]{:S(2)}) collective-permute-start(bf16[64,8,128]{2,1,0:T(8,128)(2,1)S(1)} %slice.14.p0), channel_id=1, source_target_pairs={{0,1},{1,2},{2,3},{3,0},{4,5},{5,6},{6,7},{7,4},{8,9},{9,10},{10,1... | collective-permute-start | bytes 393224 | tf_op jit(solution)/shard_map/ppermute | solution.py:273
  58.9 0.7 copy-start.8
  59.6 10.6 %collective-permute-start.8 = (bf16[256,768]{1,0:T(8,128)(2,1)}, bf16[256,768]{1,0:T(8,128)(2,1)S(1)}, u32[]{:S(2)}, u32[]{:S(2)}) collective-permute-start(bf16[256,768]{1,0:T(8,128)(2,1)} %bitcast.7.m0), channel_id=1, source_target_pairs={{0,3},{1,0},{2,1},{3,2},{4,7},{5,4},{6,5},{7,6},{8,11},{9,8},{10,9... | collective-permute-start | bytes 1179656 | tf_op jit(solution)/shard_map/ppermute | solution.py:325
  61.9 11.9 %collective-permute-start.6 = (bf16[256,768]{1,0:T(8,128)(2,1)}, bf16[256,768]{1,0:T(8,128)(2,1)S(1)}, u32[]{:S(2)}, u32[]{:S(2)}) collective-permute-start(bf16[256,768]{1,0:T(8,128)(2,1)} %bitcast.7.m0), channel_id=1, source_target_pairs={{0,1},{1,2},{2,3},{3,0},{4,5},{5,6},{6,7},{7,4},{8,9},{9,10},{10,1... | collective-permute-start | bytes 1179656 | tf_op jit(solution)/shard_map/ppermute | solution.py:324
  61.9 0.9 %copy-start.9 = (bf16[64,8,128]{2,1,0:T(8,128)(2,1)S(1)}, bf16[64,8,128]{2,1,0:T(8,128)(2,1)}, u32[]{:S(2)}) copy-start(bf16[64,8,128]{2,1,0:T(8,128)(2,1)} %copy-done.8) | copy-start | bytes 393220
  70.2 11.3 %collective-permute-start.9 = (bf16[128,768]{1,0:T(8,128)(2,1)S(1)}, bf16[128,768]{1,0:T(8,128)(2,1)S(1)}, u32[]{:S(2)}, u32[]{:S(2)}) collective-permute-start(bf16[128,768]{1,0:T(8,128)(2,1)S(1)} %slice.16), channel_id=1, source_target_pairs={{0,3},{1,0},{2,1},{3,2},{4,7},{5,4},{6,5},{7,6},{8,11},{9,8},{10,9... | collective-permute-start | bytes 589832 | tf_op jit(solution)/shard_map/ppermute | solution.py:327
  73.8 7.8 %copy-start.6 = (bf16[768,768]{1,0:T(8,128)(2,1)S(1)}, bf16[768,768]{1,0:T(8,128)(2,1)}, u32[]{:S(2)}) copy-start(bf16[768,768]{1,0:T(8,128)(2,1)} %wo.1) | copy-start | bytes 3538948
  73.8 7.8 %copy-start.7 = (f32[256,768]{1,0:T(8,128)S(1)}, f32[256,768]{1,0:T(8,128)}, u32[]{:S(2)}) copy-start(f32[256,768]{1,0:T(8,128)} %self_attention.1.b_ref) | copy-start | bytes 2359300
  73.8 7.7 %collective-permute-start.7 = (bf16[128,768]{1,0:T(8,128)(2,1)S(1)}, bf16[128,768]{1,0:T(8,128)(2,1)S(1)}, u32[]{:S(2)}, u32[]{:S(2)}) collective-permute-start(bf16[128,768]{1,0:T(8,128)(2,1)S(1)} %slice.15), channel_id=1, source_target_pairs={{0,1},{1,2},{2,3},{3,0},{4,5},{5,6},{6,7},{7,4},{8,9},{9,10},{10,1... | collective-permute-start | bytes 589832 | tf_op jit(solution)/shard_map/ppermute | solution.py:326

commit v3 on v2

--- a/solution.py
+++ b/solution.py
@@ -1,3 +1,5 @@
+import functools
+
 import jax
 import jax.numpy as jnp
 from jax import lax
@@ -68,11 +70,6 @@
 
 def mm_tn(left, right):
     return lax.dot_general(left, right, (((0,), (0,)), ((), ())), preferred_element_type=jnp.float32)
-
-
-def project(refs, w, out):
-    for i, ref in enumerate(refs):
-        out[i * ROWS : (i + 1) * ROWS] = mm(ref[...], w).astype(BF)
 
 
 def pack_kernel(cams, x_ref, gain, shift, o_ref):
@@ -107,33 +104,6 @@
     s_ref[...] = mm(h_ref[...], ws[...]).astype(BF) * BF(0.125)
 
 
-def self_kernel(*refs):
-    sources, o_ref, held, k_ref, v_ref, c_ref, sems = refs[:9], refs[9], refs[10:19], *refs[19:23]
-    copies = [
-        pltpu.make_async_copy(src, dst, sems.at[i])
-        for i, (src, dst) in enumerate(zip(sources, held))
-    ]
-    for copy in copies:
-        copy.start()
-    (h0, wk, h1, h2, h3, wv, q_ref, x_ref, wo) = held
-    copies[0].wait()
-    copies[1].wait()
-    for i, h in enumerate((h0, h1, h2, h3)):
-        if i:
-            copies[i + 1].wait()
-        k_ref[i * ROWS : (i + 1) * ROWS] = mm(h[...], wk[...]).astype(BF)
-    copies[5].wait()
-    for i, h in enumerate((h0, h1, h2, h3)):
-        v_ref[i * ROWS : (i + 1) * ROWS] = mm(h[...], wv[...]).astype(BF)
-    copies[6].wait()
-    for step in range(STEPS):
-        at = slice(step * COLS, (step + 1) * COLS)
-        c_ref[:, at] = attend(q_ref[:, at], k_ref[:, at], v_ref[:, at]).astype(BF)
-    copies[7].wait()
-    copies[8].wait()
-    o_ref[...] = x_ref[...].astype(jnp.float32) + mm(c_ref[...], wo[...])
-
-
 def camera_kernel(p0, p1, p2, p3, q_ref, wk, wv, c_ref, m_ref):
     @pl.when(pl.program_id(0) == 0)
     def _():
@@ -155,32 +125,120 @@
         c_ref[at] = c * (1.0 / total)
 
 
-def early_kernel(m0, m1, m2, q_ref, wk, wv, c_ref, t_ref, l_ref, k_ref, v_ref):
-    project((m0, m1, m2), wk[...], k_ref)
-    project((m0, m1, m2), wv[...], v_ref)
-    for at, head, top, total, c in heads_t(q_ref[...], k_ref[...], jnp.transpose(v_ref[...])):
-        c_ref[at] = c
-        t_ref[head : head + 1] = top
-        l_ref[head : head + 1] = total
-
-
-def late_kernel(ma, mb, q_ref, wk, wv, wo, c_ref, t_ref, l_ref, cam_ref, b_ref, o_ref):
-    @pl.when(pl.program_id(0) == 0)
-    def _():
-        o_ref[...] = b_ref[...]
-
-    m = jnp.concatenate([ma[...], mb[...]], axis=0)
-    k = mm(m, wk[...]).astype(BF)
-    v = mm(m, wv[...]).astype(BF)
-    ctx = []
-    for at, head, top, total, c in heads_t(q_ref[...], k, jnp.transpose(v)):
+def keys_values(blocks, wk, wv):
+    m = blocks[0][...] if len(blocks) == 1 else jnp.concatenate([r[...] for r in blocks], axis=0)
+    return mm(m, wk[...]).astype(BF), jnp.transpose(mm(m, wv[...]).astype(BF))
+
+
+def merged(parts, state):
+    c_ref, t_ref, l_ref = state
+    for at, head, top, total, c in parts:
         top0 = t_ref[head : head + 1]
         best = jnp.maximum(top, top0)
         w0 = jnp.exp(top0 - best)
         w1 = jnp.exp(top - best)
-        down = 1.0 / (w0 * l_ref[head : head + 1] + w1 * total)
-        ctx.append(c_ref[at] * (w0 * down) + c * (w1 * down) + cam_ref[at])
+        yield at, head, best, w0 * l_ref[head : head + 1] + w1 * total, c_ref[at] * w0 + c * w1
+
+
+def part_kernel(blocks, *refs):
+    q_ref, wk, wv, c_ref, t_ref, l_ref = refs[blocks:][-6:]
+    k, vt = keys_values(refs[:blocks], wk, wv)
+    parts = heads_t(q_ref[...], k, vt)
+    state = refs[blocks : len(refs) - 6]
+    for at, head, top, total, c in merged(parts, state) if state else parts:
+        c_ref[at] = c
+        t_ref[head : head + 1] = top
+        l_ref[head : head + 1] = total
+
+
+def last_kernel(blocks, *refs):
+    *extra, q_ref, wk, wv, wo, c_ref, t_ref, l_ref, b_ref, o_ref = refs[blocks:]
+
+    @pl.when(pl.program_id(0) == 0)
+    def _():
+        o_ref[...] = b_ref[...].astype(jnp.float32)
+
+    k, vt = keys_values(refs[:blocks], wk, wv)
+    ctx = []
+    for at, _, _, total, c in merged(heads_t(q_ref[...], k, vt), (c_ref, t_ref, l_ref)):
+        c = c * (1.0 / total)
+        ctx.append(c + extra[0][at] if extra else c)
     o_ref[...] += mm_tn(jnp.concatenate(ctx, axis=0).astype(BF), wo[...])
+
+
+def others_kernel(*refs):
+    h1, h2, h3, wk, q, wv, c, t, l, x, wo = refs[:11]
+    o_ref = refs[11]
+    hb, kb, qb, vb, cb, tb, lb, xb, ob, sems = refs[12:]
+    moves = {}
+
+    def start(name, src, dst):
+        moves[name] = pltpu.make_async_copy(src, dst, sems.at[len(moves)])
+        moves[name].start()
+
+    def weights(step):
+        at = pl.ds(step * COLS, COLS)
+        start(("k", step), wk.at[:, at], kb.at[:, at])
+        start(("v", step), wv.at[:, at], vb.at[:, at])
+
+    for i, h in enumerate((h1, h2, h3)):
+        start(("h", i), h, hb.at[pl.ds(i * ROWS, ROWS)])
+        if i == 0:
+            weights(0)
+    start("q", q, qb)
+    ctx = []
+    for step in range(STEPS):
+        at = slice(step * COLS, (step + 1) * COLS)
+        moves[("k", step)].wait()
+        moves[("v", step)].wait()
+        if step == 0:
+            for i in range(3):
+                moves[("h", i)].wait()
+            moves["q"].wait()
+            for name, src, dst in (("c", c, cb), ("t", t, tb), ("l", l, lb)):
+                start(name, src, dst)
+        if step + 1 < STEPS:
+            weights(step + 1)
+        if step == 1:
+            start("x", x, xb)
+            start("o", wo, ob)
+        k = mm(hb[...], kb[:, at]).astype(BF)
+        vt = jnp.transpose(mm(hb[...], vb[:, at]).astype(BF))
+        parts = heads_t(qb[:, at], k, vt)
+        if step == 0:
+            for name in "ctl":
+                moves[name].wait()
+        state = (
+            cb.at[pl.ds(step * COLS, COLS)],
+            tb.at[pl.ds(step * 8, 8)],
+            lb.at[pl.ds(step * 8, 8)],
+        )
+        for _, _, _, total, value in merged(parts, state):
+            ctx.append((value * (1.0 / total)).astype(BF))
+    moves["x"].wait()
+    moves["o"].wait()
+    o_ref[...] = xb[...].astype(jnp.float32) + mm_tn(jnp.concatenate(ctx, axis=0), ob[...])
+
+
+def call_others(others, q, wk, wv, wo, state, tokens):
+    operands = (*others, wk, q, wv, *state, tokens, wo)
+    buffers = [(3 * ROWS, D), (D, D), (ROWS, D), (D, D)]
+    return pl.pallas_call(
+        others_kernel,
+        in_specs=[pl.BlockSpec(memory_space=pl.ANY)] * len(operands),
+        out_specs=pl.BlockSpec(memory_space=pltpu.VMEM),
+        out_shape=shape(ROWS, D, dtype=jnp.float32),
+        scratch_shapes=[pltpu.VMEM(dims, BF) for dims in buffers]
+        + [pltpu.VMEM(value.shape, value.dtype) for value in (*state, tokens, wo)]
+        + [pltpu.SemaphoreType.DMA((15,))],
+        compiler_params=pltpu.CompilerParams(vmem_limit_bytes=60 * 1024 * 1024),
+        cost_estimate=pl.CostEstimate(
+            flops=12 * ROWS * D * D + 48 * ROWS * ROWS * D,
+            bytes_accessed=8 * D * D,
+            transcendentals=0,
+        ),
+        name="self_others",
+    )(*operands)
 
 
 def full(shape):
@@ -221,40 +279,41 @@
 
 
 def call_pack(camera_rows, tokens, gain, shift):
+    vmem = pl.BlockSpec(memory_space=pltpu.VMEM)
     return pl.pallas_call(
         pack_kernel,
-        grid_spec=pltpu.PrefetchScalarGridSpec(
-            num_scalar_prefetch=1,
-            grid=(1,),
-            in_specs=[
-                pl.BlockSpec((ROWS, D), lambda i, *_: (0, 0)),
-                pl.BlockSpec((D,), lambda i, *_: (0,)),
-                pl.BlockSpec((D,), lambda i, *_: (0,)),
-            ],
-            out_specs=pl.BlockSpec((ROWS // 8, 2, 4, 8, 128), lambda i, *_: (0, 0, 0, 0, 0)),
-        ),
+        in_specs=[pl.BlockSpec(memory_space=pltpu.SMEM), vmem, vmem, vmem],
+        out_specs=vmem,
         out_shape=shape(ROWS // 8, 2, 4, 8, 128),
         name="memory_norm",
     )(camera_rows, tokens, gain, shift)
 
 
-def call_self(*operands):
-    return pl.pallas_call(
-        self_kernel,
-        in_specs=[pl.BlockSpec(memory_space=pl.ANY)] * 9,
-        out_specs=pl.BlockSpec(memory_space=pltpu.VMEM),
-        out_shape=shape(ROWS, D, dtype=jnp.float32),
-        scratch_shapes=[pltpu.VMEM(v.shape, BF) for v in operands]
-        + [pltpu.VMEM((VIEW, D), BF)] * 2
-        + [pltpu.VMEM((ROWS, D), BF), pltpu.SemaphoreType.DMA((9,))],
-        compiler_params=pltpu.CompilerParams(vmem_limit_bytes=60 * 1024 * 1024),
-        cost_estimate=pl.CostEstimate(
-            flops=4 * VIEW * D * D + 16 * ROWS * VIEW * D,
-            bytes_accessed=10 * D * D,
-            transcendentals=0,
-        ),
-        name="self_attention",
-    )(*operands)
+def call_part(name, blocks, state, *rest):
+    rows = sum(b.shape[0] for b in blocks)
+    return call(
+        name,
+        functools.partial(part_kernel, len(blocks)),
+        [full(b.shape) for b in blocks] + [CTX, STAT, STAT][: len(state)] + [XCOL, WCOL, WCOL],
+        [CTX, STAT, STAT],
+        [shape(n, ROWS, dtype=jnp.float32) for n in (D, 8 * STEPS, 8 * STEPS)],
+        work=4 * rows * D * D + 16 * rows * ROWS * D,
+    )(*blocks, *state, *rest)
+
+
+def call_last(name, blocks, extra, rest, state, base, limit=32):
+    rows = sum(b.shape[0] for b in blocks)
+    return call(
+        name,
+        functools.partial(last_kernel, len(blocks)),
+        [full(b.shape) for b in blocks]
+        + [CTX] * len(extra)
+        + [XCOL, WCOL, WCOL, WROW, CTX, STAT, STAT, X],
+        X,
+        shape(ROWS, D, dtype=jnp.float32),
+        work=4 * rows * D * D + 16 * rows * ROWS * D + 2 * ROWS * D * D,
+        limit=limit,
+    )(*blocks, *extra, *rest, *state, base)
 
 
 def to_tiles(x):
@@ -314,12 +373,15 @@
         [pltpu.VMEM((ROWS, D), BF)],
         work=4 * ROWS * D * D,
     )(tokens, hidden, query_gain, query_shift, cross_query, self_query)
-    sq, onward = lax.optimization_barrier((sq, onward))
-    base = call_self(hidden, self_key, *others, self_value, sq, tokens, self_output)
+    self_state = call_part("self_own", [hidden], [], sq, self_key, self_value)
+    *self_state, onward = lax.optimization_barrier((*self_state, onward))
+    base = call_others(
+        others, sq, self_key, self_value, self_output, self_state, tokens
+    )
 
     mine = lax.all_to_all(onward, ROUTE, split_axis=0, concat_axis=0, tiled=True)
     cam_parts = [cam_own] + around(cam_own)
-    mine, base, cq, *cam_parts = lax.optimization_barrier((mine, base, cq, *cam_parts))
+    mine, base, *cam_parts[1:] = lax.optimization_barrier((mine, base, *cam_parts[1:]))
     mine = from_tiles(mine)
     near_a = lax.ppermute(mine, "tok", turn(1))
     near_b = lax.ppermute(mine, "tok", turn(3))
@@ -334,23 +396,16 @@
         [pltpu.VMEM((2 * PIECES, D), BF)],
         work=4 * 128 * D * D + 16 * ROWS * 128 * D,
     )(*cam_parts, cq, cross_key, cross_value)
-    ctx, tops, sums = call(
-        "cross_early",
-        early_kernel,
-        [X] * 3 + [XCOL, WCOL, WCOL],
-        [CTX, STAT, STAT],
-        [shape(n, ROWS, dtype=jnp.float32) for n in (D, 8 * STEPS, 8 * STEPS)],
-        [pltpu.VMEM((3 * ROWS, COLS), BF)] * 2,
-        work=12 * ROWS * D * D + 48 * ROWS * ROWS * D,
-    )(mine, near_a, near_b, cq, cross_key, cross_value)
-    return call(
-        "cross_late",
-        late_kernel,
-        [HALF, HALF, XCOL, WCOL, WCOL, WROW, CTX, STAT, STAT, CTX, X],
-        X,
-        shape(ROWS, D, dtype=jnp.float32),
-        work=4 * ROWS * D * D + 16 * ROWS * ROWS * D,
-    )(far_a, far_b, cq, cross_key, cross_value, cross_output, ctx, tops, sums, cam_ctx, base)
+    state = call_part("cross_own", [mine], [], cq, cross_key, cross_value)
+    state = call_part("cross_near", [near_a, near_b], state, cq, cross_key, cross_value)
+    return call_last(
+        "cross_far",
+        [far_a, far_b],
+        [cam_ctx],
+        (cq, cross_key, cross_value, cross_output),
+        state,
+        base,
+    )
 
 
 def solution(mesh):

time: 86.7 us -> 82.5 us (0.952)
  waiting for transfers between devices: 11 us -> 3.15 us
  Pallas kernels: 31.8 us -> 33.6 us
  local copies, waits for them, and re-layouts: 6.32 us -> 7.64 us
    all_to_all x1, waiting for transfers between devices: 6.89 us -> 2.62 us  [local(): lax.all_to_all(packed, ROUTE, split_axis=0, concat_axis=0, tiled=True)]
    ppermute x1, waiting for transfers between devices: 4.11 us -> 0.01 us  [local(): near_b = lax.ppermute(mine, 'tok', turn(3))]
    pallas_call x4 -> x6, Pallas kernels: 26.4 us -> 28.2 us  [the longest x3 11.4 us: call_part(): call(name, functools.partial(part_kernel, len(blocks)), [full(b.shape) fo...]
    unnamed x32 -> x40, local copies, waits for them, and re-layouts: 2.34 us -> 3.7 us
  transfers between devices with their start and end apart: 12 -> 12, of which waited for: 2 -> 2; matrix products, arithmetic and copies ran while one was open for 5% -> 5% of each run, Pallas kernels for 28% -> 32%
where the time goes in v3:
time: 82.5 us; the launch traced here: 82.1 us
  starting transfers between devices  37.3 us (45%)
  Pallas kernels  33.6 us (41%)
  local copies, waits for them, and re-layouts  7.64 us (9%)
  waiting for transfers between devices  3.15 us (4%)
    all_to_all x1, starting transfers between devices, local(): lax.all_to_all(packed, ROUTE, split_axis=0, concat_axis=0, tiled=True)  12.3 us
    pallas_call x3, Pallas kernels, call_part(): call(name, functools.partial(part_kernel, len(blocks)), [full(b.shape) fo...  11.4 us
    ppermute x6, starting transfers between devices, around(): return [lax.ppermute(value, 'tok', turn(shift)) for shift in (1, 3, 2)]  10.6 us
    pallas_call x1, Pallas kernels, call_others(): pl.pallas_call(others_kernel, in_specs=[pl.BlockSpec(memory_space=pl.ANY)...  9.68 us
    all_to_all x1, starting transfers between devices, local(): lax.all_to_all(onward, ROUTE, split_axis=0, concat_axis=0, tiled=True)  7.74 us
    pallas_call x1, Pallas kernels, call_last(): call(name, functools.partial(last_kernel, len(blocks)), [full(b.shape) fo...  4.73 us
    unnamed x40, local copies, waits for them, and re-layouts  3.7 us
    pallas_call x1, Pallas kernels, local(): call('camera_attention', camera_kernel, [CAMS] * 4 + [XCOL, WCOL, WCOL],...  3.31 us
  transfers between devices with their start and end apart: 12, of which 2 were waited for; matrix products, arithmetic and copies ran while one was open for 5% of the time, Pallas kernels for 32%

profile of v3, /device:TPU:2, one launch (start us, length us, event | category | flops | bytes accessed | tf_op | source)
XLA Modules:
  0.0 82.1 jit_solution(3363776715546698231)
XLA Ops:
  0.0 2.4 %memory_norm.1 = bf16[32,2,4,8,128]{4,3,2,1,0:T(8,128)(2,1)} custom-call(s32[8,16]{1,0:T(8,128)} %cams.1, bf16[256,768]{1,0:T(8,128)(2,1)} %refs_9_.1, f32[768]{0:T(1024)} %gain.5, f32[768]{0:T(1024)} %shift.5), custom_call_target="tpu_custom_call" | custom-call | tf_op jit(solution)/shard_map/memory_norm/pallas_call | solution.py:283
  2.5 12.3 %all-to-all-start = ((bf16[64,32,128]{2,1,0:T(8,128)(2,1)}), bf16[64,32,128]{2,1,0:T(8,128)(2,1)}, u32[]{:S(2)}, u32[]{:S(2)}) async-start(bf16[64,32,128]{2,1,0:T(8,128)(2,1)} %bitcast.10), calls=%async_computation | async-start | bytes 1048576 | tf_op jit(solution)/shard_map/all_to_all | solution.py:355
  14.8 0.3 self_norm.1.h_ref.refs_0_
  15.2 1.7 %collective-permute-start = (bf16[256,768]{1,0:T(8,128)(2,1)S(1)}, bf16[256,768]{1,0:T(8,128)(2,1)}, u32[]{:S(2)}, u32[]{:S(2)}) collective-permute-start(bf16[256,768]{1,0:T(8,128)(2,1)S(1)} %self_norm.1.h_ref.refs_0_), channel_id=1, source_target_pairs={{0,1},{1,2},{2,3},{3,0},{4,5},{5,6},{6,7},{7,4},{8,9},{9,10},{10,1... | collective-permute-start | bytes 1179656 | tf_op jit(solution)/shard_map/ppermute | solution.py:332
  16.8 1.7 %collective-permute-start.1 = (bf16[256,768]{1,0:T(8,128)(2,1)S(1)}, bf16[256,768]{1,0:T(8,128)(2,1)}, u32[]{:S(2)}, u32[]{:S(2)}) collective-permute-start(bf16[256,768]{1,0:T(8,128)(2,1)S(1)} %self_norm.1.h_ref.refs_0_), channel_id=1, source_target_pairs={{0,3},{1,0},{2,1},{3,2},{4,7},{5,4},{6,5},{7,6},{8,11},{9,8},{10,9... | collective-permute-start | bytes 1179656 | tf_op jit(solution)/shard_map/ppermute | solution.py:332
  18.5 2.0 %collective-permute-start.2 = (bf16[256,768]{1,0:T(8,128)(2,1)S(1)}, bf16[256,768]{1,0:T(8,128)(2,1)}, u32[]{:S(2)}, u32[]{:S(2)}) collective-permute-start(bf16[256,768]{1,0:T(8,128)(2,1)S(1)} %self_norm.1.h_ref.refs_0_), channel_id=1, source_target_pairs={{0,2},{1,3},{2,0},{3,1},{4,6},{5,7},{6,4},{7,5},{8,10},{9,11},{10,... | collective-permute-start | bytes 1179656 | tf_op jit(solution)/shard_map/ppermute | solution.py:332
  20.5 0.1 reshape.151
  20.6 0.1 copy.19
  20.9 0.1 add.108
  21.1 1.7 %queries.1 = (bf16[256,768]{1,0:T(8,128)(2,1)S(1)}, bf16[256,768]{1,0:T(8,128)(2,1)S(1)}) custom-call(bf16[256,768]{1,0:T(8,128)(2,1)S(1)} %copy-done.2, bf16[256,768]{1,0:T(8,128)(2,1)S(1)} %self_norm.1.h_ref.refs_0_, f32[768]{0:T(1024)S(1)} %copy-done.11, f32[768]{0:T(1024)S(1)} %copy-done.12, bf16[768,768]{1,0:T(8,128)(2,1)S(1)} %copy-done.3, ...), custom_call_target="tpu_custom_call" | custom-call | flops 603979776 | bytes 2359296 | tf_op jit(solution)/shard_map/queries/pallas_call | solution.py:367
  22.9 2.9 %self_own.1 = (f32[768,256]{1,0:T(8,128)S(1)}, f32[24,256]{1,0:T(8,128)S(1)}, f32[24,256]{1,0:T(8,128)S(1)}) custom-call(bf16[256,768]{1,0:T(8,128)(2,1)S(1)} %self_norm.1.h_ref.refs_0_, bf16[256,768]{1,0:T(8,128)(2,1)S(1)} %get-tuple-element.25.refs_1_.refs_4_, bf16[768,768]{1,0:T(8,128)(2,1)S(1)} %copy-done.13, bf16[768,768]{1,0:T(8,128)(2,1)S(1)} %copy-done.14), custom_call_target="tpu_custom_call" | custom-call | flops 1409286144 | bytes 2359296 | tf_op jit(solution)/shard_map/self_own/pallas_call | solution.py:294
  25.8 0.9 %copy-done.16 = f32[768,256]{1,0:T(8,128)} copy-done((f32[768,256]{1,0:T(8,128)}, f32[768,256]{1,0:T(8,128)S(1)}, u32[]{:S(2)}) %copy-start.16) | copy-done | bytes 786456
  26.7 0.6 copy-done.17
  27.3 0.6 copy-done.18
  27.9 2.6 %all-to-all-done = bf16[64,32,128]{2,1,0:T(8,128)(2,1)} async-done(((bf16[64,32,128]{2,1,0:T(8,128)(2,1)}), bf16[64,32,128]{2,1,0:T(8,128)(2,1)}, u32[]{:S(2)}, u32[]{:S(2)}) %all-to-all-start) | async-done | bytes 524320 | tf_op jit(solution)/shard_map/all_to_all | solution.py:355
  30.6 2.5 %gather_fusion = bf16[192,8,128]{2,1,0:T(8,128)(2,1)} fusion(bf16[256,8,128]{2,1,0:T(8,128)(2,1)} %bitcast.1, s32[1024]{0:T(1024)S(1)} %pad_clamp_fusion), kind=kCustom, calls=%fused_computation | custom fusion | bytes 787200 | tf_op jit(solution)/shard_map/gather | solution.py:359
  33.1 7.7 %all-to-all-start.1 = ((bf16[64,24,128]{2,1,0:T(8,128)(2,1)}), bf16[64,24,128]{2,1,0:T(8,128)(2,1)}, u32[]{:S(2)}, u32[]{:S(2)}) async-start(bf16[64,24,128]{2,1,0:T(8,128)(2,1)} %bitcast.4), calls=%async_computation.1 | async-start | bytes 786432 | tf_op jit(solution)/shard_map/all_to_all | solution.py:382
  40.8 0.9 %slice.14.p0 = bf16[64,8,128]{2,1,0:T(8,128)(2,1)S(1)} slice(bf16[64,32,128]{2,1,0:T(8,128)(2,1)} %all-to-all-done), slice={[0:64], [24:32], [0:128]} | slice | bytes 262144 | tf_op jit(solution)/shard_map/slice | solution.py:361
  41.7 1.6 %collective-permute-start.3 = (bf16[64,8,128]{2,1,0:T(8,128)(2,1)S(1)}, bf16[64,8,128]{2,1,0:T(8,128)(2,1)S(1)}, u32[]{:S(2)}, u32[]{:S(2)}) collective-permute-start(bf16[64,8,128]{2,1,0:T(8,128)(2,1)S(1)} %slice.14.p0), channel_id=1, source_target_pairs={{0,1},{1,2},{2,3},{3,0},{4,5},{5,6},{6,7},{7,4},{8,9},{9,10},{10,1... | collective-permute-start | bytes 393224 | tf_op jit(solution)/shard_map/ppermute | solution.py:332
  43.4 1.7 %collective-permute-start.4 = (bf16[64,8,128]{2,1,0:T(8,128)(2,1)S(1)}, bf16[64,8,128]{2,1,0:T(8,128)(2,1)S(1)}, u32[]{:S(2)}, u32[]{:S(2)}) collective-permute-start(bf16[64,8,128]{2,1,0:T(8,128)(2,1)S(1)} %slice.14.p0), channel_id=1, source_target_pairs={{0,3},{1,0},{2,1},{3,2},{4,7},{5,4},{6,5},{7,6},{8,11},{9,8},{10,9... | collective-permute-start | bytes 393224 | tf_op jit(solution)/shard_map/ppermute | solution.py:332
  45.1 2.0 %collective-permute-start.5 = (bf16[64,8,128]{2,1,0:T(8,128)(2,1)S(1)}, bf16[64,8,128]{2,1,0:T(8,128)(2,1)S(1)}, u32[]{:S(2)}, u32[]{:S(2)}) collective-permute-start(bf16[64,8,128]{2,1,0:T(8,128)(2,1)S(1)} %slice.14.p0), channel_id=1, source_target_pairs={{0,2},{1,3},{2,0},{3,1},{4,6},{5,7},{6,4},{7,5},{8,10},{9,11},{10,... | collective-permute-start | bytes 393224 | tf_op jit(solution)/shard_map/ppermute | solution.py:332
  47.0 9.7 %self_others.1.refs_10_ = f32[256,768]{1,0:T(8,128)} custom-call(bf16[256,768]{1,0:T(8,128)(2,1)} %collective-permute-done.refs_0_, bf16[256,768]{1,0:T(8,128)(2,1)} %collective-permute-done.1.refs_1_, bf16[256,768]{1,0:T(8,128)(2,1)} %collective-permute-done.2.refs_2_, bf16[768,768]{1,0:T(8,128)(2,1)} %refs_3_.4, bf16[256,768]{1,0:T(8,128)(2,1)} %copy-done.15, ...), custom_call_target="tpu_custom_call" | custom-call | flops 4227858432 | bytes 4718592 | tf_op jit(solution)/shard_map/self_others/pallas_call | solution.py:226
  56.8 0.6 copy-done.7
  57.4 0.7 collective-permute-start.6
  58.1 2.6 %collective-permute-start.8 = (bf16[256,768]{1,0:T(8,128)(2,1)}, bf16[256,768]{1,0:T(8,128)(2,1)S(1)}, u32[]{:S(2)}, u32[]{:S(2)}) collective-permute-start(bf16[256,768]{1,0:T(8,128)(2,1)} %bitcast.7.refs_0_), channel_id=1, source_target_pairs={{0,3},{1,0},{2,1},{3,2},{4,7},{5,4},{6,5},{7,6},{8,11},{9,8},{10,9... | collective-permute-start | bytes 1179656 | tf_op jit(solution)/shard_map/ppermute | solution.py:387
  60.7 0.9 %copy-done.8 = bf16[64,8,128]{2,1,0:T(8,128)(2,1)S(1)} copy-done((bf16[64,8,128]{2,1,0:T(8,128)(2,1)S(1)}, bf16[64,8,128]{2,1,0:T(8,128)(2,1)}, u32[]{:S(2)}) %copy-start.8) | copy-done | bytes 131096
  61.6 3.3 %camera_attention.1.refs_2_ = f32[768,256]{1,0:T(8,128)S(1)} custom-call(bf16[64,8,128]{2,1,0:T(8,128)(2,1)S(1)} %slice.14.p0, bf16[64,8,128]{2,1,0:T(8,128)(2,1)S(1)} %collective-permute-done.3.p1, bf16[64,8,128]{2,1,0:T(8,128)(2,1)S(1)} %collective-permute-done.4.p2, bf16[64,8,128]{2,1,0:T(8,128)(2,1)S(1)} %copy-done.8, ...), custom_call_target="tpu_custom_call" | custom-call | flops 704643072 | bytes 2359296 | tf_op jit(solution)/shard_map/camera_attention/pallas_call | solution.py:390
  64.9 3.8 %cross_own.1 = (f32[768,256]{1,0:T(8,128)S(1)}, f32[24,256]{1,0:T(8,128)S(1)}, f32[24,256]{1,0:T(8,128)S(1)}) custom-call(bf16[256,768]{1,0:T(8,128)(2,1)} %bitcast.7.refs_0_, bf16[256,768]{1,0:T(8,128)(2,1)S(1)} %get-tuple-element.37.q_ref.refs_1_.refs_5_.refs_3_, bf16[768,768]{1,0:T(8,128)(2,1)S(1)} %copy-done, bf16[768,768]{1,0:T(8,128)(2,1)S(1)} %copy-done.1), custom_call_target="tpu_custom_call" | custom-call | flops 1409286144 | bytes 2359296 | tf_op jit(solution)/shard_map/cross_own/pallas_call | solution.py:294
  68.7 0.5 collective-permute-done.6.refs_0_
  69.4 3.3 %collective-permute-start.9 = (bf16[128,768]{1,0:T(8,128)(2,1)S(1)}, bf16[128,768]{1,0:T(8,128)(2,1)S(1)}, u32[]{:S(2)}, u32[]{:S(2)}) collective-permute-start(bf16[128,768]{1,0:T(8,128)(2,1)S(1)} %slice.16), channel_id=1, source_target_pairs={{0,3},{1,0},{2,1},{3,2},{4,7},{5,4},{6,5},{7,6},{8,11},{9,8},{10,9... | collective-permute-start | bytes 589832 | tf_op jit(solution)/shard_map/ppermute | solution.py:389
  72.7 4.7 %cross_near.1 = (f32[768,256]{1,0:T(8,128)S(1)}, f32[24,256]{1,0:T(8,128)S(1)}, f32[24,256]{1,0:T(8,128)S(1)}) custom-call(bf16[256,768]{1,0:T(8,128)(2,1)S(1)} %collective-permute-done.6.refs_0_, bf16[256,768]{1,0:T(8,128)(2,1)S(1)} %collective-permute-done.8.refs_1_, f32[768,256]{1,0:T(8,128)S(1)} %get-tuple-element.38.refs_2_, ...), custom_call_target="tpu_custom_call" | custom-call | flops 2818572288 | bytes 2359296 | tf_op jit(solution)/shard_map/cross_near/pallas_call | solution.py:294
  77.4 4.7 %cross_far.1 = f32[256,768]{1,0:T(8,128)} custom-call(bf16[128,768]{1,0:T(8,128)(2,1)S(1)} %collective-permute-done.7.refs_0_, bf16[128,768]{1,0:T(8,128)(2,1)S(1)} %collective-permute-done.9.refs_1_, f32[768,256]{1,0:T(8,128)S(1)} %camera_attention.1.refs_2_, bf16[256,768]{1,0:T(8,128)(2,1)S(1)} %get-tuple-element.37.q_ref.refs_1_.refs_5_.refs_3_, ...), custom_call_target="tpu_custom_call" | custom-call | flops 1711276032 | bytes 2359296 | tf_op jit(solution)/shard_map/cross_far/pallas_call | solution.py:306
  (53 shorter events, 0.4 us)
Async XLA Ops:
  0.0 14.8 %copy-start.2 = (bf16[256,768]{1,0:T(8,128)(2,1)S(1)}, bf16[256,768]{1,0:T(8,128)(2,1)}, u32[]{:S(2)}) copy-start(bf16[256,768]{1,0:T(8,128)(2,1)} %refs_9_.1) | copy-start | bytes 1179652
  0.0 14.8 %copy-start.9 = (f32[768]{0:T(1024)S(1)}, f32[768]{0:T(1024)}, u32[]{:S(2)}) copy-start(f32[768]{0:T(1024)} %gain.3) | copy-start | bytes 9220
  0.0 14.8 %copy-start.10 = (f32[768]{0:T(1024)S(1)}, f32[768]{0:T(1024)}, u32[]{:S(2)}) copy-start(f32[768]{0:T(1024)} %shift.3) | copy-start | bytes 9220
  0.0 20.5 %copy-start.19 = (s32[64]{0:T(128)S(1)}, s32[64]{0:T(128)}, u32[]{:S(2)}) copy-start(s32[64]{0:T(128)} %param.32) | copy-start | bytes 772
  0.0 21.1 %copy-start.4 = (bf16[768,768]{1,0:T(8,128)(2,1)S(1)}, bf16[768,768]{1,0:T(8,128)(2,1)}, u32[]{:S(2)}) copy-start(bf16[768,768]{1,0:T(8,128)(2,1)} %ws.1) | copy-start | bytes 3538948
  2.5 18.6 %copy-start.3 = (bf16[768,768]{1,0:T(8,128)(2,1)S(1)}, bf16[768,768]{1,0:T(8,128)(2,1)}, u32[]{:S(2)}) copy-start(bf16[768,768]{1,0:T(8,128)(2,1)} %wc.1) | copy-start | bytes 3538948
  2.5 18.6 %copy-start.11 = (f32[768]{0:T(1024)S(1)}, f32[768]{0:T(1024)}, u32[]{:S(2)}) copy-start(f32[768]{0:T(1024)} %gain.4) | copy-start | bytes 9220
  2.5 18.6 %copy-start.12 = (f32[768]{0:T(1024)S(1)}, f32[768]{0:T(1024)}, u32[]{:S(2)}) copy-start(f32[768]{0:T(1024)} %shift.4) | copy-start | bytes 9220
  2.5 28.1 %all-to-all-start = ((bf16[64,32,128]{2,1,0:T(8,128)(2,1)}), bf16[64,32,128]{2,1,0:T(8,128)(2,1)}, u32[]{:S(2)}, u32[]{:S(2)}) async-start(bf16[64,32,128]{2,1,0:T(8,128)(2,1)} %bitcast.10), calls=%async_computation | async-start | bytes 1048576 | tf_op jit(solution)/shard_map/all_to_all | solution.py:355
  15.2 29.9 %collective-permute-start = (bf16[256,768]{1,0:T(8,128)(2,1)S(1)}, bf16[256,768]{1,0:T(8,128)(2,1)}, u32[]{:S(2)}, u32[]{:S(2)}) collective-permute-start(bf16[256,768]{1,0:T(8,128)(2,1)S(1)} %self_norm.1.h_ref.refs_0_), channel_id=1, source_target_pairs={{0,1},{1,2},{2,3},{3,0},{4,5},{5,6},{6,7},{7,4},{8,9},{9,10},{10,1... | collective-permute-start | bytes 1179656 | tf_op jit(solution)/shard_map/ppermute | solution.py:332
  16.8 30.2 %collective-permute-start.1 = (bf16[256,768]{1,0:T(8,128)(2,1)S(1)}, bf16[256,768]{1,0:T(8,128)(2,1)}, u32[]{:S(2)}, u32[]{:S(2)}) collective-permute-start(bf16[256,768]{1,0:T(8,128)(2,1)S(1)} %self_norm.1.h_ref.refs_0_), channel_id=1, source_target_pairs={{0,3},{1,0},{2,1},{3,2},{4,7},{5,4},{6,5},{7,6},{8,11},{9,8},{10,9... | collective-permute-start | bytes 1179656 | tf_op jit(solution)/shard_map/ppermute | solution.py:332
  18.5 28.5 %collective-permute-start.2 = (bf16[256,768]{1,0:T(8,128)(2,1)S(1)}, bf16[256,768]{1,0:T(8,128)(2,1)}, u32[]{:S(2)}, u32[]{:S(2)}) collective-permute-start(bf16[256,768]{1,0:T(8,128)(2,1)S(1)} %self_norm.1.h_ref.refs_0_), channel_id=1, source_target_pairs={{0,2},{1,3},{2,0},{3,1},{4,6},{5,7},{6,4},{7,5},{8,10},{9,11},{10,... | collective-permute-start | bytes 1179656 | tf_op jit(solution)/shard_map/ppermute | solution.py:332
  21.1 1.8 %copy-start.13 = (bf16[768,768]{1,0:T(8,128)(2,1)S(1)}, bf16[768,768]{1,0:T(8,128)(2,1)}, u32[]{:S(2)}) copy-start(bf16[768,768]{1,0:T(8,128)(2,1)} %refs_3_.4) | copy-start | bytes 3538948
  21.1 1.8 %copy-start.14 = (bf16[768,768]{1,0:T(8,128)(2,1)S(1)}, bf16[768,768]{1,0:T(8,128)(2,1)}, u32[]{:S(2)}) copy-start(bf16[768,768]{1,0:T(8,128)(2,1)} %refs_5_.2) | copy-start | bytes 3538948
  22.9 2.9 %copy-start.15 = (bf16[256,768]{1,0:T(8,128)(2,1)}, bf16[256,768]{1,0:T(8,128)(2,1)S(1)}, u32[]{:S(2)}) copy-start(bf16[256,768]{1,0:T(8,128)(2,1)S(1)} %get-tuple-element.25.refs_1_.refs_4_) | copy-start | bytes 1179652
  25.8 0.9 %copy-start.16 = (f32[768,256]{1,0:T(8,128)}, f32[768,256]{1,0:T(8,128)S(1)}, u32[]{:S(2)}) copy-start(f32[768,256]{1,0:T(8,128)S(1)} %get-tuple-element.30.refs_6_) | copy-start | bytes 2359300
  26.7 0.6 copy-start.17
  27.3 0.6 copy-start.18
  33.1 24.3 %all-to-all-start.1 = ((bf16[64,24,128]{2,1,0:T(8,128)(2,1)}), bf16[64,24,128]{2,1,0:T(8,128)(2,1)}, u32[]{:S(2)}, u32[]{:S(2)}) async-start(bf16[64,24,128]{2,1,0:T(8,128)(2,1)} %bitcast.4), calls=%async_computation.1 | async-start | bytes 786432 | tf_op jit(solution)/shard_map/all_to_all | solution.py:382
  41.7 18.9 %copy-start = (bf16[768,768]{1,0:T(8,128)(2,1)S(1)}, bf16[768,768]{1,0:T(8,128)(2,1)}, u32[]{:S(2)}) copy-start(bf16[768,768]{1,0:T(8,128)(2,1)} %refs_4_.1) | copy-start | bytes 3538948
  41.7 18.9 %copy-start.1 = (bf16[768,768]{1,0:T(8,128)(2,1)S(1)}, bf16[768,768]{1,0:T(8,128)(2,1)}, u32[]{:S(2)}) copy-start(bf16[768,768]{1,0:T(8,128)(2,1)} %refs_5_.3) | copy-start | bytes 3538948
  41.7 15.0 %collective-permute-start.3 = (bf16[64,8,128]{2,1,0:T(8,128)(2,1)S(1)}, bf16[64,8,128]{2,1,0:T(8,128)(2,1)S(1)}, u32[]{:S(2)}, u32[]{:S(2)}) collective-permute-start(bf16[64,8,128]{2,1,0:T(8,128)(2,1)S(1)} %slice.14.p0), channel_id=1, source_target_pairs={{0,1},{1,2},{2,3},{3,0},{4,5},{5,6},{6,7},{7,4},{8,9},{9,10},{10,1... | collective-permute-start | bytes 393224 | tf_op jit(solution)/shard_map/ppermute | solution.py:332
  43.4 13.4 %collective-permute-start.4 = (bf16[64,8,128]{2,1,0:T(8,128)(2,1)S(1)}, bf16[64,8,128]{2,1,0:T(8,128)(2,1)S(1)}, u32[]{:S(2)}, u32[]{:S(2)}) collective-permute-start(bf16[64,8,128]{2,1,0:T(8,128)(2,1)S(1)} %slice.14.p0), channel_id=1, source_target_pairs={{0,3},{1,0},{2,1},{3,2},{4,7},{5,4},{6,5},{7,6},{8,11},{9,8},{10,9... | collective-permute-start | bytes 393224 | tf_op jit(solution)/shard_map/ppermute | solution.py:332
  45.1 11.7 %collective-permute-start.5 = (bf16[64,8,128]{2,1,0:T(8,128)(2,1)S(1)}, bf16[64,8,128]{2,1,0:T(8,128)(2,1)S(1)}, u32[]{:S(2)}, u32[]{:S(2)}) collective-permute-start(bf16[64,8,128]{2,1,0:T(8,128)(2,1)S(1)} %slice.14.p0), channel_id=1, source_target_pairs={{0,2},{1,3},{2,0},{3,1},{4,6},{5,7},{6,4},{7,5},{8,10},{9,11},{10,... | collective-permute-start | bytes 393224 | tf_op jit(solution)/shard_map/ppermute | solution.py:332
  56.7 0.7 copy-start.7
  57.4 11.8 %collective-permute-start.6 = (bf16[256,768]{1,0:T(8,128)(2,1)}, bf16[256,768]{1,0:T(8,128)(2,1)S(1)}, u32[]{:S(2)}, u32[]{:S(2)}) collective-permute-start(bf16[256,768]{1,0:T(8,128)(2,1)} %bitcast.7.refs_0_), channel_id=1, source_target_pairs={{0,1},{1,2},{2,3},{3,0},{4,5},{5,6},{6,7},{7,4},{8,9},{9,10},{10,1... | collective-permute-start | bytes 1179656 | tf_op jit(solution)/shard_map/ppermute | solution.py:386
  58.1 11.3 %collective-permute-start.8 = (bf16[256,768]{1,0:T(8,128)(2,1)}, bf16[256,768]{1,0:T(8,128)(2,1)S(1)}, u32[]{:S(2)}, u32[]{:S(2)}) collective-permute-start(bf16[256,768]{1,0:T(8,128)(2,1)} %bitcast.7.refs_0_), channel_id=1, source_target_pairs={{0,3},{1,0},{2,1},{3,2},{4,7},{5,4},{6,5},{7,6},{8,11},{9,8},{10,9... | collective-permute-start | bytes 1179656 | tf_op jit(solution)/shard_map/ppermute | solution.py:387
  60.7 0.9 %copy-start.8 = (bf16[64,8,128]{2,1,0:T(8,128)(2,1)S(1)}, bf16[64,8,128]{2,1,0:T(8,128)(2,1)}, u32[]{:S(2)}) copy-start(bf16[64,8,128]{2,1,0:T(8,128)(2,1)} %copy-done.7) | copy-start | bytes 393220
  69.3 8.1 %collective-permute-start.7 = (bf16[128,768]{1,0:T(8,128)(2,1)S(1)}, bf16[128,768]{1,0:T(8,128)(2,1)S(1)}, u32[]{:S(2)}, u32[]{:S(2)}) collective-permute-start(bf16[128,768]{1,0:T(8,128)(2,1)S(1)} %slice.15), channel_id=1, source_target_pairs={{0,1},{1,2},{2,3},{3,0},{4,5},{5,6},{6,7},{7,4},{8,9},{9,10},{10,1... | collective-permute-start | bytes 589832 | tf_op jit(solution)/shard_map/ppermute | solution.py:388
  69.4 8.0 %collective-permute-start.9 = (bf16[128,768]{1,0:T(8,128)(2,1)S(1)}, bf16[128,768]{1,0:T(8,128)(2,1)S(1)}, u32[]{:S(2)}, u32[]{:S(2)}) collective-permute-start(bf16[128,768]{1,0:T(8,128)(2,1)S(1)} %slice.16), channel_id=1, source_target_pairs={{0,3},{1,0},{2,1},{3,2},{4,7},{5,4},{6,5},{7,6},{8,11},{9,8},{10,9... | collective-permute-start | bytes 589832 | tf_op jit(solution)/shard_map/ppermute | solution.py:389
  72.7 4.7 %copy-start.5 = (bf16[768,768]{1,0:T(8,128)(2,1)S(1)}, bf16[768,768]{1,0:T(8,128)(2,1)}, u32[]{:S(2)}) copy-start(bf16[768,768]{1,0:T(8,128)(2,1)} %refs_6_.3) | copy-start | bytes 3538948
  72.7 4.7 %copy-start.6 = (f32[256,768]{1,0:T(8,128)S(1)}, f32[256,768]{1,0:T(8,128)}, u32[]{:S(2)}) copy-start(f32[256,768]{1,0:T(8,128)} %self_others.1.refs_10_) | copy-start | bytes 2359300

commit v4 on v3

--- a/solution.py
+++ b/solution.py
@@ -140,30 +140,43 @@
         yield at, head, best, w0 * l_ref[head : head + 1] + w1 * total, c_ref[at] * w0 + c * w1
 
 
+def column_parts(step, q_ref, wk, wv, m, state):
+    at = slice(step * COLS, (step + 1) * COLS)
+    k = mm(m, wk[:, at]).astype(BF)
+    vt = jnp.transpose(mm(m, wv[:, at]).astype(BF))
+    parts = heads_t(q_ref[:, at], k, vt)
+    if not state:
+        return parts
+    c_ref, t_ref, l_ref = state
+    rows = pl.ds(step * 8, 8)
+    return merged(parts, (c_ref.at[pl.ds(step * COLS, COLS)], t_ref.at[rows], l_ref.at[rows]))
+
+
+def joined(blocks):
+    return blocks[0][...] if len(blocks) == 1 else jnp.concatenate([r[...] for r in blocks], axis=0)
+
+
 def part_kernel(blocks, *refs):
     q_ref, wk, wv, c_ref, t_ref, l_ref = refs[blocks:][-6:]
-    k, vt = keys_values(refs[:blocks], wk, wv)
-    parts = heads_t(q_ref[...], k, vt)
-    state = refs[blocks : len(refs) - 6]
-    for at, head, top, total, c in merged(parts, state) if state else parts:
-        c_ref[at] = c
-        t_ref[head : head + 1] = top
-        l_ref[head : head + 1] = total
+    m = joined(refs[:blocks])
+    for step in range(STEPS):
+        for at, head, top, total, c in column_parts(
+            step, q_ref, wk, wv, m, refs[blocks : len(refs) - 6]
+        ):
+            c_ref[step * COLS + at.start : step * COLS + at.stop] = c
+            t_ref[step * 8 + head : step * 8 + head + 1] = top
+            l_ref[step * 8 + head : step * 8 + head + 1] = total
 
 
 def last_kernel(blocks, *refs):
-    *extra, q_ref, wk, wv, wo, c_ref, t_ref, l_ref, b_ref, o_ref = refs[blocks:]
-
-    @pl.when(pl.program_id(0) == 0)
-    def _():
-        o_ref[...] = b_ref[...].astype(jnp.float32)
-
-    k, vt = keys_values(refs[:blocks], wk, wv)
+    extra, q_ref, wk, wv, wo, c_ref, t_ref, l_ref, b_ref, o_ref = refs[blocks:]
+    m = joined(refs[:blocks])
     ctx = []
-    for at, _, _, total, c in merged(heads_t(q_ref[...], k, vt), (c_ref, t_ref, l_ref)):
-        c = c * (1.0 / total)
-        ctx.append(c + extra[0][at] if extra else c)
-    o_ref[...] += mm_tn(jnp.concatenate(ctx, axis=0).astype(BF), wo[...])
+    for step in range(STEPS):
+        for at, _, _, total, c in column_parts(step, q_ref, wk, wv, m, (c_ref, t_ref, l_ref)):
+            c = c * (1.0 / total) + extra[step * COLS + at.start : step * COLS + at.stop]
+            ctx.append(c.astype(BF))
+    o_ref[...] = b_ref[...] + mm_tn(jnp.concatenate(ctx, axis=0), wo[...])
 
 
 def others_kernel(*refs):
@@ -231,7 +244,7 @@
         scratch_shapes=[pltpu.VMEM(dims, BF) for dims in buffers]
         + [pltpu.VMEM(value.shape, value.dtype) for value in (*state, tokens, wo)]
         + [pltpu.SemaphoreType.DMA((15,))],
-        compiler_params=pltpu.CompilerParams(vmem_limit_bytes=60 * 1024 * 1024),
+        compiler_params=pltpu.CompilerParams(vmem_limit_bytes=63 * 1024 * 1024),
         cost_estimate=pl.CostEstimate(
             flops=12 * ROWS * D * D + 48 * ROWS * ROWS * D,
             bytes_accessed=8 * D * D,
@@ -252,6 +265,9 @@
 STAT = pl.BlockSpec((8, ROWS), lambda i: (i, 0))
 VEC = full((D,))
 X = full((ROWS, D))
+W = full((D, D))
+ALL = full((D, ROWS))
+ALLSTAT = full((8 * STEPS, ROWS))
 HALF = full((ROWS // 2, D))
 CAMS = full((PIECES, 8, 128))
 
@@ -294,9 +310,10 @@
     return call(
         name,
         functools.partial(part_kernel, len(blocks)),
-        [full(b.shape) for b in blocks] + [CTX, STAT, STAT][: len(state)] + [XCOL, WCOL, WCOL],
-        [CTX, STAT, STAT],
+        [full(b.shape) for b in blocks] + [ALL, ALLSTAT, ALLSTAT][: len(state)] + [X, W, W],
+        [ALL, ALLSTAT, ALLSTAT],
         [shape(n, ROWS, dtype=jnp.float32) for n in (D, 8 * STEPS, 8 * STEPS)],
+        steps=1,
         work=4 * rows * D * D + 16 * rows * ROWS * D,
     )(*blocks, *state, *rest)
 
@@ -307,10 +324,11 @@
         name,
         functools.partial(last_kernel, len(blocks)),
         [full(b.shape) for b in blocks]
-        + [CTX] * len(extra)
-        + [XCOL, WCOL, WCOL, WROW, CTX, STAT, STAT, X],
+        + [ALL] * len(extra)
+        + [X, W, W, W, ALL, ALLSTAT, ALLSTAT, X],
         X,
         shape(ROWS, D, dtype=jnp.float32),
+        steps=1,
         work=4 * rows * D * D + 16 * rows * ROWS * D + 2 * ROWS * D * D,
         limit=limit,
     )(*blocks, *extra, *rest, *state, base)

time: 82.5 us -> 79.3 us (0.961)
  Pallas kernels: 33.6 us -> 31 us
  local copies, waits for them, and re-layouts: 7.64 us -> 5.9 us
  waiting for transfers between devices: 3.15 us -> 4.06 us
    pallas_call x3, Pallas kernels: 11.4 us -> 9.87 us  [call_part(): call(name, functools.partial(part_kernel, len(blocks)), [full(b.shape) fo...]
    all_to_all x1, waiting for transfers between devices: 2.62 us -> 4.03 us  [local(): lax.all_to_all(packed, ROUTE, split_axis=0, concat_axis=0, tiled=True)]
    gather x1, local copies, waits for them, and re-layouts: 2.51 us -> 1.48 us  [local(): first.reshape(PIECES * 4, 8, 128).at[place].get(mode='promise_in_bounds')]
    pallas_call x1, Pallas kernels: 4.73 us -> 3.77 us  [call_last(): call(name, functools.partial(last_kernel, len(blocks)), [full(b.shape) fo...]
    slice x1, local copies, waits for them, and re-layouts: 0.91 us -> 0.02 us  [local(): cam_own = first[:, 24:]]
  transfers between devices with their start and end apart: 12 -> 12, of which waited for: 2 -> 1; matrix products, arithmetic and copies ran while one was open for 5% -> 3% of each run, Pallas kernels for 32% -> 32%
where the time goes in v4:
time: 79.3 us; the launch traced here: 78.8 us
  starting transfers between devices  37.4 us (47%)
  Pallas kernels  31 us (39%)
  local copies, waits for them, and re-layouts  5.9 us (7%)
  waiting for transfers between devices  4.06 us (5%)
    all_to_all x1, starting transfers between devices, local(): lax.all_to_all(packed, ROUTE, split_axis=0, concat_axis=0, tiled=True)  12.2 us
    ppermute x6, starting transfers between devices, around(): return [lax.ppermute(value, 'tok', turn(shift)) for shift in (1, 3, 2)]  10.6 us
    pallas_call x3, Pallas kernels, call_part(): call(name, functools.partial(part_kernel, len(blocks)), [full(b.shape) fo...  9.87 us
    pallas_call x1, Pallas kernels, call_others(): pl.pallas_call(others_kernel, in_specs=[pl.BlockSpec(memory_space=pl.ANY)...  9.68 us
    all_to_all x1, starting transfers between devices, local(): lax.all_to_all(onward, ROUTE, split_axis=0, concat_axis=0, tiled=True)  7.71 us
    all_to_all x1, waiting for transfers between devices, local(): lax.all_to_all(packed, ROUTE, split_axis=0, concat_axis=0, tiled=True)  4.03 us
    unnamed x40, local copies, waits for them, and re-layouts  3.87 us
    pallas_call x1, Pallas kernels, call_last(): call(name, functools.partial(last_kernel, len(blocks)), [full(b.shape) fo...  3.77 us
  transfers between devices with their start and end apart: 12, of which 1 were waited for; matrix products, arithmetic and copies ran while one was open for 3% of the time, Pallas kernels for 32%

profile of v4, /device:TPU:2, one launch (start us, length us, event | category | flops | bytes accessed | tf_op | source)
XLA Modules:
  0.0 78.8 jit_solution(17547488863004151800)
XLA Ops:
  0.0 2.4 %memory_norm.1 = bf16[32,2,4,8,128]{4,3,2,1,0:T(8,128)(2,1)} custom-call(s32[8,16]{1,0:T(8,128)} %cams.1, bf16[256,768]{1,0:T(8,128)(2,1)} %refs_9_.1, f32[768]{0:T(1024)} %gain.5, f32[768]{0:T(1024)} %shift.5), custom_call_target="tpu_custom_call" | custom-call | tf_op jit(solution)/shard_map/memory_norm/pallas_call | solution.py:299
  2.4 12.2 %all-to-all-start = ((bf16[64,32,128]{2,1,0:T(8,128)(2,1)}), bf16[64,32,128]{2,1,0:T(8,128)(2,1)S(1)}, u32[]{:S(2)}, u32[]{:S(2)}) async-start(bf16[64,32,128]{2,1,0:T(8,128)(2,1)} %bitcast.11), calls=%async_computation | async-start | bytes 1048576 | tf_op jit(solution)/shard_map/all_to_all | solution.py:373
  14.6 0.3 self_norm.1.h_ref.refs_0_
  14.9 1.7 %collective-permute-start = (bf16[256,768]{1,0:T(8,128)(2,1)S(1)}, bf16[256,768]{1,0:T(8,128)(2,1)}, u32[]{:S(2)}, u32[]{:S(2)}) collective-permute-start(bf16[256,768]{1,0:T(8,128)(2,1)S(1)} %self_norm.1.h_ref.refs_0_), channel_id=1, source_target_pairs={{0,1},{1,2},{2,3},{3,0},{4,5},{5,6},{6,7},{7,4},{8,9},{9,10},{10,1... | collective-permute-start | bytes 1179656 | tf_op jit(solution)/shard_map/ppermute | solution.py:350
  16.5 1.7 %collective-permute-start.1 = (bf16[256,768]{1,0:T(8,128)(2,1)S(1)}, bf16[256,768]{1,0:T(8,128)(2,1)}, u32[]{:S(2)}, u32[]{:S(2)}) collective-permute-start(bf16[256,768]{1,0:T(8,128)(2,1)S(1)} %self_norm.1.h_ref.refs_0_), channel_id=1, source_target_pairs={{0,3},{1,0},{2,1},{3,2},{4,7},{5,4},{6,5},{7,6},{8,11},{9,8},{10,9... | collective-permute-start | bytes 1179656 | tf_op jit(solution)/shard_map/ppermute | solution.py:350
  18.2 2.0 %collective-permute-start.2 = (bf16[256,768]{1,0:T(8,128)(2,1)S(1)}, bf16[256,768]{1,0:T(8,128)(2,1)}, u32[]{:S(2)}, u32[]{:S(2)}) collective-permute-start(bf16[256,768]{1,0:T(8,128)(2,1)S(1)} %self_norm.1.h_ref.refs_0_), channel_id=1, source_target_pairs={{0,2},{1,3},{2,0},{3,1},{4,6},{5,7},{6,4},{7,5},{8,10},{9,11},{10,... | collective-permute-start | bytes 1179656 | tf_op jit(solution)/shard_map/ppermute | solution.py:350
  20.2 0.1 reshape.151
  20.3 0.1 copy.19
  20.4 0.1 reshape.152
  20.6 0.1 iota_add_fusion
  20.7 0.1 add.108
  20.8 1.3 %copy-done.6 = bf16[768,768]{1,0:T(8,128)(2,1)S(1)} copy-done((bf16[768,768]{1,0:T(8,128)(2,1)S(1)}, bf16[768,768]{1,0:T(8,128)(2,1)}, u32[]{:S(2)}) %copy-start.6) | copy-done | bytes 1179672
  22.1 1.7 %queries.1 = (bf16[256,768]{1,0:T(8,128)(2,1)S(1)}, bf16[256,768]{1,0:T(8,128)(2,1)S(1)}) custom-call(bf16[256,768]{1,0:T(8,128)(2,1)S(1)} %copy-done.4, bf16[256,768]{1,0:T(8,128)(2,1)S(1)} %self_norm.1.h_ref.refs_0_, f32[768]{0:T(1024)S(1)} %copy-done.11, f32[768]{0:T(1024)S(1)} %copy-done.12, bf16[768,768]{1,0:T(8,128)(2,1)S(1)} %copy-done.5, ...), custom_call_target="tpu_custom_call" | custom-call | flops 603979776 | bytes 2359296 | tf_op jit(solution)/shard_map/queries/pallas_call | solution.py:385
  23.9 2.4 %self_own.1 = (f32[768,256]{1,0:T(8,128)S(1)}, f32[24,256]{1,0:T(8,128)S(1)}, f32[24,256]{1,0:T(8,128)S(1)}) custom-call(bf16[256,768]{1,0:T(8,128)(2,1)S(1)} %self_norm.1.h_ref.refs_0_, bf16[256,768]{1,0:T(8,128)(2,1)S(1)} %get-tuple-element.25.refs_1_.refs_4_, bf16[768,768]{1,0:T(8,128)(2,1)S(1)} %copy-done.13, bf16[768,768]{1,0:T(8,128)(2,1)S(1)} %copy-done.14), custom_call_target="tpu_custom_call" | custom-call | flops 1409286144 | bytes 2359296 | tf_op jit(solution)/shard_map/self_own/pallas_call | solution.py:310
  26.3 0.0 copy-start.16
  26.3 4.0 %all-to-all-done = bf16[64,32,128]{2,1,0:T(8,128)(2,1)S(1)} async-done(((bf16[64,32,128]{2,1,0:T(8,128)(2,1)}), bf16[64,32,128]{2,1,0:T(8,128)(2,1)S(1)}, u32[]{:S(2)}, u32[]{:S(2)}) %all-to-all-start) | async-done | bytes 524320 | tf_op jit(solution)/shard_map/all_to_all | solution.py:373
  30.4 1.5 %gather_fusion = bf16[192,8,128]{2,1,0:T(8,128)(2,1)} fusion(bf16[256,8,128]{2,1,0:T(8,128)(2,1)S(1)} %bitcast.10, s32[1024]{0:T(1024)S(1)} %pad_clamp_fusion), kind=kCustom, calls=%fused_computation | custom fusion | bytes 787200 | tf_op jit(solution)/shard_map/gather | solution.py:377
  31.8 7.7 %all-to-all-start.1 = ((bf16[64,24,128]{2,1,0:T(8,128)(2,1)}), bf16[64,24,128]{2,1,0:T(8,128)(2,1)}, u32[]{:S(2)}, u32[]{:S(2)}) async-start(bf16[64,24,128]{2,1,0:T(8,128)(2,1)} %bitcast.4), calls=%async_computation.1 | async-start | bytes 786432 | tf_op jit(solution)/shard_map/all_to_all | solution.py:400
  39.6 1.7 %collective-permute-start.3 = (bf16[64,8,128]{2,1,0:T(8,128)(2,1)S(1)}, bf16[64,8,128]{2,1,0:T(8,128)(2,1)S(1)}, u32[]{:S(2)}, u32[]{:S(2)}) collective-permute-start(bf16[64,8,128]{2,1,0:T(8,128)(2,1)S(1)} %slice.14.p0), channel_id=1, source_target_pairs={{0,1},{1,2},{2,3},{3,0},{4,5},{5,6},{6,7},{7,4},{8,9},{9,10},{10,1... | collective-permute-start | bytes 393224 | tf_op jit(solution)/shard_map/ppermute | solution.py:350
  41.2 1.7 %collective-permute-start.4 = (bf16[64,8,128]{2,1,0:T(8,128)(2,1)S(1)}, bf16[64,8,128]{2,1,0:T(8,128)(2,1)S(1)}, u32[]{:S(2)}, u32[]{:S(2)}) collective-permute-start(bf16[64,8,128]{2,1,0:T(8,128)(2,1)S(1)} %slice.14.p0), channel_id=1, source_target_pairs={{0,3},{1,0},{2,1},{3,2},{4,7},{5,4},{6,5},{7,6},{8,11},{9,8},{10,9... | collective-permute-start | bytes 393224 | tf_op jit(solution)/shard_map/ppermute | solution.py:350
  42.9 2.0 %collective-permute-start.5 = (bf16[64,8,128]{2,1,0:T(8,128)(2,1)S(1)}, bf16[64,8,128]{2,1,0:T(8,128)(2,1)S(1)}, u32[]{:S(2)}, u32[]{:S(2)}) collective-permute-start(bf16[64,8,128]{2,1,0:T(8,128)(2,1)S(1)} %slice.14.p0), channel_id=1, source_target_pairs={{0,2},{1,3},{2,0},{3,1},{4,6},{5,7},{6,4},{7,5},{8,10},{9,11},{10,... | collective-permute-start | bytes 393224 | tf_op jit(solution)/shard_map/ppermute | solution.py:350
  44.9 9.7 %self_others.1.refs_10_ = f32[256,768]{1,0:T(8,128)} custom-call(bf16[256,768]{1,0:T(8,128)(2,1)} %collective-permute-done.refs_0_, bf16[256,768]{1,0:T(8,128)(2,1)} %collective-permute-done.1.refs_1_, bf16[256,768]{1,0:T(8,128)(2,1)} %collective-permute-done.2.refs_2_, bf16[768,768]{1,0:T(8,128)(2,1)} %refs_3_.4, bf16[256,768]{1,0:T(8,128)(2,1)} %copy-done.15, ...), custom_call_target="tpu_custom_call" | custom-call | flops 4227858432 | bytes 4718592 | tf_op jit(solution)/shard_map/self_others/pallas_call | solution.py:239
  54.7 0.8 collective-permute-start.6
  55.4 2.6 %collective-permute-start.8 = (bf16[256,768]{1,0:T(8,128)(2,1)}, bf16[256,768]{1,0:T(8,128)(2,1)S(1)}, u32[]{:S(2)}, u32[]{:S(2)}) collective-permute-start(bf16[256,768]{1,0:T(8,128)(2,1)} %bitcast.7.refs_0_), channel_id=1, source_target_pairs={{0,3},{1,0},{2,1},{3,2},{4,7},{5,4},{6,5},{7,6},{8,11},{9,8},{10,9... | collective-permute-start | bytes 1179656 | tf_op jit(solution)/shard_map/ppermute | solution.py:405
  58.0 1.3 %copy-done = bf16[768,768]{1,0:T(8,128)(2,1)S(1)} copy-done((bf16[768,768]{1,0:T(8,128)(2,1)S(1)}, bf16[768,768]{1,0:T(8,128)(2,1)}, u32[]{:S(2)}) %copy-start) | copy-done | bytes 1179672
  59.2 1.3 %copy-done.2 = bf16[768,768]{1,0:T(8,128)(2,1)S(1)} copy-done((bf16[768,768]{1,0:T(8,128)(2,1)S(1)}, bf16[768,768]{1,0:T(8,128)(2,1)}, u32[]{:S(2)}) %copy-start.2) | copy-done | bytes 1179672
  60.5 3.3 %camera_attention.1.refs_2_ = f32[768,256]{1,0:T(8,128)S(1)} custom-call(bf16[64,8,128]{2,1,0:T(8,128)(2,1)S(1)} %slice.14.p0, bf16[64,8,128]{2,1,0:T(8,128)(2,1)S(1)} %collective-permute-done.3.p1, bf16[64,8,128]{2,1,0:T(8,128)(2,1)S(1)} %collective-permute-done.4.p2, bf16[64,8,128]{2,1,0:T(8,128)(2,1)S(1)} %collective-permute-done.5.p3, ...), custom_call_target="tpu_custom_call" | custom-call | flops 704643072 | bytes 2359296 | tf_op jit(solution)/shard_map/camera_attention/pallas_call | solution.py:408
  63.9 3.4 %cross_own.1 = (f32[768,256]{1,0:T(8,128)S(1)}, f32[24,256]{1,0:T(8,128)S(1)}, f32[24,256]{1,0:T(8,128)S(1)}) custom-call(bf16[256,768]{1,0:T(8,128)(2,1)} %bitcast.7.refs_0_, bf16[256,768]{1,0:T(8,128)(2,1)S(1)} %get-tuple-element.37.q_ref.refs_1_.refs_5_.refs_3_, bf16[768,768]{1,0:T(8,128)(2,1)S(1)} %copy-done.1, bf16[768,768]{1,0:T(8,128)(2,1)S(1)} %copy-done.3), custom_call_target="tpu_custom_call" | custom-call | flops 1409286144 | bytes 2359296 | tf_op jit(solution)/shard_map/cross_own/pallas_call | solution.py:310
  67.3 0.1 collective-permute-start.7
  67.4 3.5 %collective-permute-start.9 = (bf16[128,768]{1,0:T(8,128)(2,1)S(1)}, bf16[128,768]{1,0:T(8,128)(2,1)S(1)}, u32[]{:S(2)}, u32[]{:S(2)}) collective-permute-start(bf16[128,768]{1,0:T(8,128)(2,1)S(1)} %slice.16), channel_id=1, source_target_pairs={{0,3},{1,0},{2,1},{3,2},{4,7},{5,4},{6,5},{7,6},{8,11},{9,8},{10,9... | collective-permute-start | bytes 589832 | tf_op jit(solution)/shard_map/ppermute | solution.py:407
  70.9 4.1 %cross_near.1 = (f32[768,256]{1,0:T(8,128)S(1)}, f32[24,256]{1,0:T(8,128)S(1)}, f32[24,256]{1,0:T(8,128)S(1)}) custom-call(bf16[256,768]{1,0:T(8,128)(2,1)S(1)} %collective-permute-done.6.refs_0_, bf16[256,768]{1,0:T(8,128)(2,1)S(1)} %collective-permute-done.8.refs_1_, f32[768,256]{1,0:T(8,128)S(1)} %get-tuple-element.38.refs_2_, ...), custom_call_target="tpu_custom_call" | custom-call | flops 2818572288 | bytes 2359296 | tf_op jit(solution)/shard_map/cross_near/pallas_call | solution.py:310
  75.1 3.8 %cross_far.1 = f32[256,768]{1,0:T(8,128)} custom-call(bf16[128,768]{1,0:T(8,128)(2,1)S(1)} %collective-permute-done.7.refs_0_, bf16[128,768]{1,0:T(8,128)(2,1)S(1)} %collective-permute-done.9.refs_1_, f32[768,256]{1,0:T(8,128)S(1)} %camera_attention.1.refs_2_, bf16[256,768]{1,0:T(8,128)(2,1)S(1)} %get-tuple-element.37.q_ref.refs_1_.refs_5_.refs_3_, ...), custom_call_target="tpu_custom_call" | custom-call | flops 1711276032 | bytes 2359296 | tf_op jit(solution)/shard_map/cross_far/pallas_call | solution.py:323
  (53 shorter events, 0.2 us)
Async XLA Ops:
  0.0 14.5 %copy-start.4 = (bf16[256,768]{1,0:T(8,128)(2,1)S(1)}, bf16[256,768]{1,0:T(8,128)(2,1)}, u32[]{:S(2)}) copy-start(bf16[256,768]{1,0:T(8,128)(2,1)} %refs_9_.1) | copy-start | bytes 1179652
  0.0 14.6 %copy-start.9 = (f32[768]{0:T(1024)S(1)}, f32[768]{0:T(1024)}, u32[]{:S(2)}) copy-start(f32[768]{0:T(1024)} %gain.3) | copy-start | bytes 9220
  0.0 14.6 %copy-start.10 = (f32[768]{0:T(1024)S(1)}, f32[768]{0:T(1024)}, u32[]{:S(2)}) copy-start(f32[768]{0:T(1024)} %shift.3) | copy-start | bytes 9220
  0.0 20.2 %copy-start.19 = (s32[64]{0:T(128)S(1)}, s32[64]{0:T(128)}, u32[]{:S(2)}) copy-start(s32[64]{0:T(128)} %param.32) | copy-start | bytes 772
  2.4 18.4 %copy-start.5 = (bf16[768,768]{1,0:T(8,128)(2,1)S(1)}, bf16[768,768]{1,0:T(8,128)(2,1)}, u32[]{:S(2)}) copy-start(bf16[768,768]{1,0:T(8,128)(2,1)} %wc.1) | copy-start | bytes 3538948
  2.4 18.4 %copy-start.11 = (f32[768]{0:T(1024)S(1)}, f32[768]{0:T(1024)}, u32[]{:S(2)}) copy-start(f32[768]{0:T(1024)} %gain.4) | copy-start | bytes 9220
  2.4 18.4 %copy-start.12 = (f32[768]{0:T(1024)S(1)}, f32[768]{0:T(1024)}, u32[]{:S(2)}) copy-start(f32[768]{0:T(1024)} %shift.4) | copy-start | bytes 9220
  2.4 28.0 %all-to-all-start = ((bf16[64,32,128]{2,1,0:T(8,128)(2,1)}), bf16[64,32,128]{2,1,0:T(8,128)(2,1)S(1)}, u32[]{:S(2)}, u32[]{:S(2)}) async-start(bf16[64,32,128]{2,1,0:T(8,128)(2,1)} %bitcast.11), calls=%async_computation | async-start | bytes 1048576 | tf_op jit(solution)/shard_map/all_to_all | solution.py:373
  14.9 28.0 %collective-permute-start = (bf16[256,768]{1,0:T(8,128)(2,1)S(1)}, bf16[256,768]{1,0:T(8,128)(2,1)}, u32[]{:S(2)}, u32[]{:S(2)}) collective-permute-start(bf16[256,768]{1,0:T(8,128)(2,1)S(1)} %self_norm.1.h_ref.refs_0_), channel_id=1, source_target_pairs={{0,1},{1,2},{2,3},{3,0},{4,5},{5,6},{6,7},{7,4},{8,9},{9,10},{10,1... | collective-permute-start | bytes 1179656 | tf_op jit(solution)/shard_map/ppermute | solution.py:350
  16.5 28.3 %collective-permute-start.1 = (bf16[256,768]{1,0:T(8,128)(2,1)S(1)}, bf16[256,768]{1,0:T(8,128)(2,1)}, u32[]{:S(2)}, u32[]{:S(2)}) collective-permute-start(bf16[256,768]{1,0:T(8,128)(2,1)S(1)} %self_norm.1.h_ref.refs_0_), channel_id=1, source_target_pairs={{0,3},{1,0},{2,1},{3,2},{4,7},{5,4},{6,5},{7,6},{8,11},{9,8},{10,9... | collective-permute-start | bytes 1179656 | tf_op jit(solution)/shard_map/ppermute | solution.py:350
  18.2 26.7 %collective-permute-start.2 = (bf16[256,768]{1,0:T(8,128)(2,1)S(1)}, bf16[256,768]{1,0:T(8,128)(2,1)}, u32[]{:S(2)}, u32[]{:S(2)}) collective-permute-start(bf16[256,768]{1,0:T(8,128)(2,1)S(1)} %self_norm.1.h_ref.refs_0_), channel_id=1, source_target_pairs={{0,2},{1,3},{2,0},{3,1},{4,6},{5,7},{6,4},{7,5},{8,10},{9,11},{10,... | collective-permute-start | bytes 1179656 | tf_op jit(solution)/shard_map/ppermute | solution.py:350
  20.8 1.3 %copy-start.6 = (bf16[768,768]{1,0:T(8,128)(2,1)S(1)}, bf16[768,768]{1,0:T(8,128)(2,1)}, u32[]{:S(2)}) copy-start(bf16[768,768]{1,0:T(8,128)(2,1)} %ws.1) | copy-start | bytes 3538948
  22.1 1.7 %copy-start.13 = (bf16[768,768]{1,0:T(8,128)(2,1)S(1)}, bf16[768,768]{1,0:T(8,128)(2,1)}, u32[]{:S(2)}) copy-start(bf16[768,768]{1,0:T(8,128)(2,1)} %refs_3_.4) | copy-start | bytes 3538948
  22.1 1.8 %copy-start.14 = (bf16[768,768]{1,0:T(8,128)(2,1)S(1)}, bf16[768,768]{1,0:T(8,128)(2,1)}, u32[]{:S(2)}) copy-start(bf16[768,768]{1,0:T(8,128)(2,1)} %refs_5_.2) | copy-start | bytes 3538948
  23.8 2.4 %copy-start.15 = (bf16[256,768]{1,0:T(8,128)(2,1)}, bf16[256,768]{1,0:T(8,128)(2,1)S(1)}, u32[]{:S(2)}) copy-start(bf16[256,768]{1,0:T(8,128)(2,1)S(1)} %get-tuple-element.25.refs_1_.refs_4_) | copy-start | bytes 1179652
  26.3 18.6 %copy-start.16 = (f32[768,256]{1,0:T(8,128)}, f32[768,256]{1,0:T(8,128)S(1)}, u32[]{:S(2)}) copy-start(f32[768,256]{1,0:T(8,128)S(1)} %get-tuple-element.30.refs_6_) | copy-start | bytes 2359300
  26.3 18.6 %copy-start.17 = (f32[24,256]{1,0:T(8,128)}, f32[24,256]{1,0:T(8,128)S(1)}, u32[]{:S(2)}) copy-start(f32[24,256]{1,0:T(8,128)S(1)} %get-tuple-element.31.refs_7_) | copy-start | bytes 73732
  26.3 18.6 %copy-start.18 = (f32[24,256]{1,0:T(8,128)}, f32[24,256]{1,0:T(8,128)S(1)}, u32[]{:S(2)}) copy-start(f32[24,256]{1,0:T(8,128)S(1)} %get-tuple-element.32.refs_8_) | copy-start | bytes 73732
  31.8 22.8 %all-to-all-start.1 = ((bf16[64,24,128]{2,1,0:T(8,128)(2,1)}), bf16[64,24,128]{2,1,0:T(8,128)(2,1)}, u32[]{:S(2)}, u32[]{:S(2)}) async-start(bf16[64,24,128]{2,1,0:T(8,128)(2,1)} %bitcast.4), calls=%async_computation.1 | async-start | bytes 786432 | tf_op jit(solution)/shard_map/all_to_all | solution.py:400
  39.6 15.0 %collective-permute-start.3 = (bf16[64,8,128]{2,1,0:T(8,128)(2,1)S(1)}, bf16[64,8,128]{2,1,0:T(8,128)(2,1)S(1)}, u32[]{:S(2)}, u32[]{:S(2)}) collective-permute-start(bf16[64,8,128]{2,1,0:T(8,128)(2,1)S(1)} %slice.14.p0), channel_id=1, source_target_pairs={{0,1},{1,2},{2,3},{3,0},{4,5},{5,6},{6,7},{7,4},{8,9},{9,10},{10,1... | collective-permute-start | bytes 393224 | tf_op jit(solution)/shard_map/ppermute | solution.py:350
  41.2 13.4 %collective-permute-start.4 = (bf16[64,8,128]{2,1,0:T(8,128)(2,1)S(1)}, bf16[64,8,128]{2,1,0:T(8,128)(2,1)S(1)}, u32[]{:S(2)}, u32[]{:S(2)}) collective-permute-start(bf16[64,8,128]{2,1,0:T(8,128)(2,1)S(1)} %slice.14.p0), channel_id=1, source_target_pairs={{0,3},{1,0},{2,1},{3,2},{4,7},{5,4},{6,5},{7,6},{8,11},{9,8},{10,9... | collective-permute-start | bytes 393224 | tf_op jit(solution)/shard_map/ppermute | solution.py:350
  42.9 11.7 %collective-permute-start.5 = (bf16[64,8,128]{2,1,0:T(8,128)(2,1)S(1)}, bf16[64,8,128]{2,1,0:T(8,128)(2,1)S(1)}, u32[]{:S(2)}, u32[]{:S(2)}) collective-permute-start(bf16[64,8,128]{2,1,0:T(8,128)(2,1)S(1)} %slice.14.p0), channel_id=1, source_target_pairs={{0,2},{1,3},{2,0},{3,1},{4,6},{5,7},{6,4},{7,5},{8,10},{9,11},{10,... | collective-permute-start | bytes 393224 | tf_op jit(solution)/shard_map/ppermute | solution.py:350
  54.7 12.6 %collective-permute-start.6 = (bf16[256,768]{1,0:T(8,128)(2,1)}, bf16[256,768]{1,0:T(8,128)(2,1)S(1)}, u32[]{:S(2)}, u32[]{:S(2)}) collective-permute-start(bf16[256,768]{1,0:T(8,128)(2,1)} %bitcast.7.refs_0_), channel_id=1, source_target_pairs={{0,1},{1,2},{2,3},{3,0},{4,5},{5,6},{6,7},{7,4},{8,9},{9,10},{10,1... | collective-permute-start | bytes 1179656 | tf_op jit(solution)/shard_map/ppermute | solution.py:404
  55.4 12.0 %collective-permute-start.8 = (bf16[256,768]{1,0:T(8,128)(2,1)}, bf16[256,768]{1,0:T(8,128)(2,1)S(1)}, u32[]{:S(2)}, u32[]{:S(2)}) collective-permute-start(bf16[256,768]{1,0:T(8,128)(2,1)} %bitcast.7.refs_0_), channel_id=1, source_target_pairs={{0,3},{1,0},{2,1},{3,2},{4,7},{5,4},{6,5},{7,6},{8,11},{9,8},{10,9... | collective-permute-start | bytes 1179656 | tf_op jit(solution)/shard_map/ppermute | solution.py:405
  58.0 1.3 %copy-start = (bf16[768,768]{1,0:T(8,128)(2,1)S(1)}, bf16[768,768]{1,0:T(8,128)(2,1)}, u32[]{:S(2)}) copy-start(bf16[768,768]{1,0:T(8,128)(2,1)} %refs_4_.1) | copy-start | bytes 3538948
  59.2 1.3 %copy-start.2 = (bf16[768,768]{1,0:T(8,128)(2,1)S(1)}, bf16[768,768]{1,0:T(8,128)(2,1)}, u32[]{:S(2)}) copy-start(bf16[768,768]{1,0:T(8,128)(2,1)} %refs_5_.3) | copy-start | bytes 3538948
  60.5 3.3 %copy-start.1 = (bf16[768,768]{1,0:T(8,128)(2,1)S(1)}, bf16[768,768]{1,0:T(8,128)(2,1)}, u32[]{:S(2)}) copy-start(bf16[768,768]{1,0:T(8,128)(2,1)} %refs_4_.1) | copy-start | bytes 3538948
  60.5 3.3 %copy-start.3 = (bf16[768,768]{1,0:T(8,128)(2,1)S(1)}, bf16[768,768]{1,0:T(8,128)(2,1)}, u32[]{:S(2)}) copy-start(bf16[768,768]{1,0:T(8,128)(2,1)} %refs_5_.3) | copy-start | bytes 3538948
  67.3 7.7 %collective-permute-start.7 = (bf16[128,768]{1,0:T(8,128)(2,1)S(1)}, bf16[128,768]{1,0:T(8,128)(2,1)S(1)}, u32[]{:S(2)}, u32[]{:S(2)}) collective-permute-start(bf16[128,768]{1,0:T(8,128)(2,1)S(1)} %slice.15), channel_id=1, source_target_pairs={{0,1},{1,2},{2,3},{3,0},{4,5},{5,6},{6,7},{7,4},{8,9},{9,10},{10,1... | collective-permute-start | bytes 589832 | tf_op jit(solution)/shard_map/ppermute | solution.py:406
  67.4 7.6 %collective-permute-start.9 = (bf16[128,768]{1,0:T(8,128)(2,1)S(1)}, bf16[128,768]{1,0:T(8,128)(2,1)S(1)}, u32[]{:S(2)}, u32[]{:S(2)}) collective-permute-start(bf16[128,768]{1,0:T(8,128)(2,1)S(1)} %slice.16), channel_id=1, source_target_pairs={{0,3},{1,0},{2,1},{3,2},{4,7},{5,4},{6,5},{7,6},{8,11},{9,8},{10,9... | collective-permute-start | bytes 589832 | tf_op jit(solution)/shard_map/ppermute | solution.py:407
  70.9 4.1 %copy-start.7 = (bf16[768,768]{1,0:T(8,128)(2,1)S(1)}, bf16[768,768]{1,0:T(8,128)(2,1)}, u32[]{:S(2)}) copy-start(bf16[768,768]{1,0:T(8,128)(2,1)} %refs_6_.3) | copy-start | bytes 3538948
  70.9 4.1 %copy-start.8 = (f32[256,768]{1,0:T(8,128)S(1)}, f32[256,768]{1,0:T(8,128)}, u32[]{:S(2)}) copy-start(f32[256,768]{1,0:T(8,128)} %self_others.1.refs_10_) | copy-start | bytes 2359300

commit v5 on v4

--- a/solution.py
+++ b/solution.py
@@ -104,25 +104,20 @@
     s_ref[...] = mm(h_ref[...], ws[...]).astype(BF) * BF(0.125)
 
 
-def camera_kernel(p0, p1, p2, p3, q_ref, wk, wv, c_ref, m_ref):
-    @pl.when(pl.program_id(0) == 0)
-    def _():
-        tok = lax.axis_index("tok")
-        parts = [ref[...].astype(jnp.float32) for ref in (p0, p1, p2, p3)]
-        for half in (0, 1):
-            total = jnp.zeros((PIECES, 8, 128), jnp.float32)
-            for shift, part in zip((0, 1, 3, 2), parts):
-                total += jnp.where((tok + 4 - shift) % 4 // 2 == half, part, 0.0)
-            for c in range(D // 128):
-                m_ref[PIECES * half : PIECES * (half + 1), 128 * c : 128 * (c + 1)] = total[
-                    :, c, :
-                ].astype(BF)
-
-    m = m_ref[...]
-    k = mm(m, wk[...]).astype(BF)
-    v = mm(m, wv[...]).astype(BF)
-    for at, _, _, total, c in heads_t(q_ref[...], k, jnp.transpose(v)):
-        c_ref[at] = c * (1.0 / total)
+def camera_kernel(p0, p1, p2, p3, q_ref, wk, wv, c_ref):
+    tok = lax.axis_index("tok")
+    parts = [ref[...].astype(jnp.float32) for ref in (p0, p1, p2, p3)]
+    first = [(tok + 4 - shift) % 4 // 2 == 0 for shift in (0, 1, 3, 2)]
+    halves = []
+    for want in (True, False):
+        total = jnp.zeros((PIECES, 8, 128), jnp.float32)
+        for flag, part in zip(first, parts):
+            total += jnp.where(flag == want, part, 0.0)
+        halves.append(jnp.concatenate([total[:, c, :] for c in range(D // 128)], axis=1))
+    m = jnp.concatenate(halves, axis=0).astype(BF)
+    for step in range(STEPS):
+        for at, _, _, total, c in column_parts(step, q_ref, wk, wv, m, ()):
+            c_ref[step * COLS + at.start : step * COLS + at.stop] = c * (1.0 / total)
 
 
 def keys_values(blocks, wk, wv):
@@ -408,10 +403,10 @@
     cam_ctx = call(
         "camera_attention",
         camera_kernel,
-        [CAMS] * 4 + [XCOL, WCOL, WCOL],
-        CTX,
+        [CAMS] * 4 + [X, W, W],
+        ALL,
         shape(D, ROWS, dtype=jnp.float32),
-        [pltpu.VMEM((2 * PIECES, D), BF)],
+        steps=1,
         work=4 * 128 * D * D + 16 * ROWS * 128 * D,
     )(*cam_parts, cq, cross_key, cross_value)
     state = call_part("cross_own", [mine], [], cq, cross_key, cross_value)

time: 79.3 us -> 79.2 us (level)
  Pallas kernels: 31 us -> 30.2 us
    pallas_call x1, Pallas kernels: 3.31 us -> 2.44 us  [local(): call('camera_attention', camera_kernel, [CAMS] * 4 + [X, W, W], ALL, shap...]
  transfers between devices with their start and end apart: 12 -> 12, of which waited for: 1 -> 2; matrix products, arithmetic and copies ran while one was open for 3% -> 3% of each run, Pallas kernels for 32% -> 31%
where the time goes in v5:
time: 79.2 us; the launch traced here: 78.1 us
  starting transfers between devices  37.4 us (47%)
  Pallas kernels  30.2 us (38%)
  local copies, waits for them, and re-layouts  5.89 us (7%)
  waiting for transfers between devices  4.23 us (5%)
    all_to_all x1, starting transfers between devices, local(): lax.all_to_all(packed, ROUTE, split_axis=0, concat_axis=0, tiled=True)  12.2 us
    ppermute x6, starting transfers between devices, around(): return [lax.ppermute(value, 'tok', turn(shift)) for shift in (1, 3, 2)]  10.6 us
    pallas_call x3, Pallas kernels, call_part(): call(name, functools.partial(part_kernel, len(blocks)), [full(b.shape) fo...  9.87 us
    pallas_call x1, Pallas kernels, call_others(): pl.pallas_call(others_kernel, in_specs=[pl.BlockSpec(memory_space=pl.ANY)...  9.69 us
    all_to_all x1, starting transfers between devices, local(): lax.all_to_all(onward, ROUTE, split_axis=0, concat_axis=0, tiled=True)  7.71 us
    all_to_all x1, waiting for transfers between devices, local(): lax.all_to_all(packed, ROUTE, split_axis=0, concat_axis=0, tiled=True)  4.03 us
    unnamed x40, local copies, waits for them, and re-layouts  3.87 us
    pallas_call x1, Pallas kernels, call_last(): call(name, functools.partial(last_kernel, len(blocks)), [full(b.shape) fo...  3.77 us
  transfers between devices with their start and end apart: 12, of which 2 were waited for; matrix products, arithmetic and copies ran while one was open for 3% of the time, Pallas kernels for 31%

profile of v5, /device:TPU:2, one launch (start us, length us, event | category | flops | bytes accessed | tf_op | source)
XLA Modules:
  0.0 78.1 jit_solution(9334769428594216024)
XLA Ops:
  0.0 2.4 %memory_norm.1 = bf16[32,2,4,8,128]{4,3,2,1,0:T(8,128)(2,1)} custom-call(s32[8,16]{1,0:T(8,128)} %cams.1, bf16[256,768]{1,0:T(8,128)(2,1)} %refs_9_.1, f32[768]{0:T(1024)} %gain.5, f32[768]{0:T(1024)} %shift.5), custom_call_target="tpu_custom_call" | custom-call | tf_op jit(solution)/shard_map/memory_norm/pallas_call | solution.py:294
  2.4 12.2 %all-to-all-start = ((bf16[64,32,128]{2,1,0:T(8,128)(2,1)}), bf16[64,32,128]{2,1,0:T(8,128)(2,1)S(1)}, u32[]{:S(2)}, u32[]{:S(2)}) async-start(bf16[64,32,128]{2,1,0:T(8,128)(2,1)} %bitcast.11), calls=%async_computation | async-start | bytes 1048576 | tf_op jit(solution)/shard_map/all_to_all | solution.py:368
  14.6 0.3 self_norm.1.h_ref.refs_0_
  14.9 1.7 %collective-permute-start = (bf16[256,768]{1,0:T(8,128)(2,1)S(1)}, bf16[256,768]{1,0:T(8,128)(2,1)}, u32[]{:S(2)}, u32[]{:S(2)}) collective-permute-start(bf16[256,768]{1,0:T(8,128)(2,1)S(1)} %self_norm.1.h_ref.refs_0_), channel_id=1, source_target_pairs={{0,1},{1,2},{2,3},{3,0},{4,5},{5,6},{6,7},{7,4},{8,9},{9,10},{10,1... | collective-permute-start | bytes 1179656 | tf_op jit(solution)/shard_map/ppermute | solution.py:345
  16.5 1.7 %collective-permute-start.1 = (bf16[256,768]{1,0:T(8,128)(2,1)S(1)}, bf16[256,768]{1,0:T(8,128)(2,1)}, u32[]{:S(2)}, u32[]{:S(2)}) collective-permute-start(bf16[256,768]{1,0:T(8,128)(2,1)S(1)} %self_norm.1.h_ref.refs_0_), channel_id=1, source_target_pairs={{0,3},{1,0},{2,1},{3,2},{4,7},{5,4},{6,5},{7,6},{8,11},{9,8},{10,9... | collective-permute-start | bytes 1179656 | tf_op jit(solution)/shard_map/ppermute | solution.py:345
  18.2 2.0 %collective-permute-start.2 = (bf16[256,768]{1,0:T(8,128)(2,1)S(1)}, bf16[256,768]{1,0:T(8,128)(2,1)}, u32[]{:S(2)}, u32[]{:S(2)}) collective-permute-start(bf16[256,768]{1,0:T(8,128)(2,1)S(1)} %self_norm.1.h_ref.refs_0_), channel_id=1, source_target_pairs={{0,2},{1,3},{2,0},{3,1},{4,6},{5,7},{6,4},{7,5},{8,10},{9,11},{10,... | collective-permute-start | bytes 1179656 | tf_op jit(solution)/shard_map/ppermute | solution.py:345
  20.2 0.1 reshape.151
  20.3 0.1 copy.19
  20.4 0.1 reshape.152
  20.6 0.1 iota_add_fusion
  20.7 0.1 add.108
  20.8 1.3 %copy-done.6 = bf16[768,768]{1,0:T(8,128)(2,1)S(1)} copy-done((bf16[768,768]{1,0:T(8,128)(2,1)S(1)}, bf16[768,768]{1,0:T(8,128)(2,1)}, u32[]{:S(2)}) %copy-start.6) | copy-done | bytes 1179672
  22.1 1.7 %queries.1 = (bf16[256,768]{1,0:T(8,128)(2,1)S(1)}, bf16[256,768]{1,0:T(8,128)(2,1)S(1)}) custom-call(bf16[256,768]{1,0:T(8,128)(2,1)S(1)} %copy-done.4, bf16[256,768]{1,0:T(8,128)(2,1)S(1)} %self_norm.1.h_ref.refs_0_, f32[768]{0:T(1024)S(1)} %copy-done.11, f32[768]{0:T(1024)S(1)} %copy-done.12, bf16[768,768]{1,0:T(8,128)(2,1)S(1)} %copy-done.5, ...), custom_call_target="tpu_custom_call" | custom-call | flops 603979776 | bytes 2359296 | tf_op jit(solution)/shard_map/queries/pallas_call | solution.py:380
  23.9 2.4 %self_own.1 = (f32[768,256]{1,0:T(8,128)S(1)}, f32[24,256]{1,0:T(8,128)S(1)}, f32[24,256]{1,0:T(8,128)S(1)}) custom-call(bf16[256,768]{1,0:T(8,128)(2,1)S(1)} %self_norm.1.h_ref.refs_0_, bf16[256,768]{1,0:T(8,128)(2,1)S(1)} %get-tuple-element.25.refs_1_.refs_4_, bf16[768,768]{1,0:T(8,128)(2,1)S(1)} %copy-done.13, bf16[768,768]{1,0:T(8,128)(2,1)S(1)} %copy-done.14), custom_call_target="tpu_custom_call" | custom-call | flops 1409286144 | bytes 2359296 | tf_op jit(solution)/shard_map/self_own/pallas_call | solution.py:305
  26.3 4.0 %all-to-all-done = bf16[64,32,128]{2,1,0:T(8,128)(2,1)S(1)} async-done(((bf16[64,32,128]{2,1,0:T(8,128)(2,1)}), bf16[64,32,128]{2,1,0:T(8,128)(2,1)S(1)}, u32[]{:S(2)}, u32[]{:S(2)}) %all-to-all-start) | async-done | bytes 524320 | tf_op jit(solution)/shard_map/all_to_all | solution.py:368
  30.4 1.5 %gather_fusion = bf16[192,8,128]{2,1,0:T(8,128)(2,1)} fusion(bf16[256,8,128]{2,1,0:T(8,128)(2,1)S(1)} %bitcast.10, s32[1024]{0:T(1024)S(1)} %pad_clamp_fusion), kind=kCustom, calls=%fused_computation | custom fusion | bytes 787200 | tf_op jit(solution)/shard_map/gather | solution.py:372
  31.8 7.7 %all-to-all-start.1 = ((bf16[64,24,128]{2,1,0:T(8,128)(2,1)}), bf16[64,24,128]{2,1,0:T(8,128)(2,1)}, u32[]{:S(2)}, u32[]{:S(2)}) async-start(bf16[64,24,128]{2,1,0:T(8,128)(2,1)} %bitcast.4), calls=%async_computation.1 | async-start | bytes 786432 | tf_op jit(solution)/shard_map/all_to_all | solution.py:395
  39.6 1.7 %collective-permute-start.3 = (bf16[64,8,128]{2,1,0:T(8,128)(2,1)S(1)}, bf16[64,8,128]{2,1,0:T(8,128)(2,1)S(1)}, u32[]{:S(2)}, u32[]{:S(2)}) collective-permute-start(bf16[64,8,128]{2,1,0:T(8,128)(2,1)S(1)} %slice.14.p0), channel_id=1, source_target_pairs={{0,1},{1,2},{2,3},{3,0},{4,5},{5,6},{6,7},{7,4},{8,9},{9,10},{10,1... | collective-permute-start | bytes 393224 | tf_op jit(solution)/shard_map/ppermute | solution.py:345
  41.2 1.7 %collective-permute-start.4 = (bf16[64,8,128]{2,1,0:T(8,128)(2,1)S(1)}, bf16[64,8,128]{2,1,0:T(8,128)(2,1)S(1)}, u32[]{:S(2)}, u32[]{:S(2)}) collective-permute-start(bf16[64,8,128]{2,1,0:T(8,128)(2,1)S(1)} %slice.14.p0), channel_id=1, source_target_pairs={{0,3},{1,0},{2,1},{3,2},{4,7},{5,4},{6,5},{7,6},{8,11},{9,8},{10,9... | collective-permute-start | bytes 393224 | tf_op jit(solution)/shard_map/ppermute | solution.py:345
  42.9 2.0 %collective-permute-start.5 = (bf16[64,8,128]{2,1,0:T(8,128)(2,1)S(1)}, bf16[64,8,128]{2,1,0:T(8,128)(2,1)S(1)}, u32[]{:S(2)}, u32[]{:S(2)}) collective-permute-start(bf16[64,8,128]{2,1,0:T(8,128)(2,1)S(1)} %slice.14.p0), channel_id=1, source_target_pairs={{0,2},{1,3},{2,0},{3,1},{4,6},{5,7},{6,4},{7,5},{8,10},{9,11},{10,... | collective-permute-start | bytes 393224 | tf_op jit(solution)/shard_map/ppermute | solution.py:345
  44.9 9.7 %self_others.1.refs_10_ = f32[256,768]{1,0:T(8,128)} custom-call(bf16[256,768]{1,0:T(8,128)(2,1)} %collective-permute-done.refs_0_, bf16[256,768]{1,0:T(8,128)(2,1)} %collective-permute-done.1.refs_1_, bf16[256,768]{1,0:T(8,128)(2,1)} %collective-permute-done.2.refs_2_, bf16[768,768]{1,0:T(8,128)(2,1)} %refs_3_.4, bf16[256,768]{1,0:T(8,128)(2,1)} %copy-done.15, ...), custom_call_target="tpu_custom_call" | custom-call | flops 4227858432 | bytes 4718592 | tf_op jit(solution)/shard_map/self_others/pallas_call | solution.py:234
  54.7 0.7 collective-permute-start.6
  55.4 2.6 %collective-permute-start.8 = (bf16[256,768]{1,0:T(8,128)(2,1)}, bf16[256,768]{1,0:T(8,128)(2,1)S(1)}, u32[]{:S(2)}, u32[]{:S(2)}) collective-permute-start(bf16[256,768]{1,0:T(8,128)(2,1)} %bitcast.7.refs_0_), channel_id=1, source_target_pairs={{0,3},{1,0},{2,1},{3,2},{4,7},{5,4},{6,5},{7,6},{8,11},{9,8},{10,9... | collective-permute-start | bytes 1179656 | tf_op jit(solution)/shard_map/ppermute | solution.py:400
  58.0 1.3 %copy-done = bf16[768,768]{1,0:T(8,128)(2,1)S(1)} copy-done((bf16[768,768]{1,0:T(8,128)(2,1)S(1)}, bf16[768,768]{1,0:T(8,128)(2,1)}, u32[]{:S(2)}) %copy-start) | copy-done | bytes 1179672
  59.2 1.3 %copy-done.2 = bf16[768,768]{1,0:T(8,128)(2,1)S(1)} copy-done((bf16[768,768]{1,0:T(8,128)(2,1)S(1)}, bf16[768,768]{1,0:T(8,128)(2,1)}, u32[]{:S(2)}) %copy-start.2) | copy-done | bytes 1179672
  60.5 2.4 %camera_attention.1.refs_2_ = f32[768,256]{1,0:T(8,128)S(1)} custom-call(bf16[64,8,128]{2,1,0:T(8,128)(2,1)S(1)} %slice.14.p0, bf16[64,8,128]{2,1,0:T(8,128)(2,1)S(1)} %collective-permute-done.3.p1, bf16[64,8,128]{2,1,0:T(8,128)(2,1)S(1)} %collective-permute-done.4.p2, bf16[64,8,128]{2,1,0:T(8,128)(2,1)S(1)} %collective-permute-done.5.p3, ...), custom_call_target="tpu_custom_call" | custom-call | flops 704643072 | bytes 2359296 | tf_op jit(solution)/shard_map/camera_attention/pallas_call | solution.py:403
  63.0 3.4 %cross_own.1 = (f32[768,256]{1,0:T(8,128)S(1)}, f32[24,256]{1,0:T(8,128)S(1)}, f32[24,256]{1,0:T(8,128)S(1)}) custom-call(bf16[256,768]{1,0:T(8,128)(2,1)} %bitcast.7.refs_0_, bf16[256,768]{1,0:T(8,128)(2,1)S(1)} %get-tuple-element.37.q_ref.refs_1_.refs_5_.refs_3_, bf16[768,768]{1,0:T(8,128)(2,1)S(1)} %copy-done.1, bf16[768,768]{1,0:T(8,128)(2,1)S(1)} %copy-done.3), custom_call_target="tpu_custom_call" | custom-call | flops 1409286144 | bytes 2359296 | tf_op jit(solution)/shard_map/cross_own/pallas_call | solution.py:305
  66.4 0.2 collective-permute-done.6.refs_0_
  66.6 0.1 collective-permute-start.7
  66.7 3.5 %collective-permute-start.9 = (bf16[128,768]{1,0:T(8,128)(2,1)S(1)}, bf16[128,768]{1,0:T(8,128)(2,1)S(1)}, u32[]{:S(2)}, u32[]{:S(2)}) collective-permute-start(bf16[128,768]{1,0:T(8,128)(2,1)S(1)} %slice.16), channel_id=1, source_target_pairs={{0,3},{1,0},{2,1},{3,2},{4,7},{5,4},{6,5},{7,6},{8,11},{9,8},{10,9... | collective-permute-start | bytes 589832 | tf_op jit(solution)/shard_map/ppermute | solution.py:402
  70.2 4.1 %cross_near.1 = (f32[768,256]{1,0:T(8,128)S(1)}, f32[24,256]{1,0:T(8,128)S(1)}, f32[24,256]{1,0:T(8,128)S(1)}) custom-call(bf16[256,768]{1,0:T(8,128)(2,1)S(1)} %collective-permute-done.6.refs_0_, bf16[256,768]{1,0:T(8,128)(2,1)S(1)} %collective-permute-done.8.refs_1_, f32[768,256]{1,0:T(8,128)S(1)} %get-tuple-element.38.refs_2_, ...), custom_call_target="tpu_custom_call" | custom-call | flops 2818572288 | bytes 2359296 | tf_op jit(solution)/shard_map/cross_near/pallas_call | solution.py:305
  74.4 3.8 %cross_far.1 = f32[256,768]{1,0:T(8,128)} custom-call(bf16[128,768]{1,0:T(8,128)(2,1)S(1)} %collective-permute-done.7.refs_0_, bf16[128,768]{1,0:T(8,128)(2,1)S(1)} %collective-permute-done.9.refs_1_, f32[768,256]{1,0:T(8,128)S(1)} %camera_attention.1.refs_2_, bf16[256,768]{1,0:T(8,128)(2,1)S(1)} %get-tuple-element.37.q_ref.refs_1_.refs_5_.refs_3_, ...), custom_call_target="tpu_custom_call" | custom-call | flops 1711276032 | bytes 2359296 | tf_op jit(solution)/shard_map/cross_far/pallas_call | solution.py:318
  (53 shorter events, 0.2 us)
Async XLA Ops:
  0.0 14.5 %copy-start.4 = (bf16[256,768]{1,0:T(8,128)(2,1)S(1)}, bf16[256,768]{1,0:T(8,128)(2,1)}, u32[]{:S(2)}) copy-start(bf16[256,768]{1,0:T(8,128)(2,1)} %refs_9_.1) | copy-start | bytes 1179652
  0.0 14.6 %copy-start.9 = (f32[768]{0:T(1024)S(1)}, f32[768]{0:T(1024)}, u32[]{:S(2)}) copy-start(f32[768]{0:T(1024)} %gain.3) | copy-start | bytes 9220
  0.0 14.6 %copy-start.10 = (f32[768]{0:T(1024)S(1)}, f32[768]{0:T(1024)}, u32[]{:S(2)}) copy-start(f32[768]{0:T(1024)} %shift.3) | copy-start | bytes 9220
  0.0 20.2 %copy-start.19 = (s32[64]{0:T(128)S(1)}, s32[64]{0:T(128)}, u32[]{:S(2)}) copy-start(s32[64]{0:T(128)} %param.32) | copy-start | bytes 772
  2.4 18.4 %copy-start.5 = (bf16[768,768]{1,0:T(8,128)(2,1)S(1)}, bf16[768,768]{1,0:T(8,128)(2,1)}, u32[]{:S(2)}) copy-start(bf16[768,768]{1,0:T(8,128)(2,1)} %wc.1) | copy-start | bytes 3538948
  2.4 18.4 %copy-start.11 = (f32[768]{0:T(1024)S(1)}, f32[768]{0:T(1024)}, u32[]{:S(2)}) copy-start(f32[768]{0:T(1024)} %gain.4) | copy-start | bytes 9220
  2.4 18.4 %copy-start.12 = (f32[768]{0:T(1024)S(1)}, f32[768]{0:T(1024)}, u32[]{:S(2)}) copy-start(f32[768]{0:T(1024)} %shift.4) | copy-start | bytes 9220
  2.4 28.0 %all-to-all-start = ((bf16[64,32,128]{2,1,0:T(8,128)(2,1)}), bf16[64,32,128]{2,1,0:T(8,128)(2,1)S(1)}, u32[]{:S(2)}, u32[]{:S(2)}) async-start(bf16[64,32,128]{2,1,0:T(8,128)(2,1)} %bitcast.11), calls=%async_computation | async-start | bytes 1048576 | tf_op jit(solution)/shard_map/all_to_all | solution.py:368
  14.9 28.0 %collective-permute-start = (bf16[256,768]{1,0:T(8,128)(2,1)S(1)}, bf16[256,768]{1,0:T(8,128)(2,1)}, u32[]{:S(2)}, u32[]{:S(2)}) collective-permute-start(bf16[256,768]{1,0:T(8,128)(2,1)S(1)} %self_norm.1.h_ref.refs_0_), channel_id=1, source_target_pairs={{0,1},{1,2},{2,3},{3,0},{4,5},{5,6},{6,7},{7,4},{8,9},{9,10},{10,1... | collective-permute-start | bytes 1179656 | tf_op jit(solution)/shard_map/ppermute | solution.py:345
  16.5 28.3 %collective-permute-start.1 = (bf16[256,768]{1,0:T(8,128)(2,1)S(1)}, bf16[256,768]{1,0:T(8,128)(2,1)}, u32[]{:S(2)}, u32[]{:S(2)}) collective-permute-start(bf16[256,768]{1,0:T(8,128)(2,1)S(1)} %self_norm.1.h_ref.refs_0_), channel_id=1, source_target_pairs={{0,3},{1,0},{2,1},{3,2},{4,7},{5,4},{6,5},{7,6},{8,11},{9,8},{10,9... | collective-permute-start | bytes 1179656 | tf_op jit(solution)/shard_map/ppermute | solution.py:345
  18.2 26.7 %collective-permute-start.2 = (bf16[256,768]{1,0:T(8,128)(2,1)S(1)}, bf16[256,768]{1,0:T(8,128)(2,1)}, u32[]{:S(2)}, u32[]{:S(2)}) collective-permute-start(bf16[256,768]{1,0:T(8,128)(2,1)S(1)} %self_norm.1.h_ref.refs_0_), channel_id=1, source_target_pairs={{0,2},{1,3},{2,0},{3,1},{4,6},{5,7},{6,4},{7,5},{8,10},{9,11},{10,... | collective-permute-start | bytes 1179656 | tf_op jit(solution)/shard_map/ppermute | solution.py:345
  20.8 1.3 %copy-start.6 = (bf16[768,768]{1,0:T(8,128)(2,1)S(1)}, bf16[768,768]{1,0:T(8,128)(2,1)}, u32[]{:S(2)}) copy-start(bf16[768,768]{1,0:T(8,128)(2,1)} %ws.1) | copy-start | bytes 3538948
  22.1 1.7 %copy-start.13 = (bf16[768,768]{1,0:T(8,128)(2,1)S(1)}, bf16[768,768]{1,0:T(8,128)(2,1)}, u32[]{:S(2)}) copy-start(bf16[768,768]{1,0:T(8,128)(2,1)} %refs_3_.4) | copy-start | bytes 3538948
  22.1 1.8 %copy-start.14 = (bf16[768,768]{1,0:T(8,128)(2,1)S(1)}, bf16[768,768]{1,0:T(8,128)(2,1)}, u32[]{:S(2)}) copy-start(bf16[768,768]{1,0:T(8,128)(2,1)} %refs_5_.2) | copy-start | bytes 3538948
  23.8 2.4 %copy-start.15 = (bf16[256,768]{1,0:T(8,128)(2,1)}, bf16[256,768]{1,0:T(8,128)(2,1)S(1)}, u32[]{:S(2)}) copy-start(bf16[256,768]{1,0:T(8,128)(2,1)S(1)} %get-tuple-element.25.refs_1_.refs_4_) | copy-start | bytes 1179652
  26.3 18.6 %copy-start.16 = (f32[768,256]{1,0:T(8,128)}, f32[768,256]{1,0:T(8,128)S(1)}, u32[]{:S(2)}) copy-start(f32[768,256]{1,0:T(8,128)S(1)} %get-tuple-element.30.refs_6_) | copy-start | bytes 2359300
  26.3 18.6 %copy-start.17 = (f32[24,256]{1,0:T(8,128)}, f32[24,256]{1,0:T(8,128)S(1)}, u32[]{:S(2)}) copy-start(f32[24,256]{1,0:T(8,128)S(1)} %get-tuple-element.31.refs_7_) | copy-start | bytes 73732
  26.3 18.6 %copy-start.18 = (f32[24,256]{1,0:T(8,128)}, f32[24,256]{1,0:T(8,128)S(1)}, u32[]{:S(2)}) copy-start(f32[24,256]{1,0:T(8,128)S(1)} %get-tuple-element.32.refs_8_) | copy-start | bytes 73732
  31.8 22.8 %all-to-all-start.1 = ((bf16[64,24,128]{2,1,0:T(8,128)(2,1)}), bf16[64,24,128]{2,1,0:T(8,128)(2,1)}, u32[]{:S(2)}, u32[]{:S(2)}) async-start(bf16[64,24,128]{2,1,0:T(8,128)(2,1)} %bitcast.4), calls=%async_computation.1 | async-start | bytes 786432 | tf_op jit(solution)/shard_map/all_to_all | solution.py:395
  39.6 15.0 %collective-permute-start.3 = (bf16[64,8,128]{2,1,0:T(8,128)(2,1)S(1)}, bf16[64,8,128]{2,1,0:T(8,128)(2,1)S(1)}, u32[]{:S(2)}, u32[]{:S(2)}) collective-permute-start(bf16[64,8,128]{2,1,0:T(8,128)(2,1)S(1)} %slice.14.p0), channel_id=1, source_target_pairs={{0,1},{1,2},{2,3},{3,0},{4,5},{5,6},{6,7},{7,4},{8,9},{9,10},{10,1... | collective-permute-start | bytes 393224 | tf_op jit(solution)/shard_map/ppermute | solution.py:345
  41.2 13.4 %collective-permute-start.4 = (bf16[64,8,128]{2,1,0:T(8,128)(2,1)S(1)}, bf16[64,8,128]{2,1,0:T(8,128)(2,1)S(1)}, u32[]{:S(2)}, u32[]{:S(2)}) collective-permute-start(bf16[64,8,128]{2,1,0:T(8,128)(2,1)S(1)} %slice.14.p0), channel_id=1, source_target_pairs={{0,3},{1,0},{2,1},{3,2},{4,7},{5,4},{6,5},{7,6},{8,11},{9,8},{10,9... | collective-permute-start | bytes 393224 | tf_op jit(solution)/shard_map/ppermute | solution.py:345
  42.9 11.7 %collective-permute-start.5 = (bf16[64,8,128]{2,1,0:T(8,128)(2,1)S(1)}, bf16[64,8,128]{2,1,0:T(8,128)(2,1)S(1)}, u32[]{:S(2)}, u32[]{:S(2)}) collective-permute-start(bf16[64,8,128]{2,1,0:T(8,128)(2,1)S(1)} %slice.14.p0), channel_id=1, source_target_pairs={{0,2},{1,3},{2,0},{3,1},{4,6},{5,7},{6,4},{7,5},{8,10},{9,11},{10,... | collective-permute-start | bytes 393224 | tf_op jit(solution)/shard_map/ppermute | solution.py:345
  54.7 11.9 %collective-permute-start.6 = (bf16[256,768]{1,0:T(8,128)(2,1)}, bf16[256,768]{1,0:T(8,128)(2,1)S(1)}, u32[]{:S(2)}, u32[]{:S(2)}) collective-permute-start(bf16[256,768]{1,0:T(8,128)(2,1)} %bitcast.7.refs_0_), channel_id=1, source_target_pairs={{0,1},{1,2},{2,3},{3,0},{4,5},{5,6},{6,7},{7,4},{8,9},{9,10},{10,1... | collective-permute-start | bytes 1179656 | tf_op jit(solution)/shard_map/ppermute | solution.py:399
  55.4 11.3 %collective-permute-start.8 = (bf16[256,768]{1,0:T(8,128)(2,1)}, bf16[256,768]{1,0:T(8,128)(2,1)S(1)}, u32[]{:S(2)}, u32[]{:S(2)}) collective-permute-start(bf16[256,768]{1,0:T(8,128)(2,1)} %bitcast.7.refs_0_), channel_id=1, source_target_pairs={{0,3},{1,0},{2,1},{3,2},{4,7},{5,4},{6,5},{7,6},{8,11},{9,8},{10,9... | collective-permute-start | bytes 1179656 | tf_op jit(solution)/shard_map/ppermute | solution.py:400
  58.0 1.3 %copy-start = (bf16[768,768]{1,0:T(8,128)(2,1)S(1)}, bf16[768,768]{1,0:T(8,128)(2,1)}, u32[]{:S(2)}) copy-start(bf16[768,768]{1,0:T(8,128)(2,1)} %refs_4_.1) | copy-start | bytes 3538948
  59.2 1.3 %copy-start.2 = (bf16[768,768]{1,0:T(8,128)(2,1)S(1)}, bf16[768,768]{1,0:T(8,128)(2,1)}, u32[]{:S(2)}) copy-start(bf16[768,768]{1,0:T(8,128)(2,1)} %refs_5_.3) | copy-start | bytes 3538948
  60.5 2.5 %copy-start.1 = (bf16[768,768]{1,0:T(8,128)(2,1)S(1)}, bf16[768,768]{1,0:T(8,128)(2,1)}, u32[]{:S(2)}) copy-start(bf16[768,768]{1,0:T(8,128)(2,1)} %refs_4_.1) | copy-start | bytes 3538948
  60.5 2.5 %copy-start.3 = (bf16[768,768]{1,0:T(8,128)(2,1)S(1)}, bf16[768,768]{1,0:T(8,128)(2,1)}, u32[]{:S(2)}) copy-start(bf16[768,768]{1,0:T(8,128)(2,1)} %refs_5_.3) | copy-start | bytes 3538948
  66.6 7.7 %collective-permute-start.7 = (bf16[128,768]{1,0:T(8,128)(2,1)S(1)}, bf16[128,768]{1,0:T(8,128)(2,1)S(1)}, u32[]{:S(2)}, u32[]{:S(2)}) collective-permute-start(bf16[128,768]{1,0:T(8,128)(2,1)S(1)} %slice.15), channel_id=1, source_target_pairs={{0,1},{1,2},{2,3},{3,0},{4,5},{5,6},{6,7},{7,4},{8,9},{9,10},{10,1... | collective-permute-start | bytes 589832 | tf_op jit(solution)/shard_map/ppermute | solution.py:401
  66.7 7.6 %collective-permute-start.9 = (bf16[128,768]{1,0:T(8,128)(2,1)S(1)}, bf16[128,768]{1,0:T(8,128)(2,1)S(1)}, u32[]{:S(2)}, u32[]{:S(2)}) collective-permute-start(bf16[128,768]{1,0:T(8,128)(2,1)S(1)} %slice.16), channel_id=1, source_target_pairs={{0,3},{1,0},{2,1},{3,2},{4,7},{5,4},{6,5},{7,6},{8,11},{9,8},{10,9... | collective-permute-start | bytes 589832 | tf_op jit(solution)/shard_map/ppermute | solution.py:402
  70.2 4.1 %copy-start.7 = (bf16[768,768]{1,0:T(8,128)(2,1)S(1)}, bf16[768,768]{1,0:T(8,128)(2,1)}, u32[]{:S(2)}) copy-start(bf16[768,768]{1,0:T(8,128)(2,1)} %refs_6_.3) | copy-start | bytes 3538948
  70.2 4.1 %copy-start.8 = (f32[256,768]{1,0:T(8,128)S(1)}, f32[256,768]{1,0:T(8,128)}, u32[]{:S(2)}) copy-start(f32[256,768]{1,0:T(8,128)} %self_others.1.refs_10_) | copy-start | bytes 2359300

commit v6 on v5

--- a/solution.py
+++ b/solution.py
@@ -33,39 +33,19 @@
     return lax.dot_general(left, right, (((1,), (1,)), ((), ())), preferred_element_type=jnp.float32)
 
 
-def heads(q, k, v):
+def heads_stacked(q, k, vt):
+    rows = q.shape[0]
     lane = lax.broadcasted_iota(jnp.int32, q.shape, 1) // HDIM
-    score = lambda head: mm_nt(jnp.where(lane == head, q, jnp.zeros_like(q)), k)
-    ahead = score(0)
+    stack = [jnp.where(lane == head, q, jnp.zeros_like(q)) for head in range(HEADS)]
+    s = mm_nt(k, jnp.concatenate(stack, axis=0))
+    top = jnp.max(s, axis=0, keepdims=True)
+    p = jnp.exp(s - top)
+    total = jnp.sum(p, axis=0, keepdims=True)
+    p = p.astype(BF)
     for head in range(HEADS):
-        s = ahead
-        if head + 1 < HEADS:
-            ahead = score(head + 1)
-        top = jnp.max(s, axis=-1, keepdims=True)
-        p = jnp.exp(s - top)
-        yield lane == head, top, jnp.sum(p, axis=-1, keepdims=True), mm(p.astype(BF), v)
-
-
-def attend(q, k, v):
-    out = None
-    for mine, _, total, c in heads(q, k, v):
-        c = c / total
-        out = c if out is None else jnp.where(mine, c, out)
-    return out
-
-
-def heads_t(q, k, vt):
-    lane = lax.broadcasted_iota(jnp.int32, q.shape, 1) // HDIM
-    score = lambda head: mm_nt(k, jnp.where(lane == head, q, jnp.zeros_like(q)))
-    ahead = score(0)
-    for head in range(HEADS):
-        s = ahead
-        if head + 1 < HEADS:
-            ahead = score(head + 1)
-        top = jnp.max(s, axis=0, keepdims=True)
-        p = jnp.exp(s - top)
-        c = mm(vt[HDIM * head : HDIM * (head + 1)], p.astype(BF))
-        yield slice(HDIM * head, HDIM * (head + 1)), head, top, jnp.sum(p, axis=0, keepdims=True), c
+        at = slice(HDIM * head, HDIM * (head + 1))
+        cols = slice(rows * head, rows * (head + 1))
+        yield at, head, top[:, cols], total[:, cols], mm(vt[at], p[:, cols])
 
 
 def mm_tn(left, right):
@@ -120,11 +100,6 @@
             c_ref[step * COLS + at.start : step * COLS + at.stop] = c * (1.0 / total)
 
 
-def keys_values(blocks, wk, wv):
-    m = blocks[0][...] if len(blocks) == 1 else jnp.concatenate([r[...] for r in blocks], axis=0)
-    return mm(m, wk[...]).astype(BF), jnp.transpose(mm(m, wv[...]).astype(BF))
-
-
 def merged(parts, state):
     c_ref, t_ref, l_ref = state
     for at, head, top, total, c in parts:
@@ -139,7 +114,7 @@
     at = slice(step * COLS, (step + 1) * COLS)
     k = mm(m, wk[:, at]).astype(BF)
     vt = jnp.transpose(mm(m, wv[:, at]).astype(BF))
-    parts = heads_t(q_ref[:, at], k, vt)
+    parts = heads_stacked(q_ref[:, at], k, vt)
     if not state:
         return parts
     c_ref, t_ref, l_ref = state
@@ -212,7 +187,7 @@
             start("o", wo, ob)
         k = mm(hb[...], kb[:, at]).astype(BF)
         vt = jnp.transpose(mm(hb[...], vb[:, at]).astype(BF))
-        parts = heads_t(qb[:, at], k, vt)
+        parts = heads_stacked(qb[:, at], k, vt)
         if step == 0:
             for name in "ctl":
                 moves[name].wait()
@@ -254,10 +229,7 @@
 
 
 WCOL = pl.BlockSpec((D, COLS), lambda i: (0, i))
-WROW = pl.BlockSpec((COLS, D), lambda i: (i, 0))
 XCOL = pl.BlockSpec((ROWS, COLS), lambda i: (0, i))
-CTX = pl.BlockSpec((COLS, ROWS), lambda i: (i, 0))
-STAT = pl.BlockSpec((8, ROWS), lambda i: (i, 0))
 VEC = full((D,))
 X = full((ROWS, D))
 W = full((D, D))

time: 79.2 us -> 79.2 us (level)
  the two profiles are of different devices: /device:TPU:2 before, /device:TPU:56 now
where the time goes in v6:
time: 79.2 us; the launch traced here: 78.7 us
  starting transfers between devices  29.3 us (37%)
  Pallas kernels  29 us (37%)
  waiting for transfers between devices  14.1 us (18%)
  local copies, waits for them, and re-layouts  5.89 us (7%)
    all_to_all x1, starting transfers between devices, local(): lax.all_to_all(packed, ROUTE, split_axis=0, concat_axis=0, tiled=True)  11.7 us
    pallas_call x3, Pallas kernels, call_part(): call(name, functools.partial(part_kernel, len(blocks)), [full(b.shape) fo...  9.73 us
    pallas_call x1, Pallas kernels, call_others(): pl.pallas_call(others_kernel, in_specs=[pl.BlockSpec(memory_space=pl.ANY)...  9.38 us
    all_to_all x1, waiting for transfers between devices, local(): lax.all_to_all(packed, ROUTE, split_axis=0, concat_axis=0, tiled=True)  7.2 us
    ppermute x6, starting transfers between devices, around(): return [lax.ppermute(value, 'tok', turn(shift)) for shift in (1, 3, 2)]  6.68 us
    all_to_all x1, starting transfers between devices, local(): lax.all_to_all(onward, ROUTE, split_axis=0, concat_axis=0, tiled=True)  6.48 us
    unnamed x40, local copies, waits for them, and re-layouts  3.87 us
    pallas_call x1, Pallas kernels, call_last(): call(name, functools.partial(last_kernel, len(blocks)), [full(b.shape) fo...  3.5 us
  transfers between devices with their start and end apart: 12, of which 5 were waited for; matrix products, arithmetic and copies ran while one was open for 3% of the time, Pallas kernels for 29%

profile of v6, /device:TPU:56, one launch (start us, length us, event | category | flops | bytes accessed | tf_op | source)
XLA Modules:
  0.0 78.7 jit_solution(12846380717769534002)
XLA Ops:
  0.0 2.4 %memory_norm.1 = bf16[32,2,4,8,128]{4,3,2,1,0:T(8,128)(2,1)} custom-call(s32[8,16]{1,0:T(8,128)} %cams.1, bf16[256,768]{1,0:T(8,128)(2,1)} %refs_9_.1, f32[768]{0:T(1024)} %gain.5, f32[768]{0:T(1024)} %shift.5), custom_call_target="tpu_custom_call" | custom-call | tf_op jit(solution)/shard_map/memory_norm/pallas_call | solution.py:266
  2.4 11.7 %all-to-all-start = ((bf16[64,32,128]{2,1,0:T(8,128)(2,1)}), bf16[64,32,128]{2,1,0:T(8,128)(2,1)S(1)}, u32[]{:S(2)}, u32[]{:S(2)}) async-start(bf16[64,32,128]{2,1,0:T(8,128)(2,1)} %bitcast.11), calls=%async_computation | async-start | bytes 1048576 | tf_op jit(solution)/shard_map/all_to_all | solution.py:340
  14.1 0.3 self_norm.1.h_ref.refs_0_
  14.5 0.3 collective-permute-start
  14.8 1.8 %collective-permute-start.1 = (bf16[256,768]{1,0:T(8,128)(2,1)S(1)}, bf16[256,768]{1,0:T(8,128)(2,1)}, u32[]{:S(2)}, u32[]{:S(2)}) collective-permute-start(bf16[256,768]{1,0:T(8,128)(2,1)S(1)} %self_norm.1.h_ref.refs_0_), channel_id=1, source_target_pairs={{0,3},{1,0},{2,1},{3,2},{4,7},{5,4},{6,5},{7,6},{8,11},{9,8},{10,9... | collective-permute-start | bytes 1179656 | tf_op jit(solution)/shard_map/ppermute | solution.py:317
  16.6 1.2 %collective-permute-start.2 = (bf16[256,768]{1,0:T(8,128)(2,1)S(1)}, bf16[256,768]{1,0:T(8,128)(2,1)}, u32[]{:S(2)}, u32[]{:S(2)}) collective-permute-start(bf16[256,768]{1,0:T(8,128)(2,1)S(1)} %self_norm.1.h_ref.refs_0_), channel_id=1, source_target_pairs={{0,2},{1,3},{2,0},{3,1},{4,6},{5,7},{6,4},{7,5},{8,10},{9,11},{10,... | collective-permute-start | bytes 1179656 | tf_op jit(solution)/shard_map/ppermute | solution.py:317
  17.9 0.1 copy.19
  18.3 0.1 add.108
  18.5 1.3 %copy-done.6 = bf16[768,768]{1,0:T(8,128)(2,1)S(1)} copy-done((bf16[768,768]{1,0:T(8,128)(2,1)S(1)}, bf16[768,768]{1,0:T(8,128)(2,1)}, u32[]{:S(2)}) %copy-start.6) | copy-done | bytes 1179672
  19.7 1.7 %queries.1 = (bf16[256,768]{1,0:T(8,128)(2,1)S(1)}, bf16[256,768]{1,0:T(8,128)(2,1)S(1)}) custom-call(bf16[256,768]{1,0:T(8,128)(2,1)S(1)} %copy-done.4, bf16[256,768]{1,0:T(8,128)(2,1)S(1)} %self_norm.1.h_ref.refs_0_, f32[768]{0:T(1024)S(1)} %copy-done.11, f32[768]{0:T(1024)S(1)} %copy-done.12, bf16[768,768]{1,0:T(8,128)(2,1)S(1)} %copy-done.5, ...), custom_call_target="tpu_custom_call" | custom-call | flops 603979776 | bytes 2359296 | tf_op jit(solution)/shard_map/queries/pallas_call | solution.py:352
  21.5 2.4 %self_own.1 = (f32[768,256]{1,0:T(8,128)S(1)}, f32[24,256]{1,0:T(8,128)S(1)}, f32[24,256]{1,0:T(8,128)S(1)}) custom-call(bf16[256,768]{1,0:T(8,128)(2,1)S(1)} %self_norm.1.h_ref.refs_0_, bf16[256,768]{1,0:T(8,128)(2,1)S(1)} %get-tuple-element.25.refs_1_.refs_4_, bf16[768,768]{1,0:T(8,128)(2,1)S(1)} %copy-done.13, bf16[768,768]{1,0:T(8,128)(2,1)S(1)} %copy-done.14), custom_call_target="tpu_custom_call" | custom-call | flops 1409286144 | bytes 2359296 | tf_op jit(solution)/shard_map/self_own/pallas_call | solution.py:277
  24.0 7.2 %all-to-all-done = bf16[64,32,128]{2,1,0:T(8,128)(2,1)S(1)} async-done(((bf16[64,32,128]{2,1,0:T(8,128)(2,1)}), bf16[64,32,128]{2,1,0:T(8,128)(2,1)S(1)}, u32[]{:S(2)}, u32[]{:S(2)}) %all-to-all-start) | async-done | bytes 524320 | tf_op jit(solution)/shard_map/all_to_all | solution.py:340
  31.2 1.5 %gather_fusion = bf16[192,8,128]{2,1,0:T(8,128)(2,1)} fusion(bf16[256,8,128]{2,1,0:T(8,128)(2,1)S(1)} %bitcast.10, s32[1024]{0:T(1024)S(1)} %pad_clamp_fusion), kind=kCustom, calls=%fused_computation | custom fusion | bytes 787200 | tf_op jit(solution)/shard_map/gather | solution.py:344
  32.7 6.5 %all-to-all-start.1 = ((bf16[64,24,128]{2,1,0:T(8,128)(2,1)}), bf16[64,24,128]{2,1,0:T(8,128)(2,1)}, u32[]{:S(2)}, u32[]{:S(2)}) async-start(bf16[64,24,128]{2,1,0:T(8,128)(2,1)} %bitcast.4), calls=%async_computation.1 | async-start | bytes 786432 | tf_op jit(solution)/shard_map/all_to_all | solution.py:367
  39.2 0.3 collective-permute-start.3
  39.5 1.8 %collective-permute-start.4 = (bf16[64,8,128]{2,1,0:T(8,128)(2,1)S(1)}, bf16[64,8,128]{2,1,0:T(8,128)(2,1)S(1)}, u32[]{:S(2)}, u32[]{:S(2)}) collective-permute-start(bf16[64,8,128]{2,1,0:T(8,128)(2,1)S(1)} %slice.14.p0), channel_id=1, source_target_pairs={{0,3},{1,0},{2,1},{3,2},{4,7},{5,4},{6,5},{7,6},{8,11},{9,8},{10,9... | collective-permute-start | bytes 393224 | tf_op jit(solution)/shard_map/ppermute | solution.py:317
  41.3 1.2 %collective-permute-start.5 = (bf16[64,8,128]{2,1,0:T(8,128)(2,1)S(1)}, bf16[64,8,128]{2,1,0:T(8,128)(2,1)S(1)}, u32[]{:S(2)}, u32[]{:S(2)}) collective-permute-start(bf16[64,8,128]{2,1,0:T(8,128)(2,1)S(1)} %slice.14.p0), channel_id=1, source_target_pairs={{0,2},{1,3},{2,0},{3,1},{4,6},{5,7},{6,4},{7,5},{8,10},{9,11},{10,... | collective-permute-start | bytes 393224 | tf_op jit(solution)/shard_map/ppermute | solution.py:317
  42.5 9.4 %self_others.1.refs_10_ = f32[256,768]{1,0:T(8,128)} custom-call(bf16[256,768]{1,0:T(8,128)(2,1)} %collective-permute-done.refs_0_, bf16[256,768]{1,0:T(8,128)(2,1)} %collective-permute-done.1.refs_1_, bf16[256,768]{1,0:T(8,128)(2,1)} %collective-permute-done.2.refs_2_, bf16[768,768]{1,0:T(8,128)(2,1)} %refs_3_.4, bf16[256,768]{1,0:T(8,128)(2,1)} %copy-done.15, ...), custom_call_target="tpu_custom_call" | custom-call | flops 4227858432 | bytes 4718592 | tf_op jit(solution)/shard_map/self_others/pallas_call | solution.py:209
  52.0 1.8 %all-to-all-done.1 = bf16[64,24,128]{2,1,0:T(8,128)(2,1)} async-done(((bf16[64,24,128]{2,1,0:T(8,128)(2,1)}), bf16[64,24,128]{2,1,0:T(8,128)(2,1)}, u32[]{:S(2)}, u32[]{:S(2)}) %all-to-all-start.1) | async-done | bytes 393248 | tf_op jit(solution)/shard_map/all_to_all | solution.py:367
  53.7 0.5 collective-permute-start.6
  54.2 1.5 %collective-permute-start.8 = (bf16[256,768]{1,0:T(8,128)(2,1)}, bf16[256,768]{1,0:T(8,128)(2,1)S(1)}, u32[]{:S(2)}, u32[]{:S(2)}) collective-permute-start(bf16[256,768]{1,0:T(8,128)(2,1)} %bitcast.7.refs_0_), channel_id=1, source_target_pairs={{0,3},{1,0},{2,1},{3,2},{4,7},{5,4},{6,5},{7,6},{8,11},{9,8},{10,9... | collective-permute-start | bytes 1179656 | tf_op jit(solution)/shard_map/ppermute | solution.py:372
  55.8 1.3 %copy-done = bf16[768,768]{1,0:T(8,128)(2,1)S(1)} copy-done((bf16[768,768]{1,0:T(8,128)(2,1)S(1)}, bf16[768,768]{1,0:T(8,128)(2,1)}, u32[]{:S(2)}) %copy-start) | copy-done | bytes 1179672
  57.0 1.3 %copy-done.2 = bf16[768,768]{1,0:T(8,128)(2,1)S(1)} copy-done((bf16[768,768]{1,0:T(8,128)(2,1)S(1)}, bf16[768,768]{1,0:T(8,128)(2,1)}, u32[]{:S(2)}) %copy-start.2) | copy-done | bytes 1179672
  58.3 2.0 %camera_attention.1.refs_2_ = f32[768,256]{1,0:T(8,128)S(1)} custom-call(bf16[64,8,128]{2,1,0:T(8,128)(2,1)S(1)} %slice.14.p0, bf16[64,8,128]{2,1,0:T(8,128)(2,1)S(1)} %collective-permute-done.3.p1, bf16[64,8,128]{2,1,0:T(8,128)(2,1)S(1)} %collective-permute-done.4.p2, bf16[64,8,128]{2,1,0:T(8,128)(2,1)S(1)} %collective-permute-done.5.p3, ...), custom_call_target="tpu_custom_call" | custom-call | flops 704643072 | bytes 2359296 | tf_op jit(solution)/shard_map/camera_attention/pallas_call | solution.py:375
  60.4 3.4 %cross_own.1 = (f32[768,256]{1,0:T(8,128)S(1)}, f32[24,256]{1,0:T(8,128)S(1)}, f32[24,256]{1,0:T(8,128)S(1)}) custom-call(bf16[256,768]{1,0:T(8,128)(2,1)} %bitcast.7.refs_0_, bf16[256,768]{1,0:T(8,128)(2,1)S(1)} %get-tuple-element.37.q_ref.refs_1_.refs_5_.refs_3_, bf16[768,768]{1,0:T(8,128)(2,1)S(1)} %copy-done.1, bf16[768,768]{1,0:T(8,128)(2,1)S(1)} %copy-done.3), custom_call_target="tpu_custom_call" | custom-call | flops 1409286144 | bytes 2359296 | tf_op jit(solution)/shard_map/cross_own/pallas_call | solution.py:277
  63.8 2.0 %collective-permute-done.6.refs_0_ = bf16[256,768]{1,0:T(8,128)(2,1)S(1)} collective-permute-done((bf16[256,768]{1,0:T(8,128)(2,1)}, bf16[256,768]{1,0:T(8,128)(2,1)S(1)}, u32[]{:S(2)}, u32[]{:S(2)}) %collective-permute-start.6) | collective-permute-done | bytes 393248 | tf_op jit(solution)/shard_map/ppermute | solution.py:371
  65.8 1.6 %collective-permute-start.7 = (bf16[128,768]{1,0:T(8,128)(2,1)S(1)}, bf16[128,768]{1,0:T(8,128)(2,1)S(1)}, u32[]{:S(2)}, u32[]{:S(2)}) collective-permute-start(bf16[128,768]{1,0:T(8,128)(2,1)S(1)} %slice.15), channel_id=1, source_target_pairs={{0,1},{1,2},{2,3},{3,0},{4,5},{5,6},{6,7},{7,4},{8,9},{9,10},{10,1... | collective-permute-start | bytes 589832 | tf_op jit(solution)/shard_map/ppermute | solution.py:373
  67.4 0.8 %collective-permute-start.9 = (bf16[128,768]{1,0:T(8,128)(2,1)S(1)}, bf16[128,768]{1,0:T(8,128)(2,1)S(1)}, u32[]{:S(2)}, u32[]{:S(2)}) collective-permute-start(bf16[128,768]{1,0:T(8,128)(2,1)S(1)} %slice.16), channel_id=1, source_target_pairs={{0,3},{1,0},{2,1},{3,2},{4,7},{5,4},{6,5},{7,6},{8,11},{9,8},{10,9... | collective-permute-start | bytes 589832 | tf_op jit(solution)/shard_map/ppermute | solution.py:374
  68.3 3.9 %cross_near.1 = (f32[768,256]{1,0:T(8,128)S(1)}, f32[24,256]{1,0:T(8,128)S(1)}, f32[24,256]{1,0:T(8,128)S(1)}) custom-call(bf16[256,768]{1,0:T(8,128)(2,1)S(1)} %collective-permute-done.6.refs_0_, bf16[256,768]{1,0:T(8,128)(2,1)S(1)} %collective-permute-done.8.refs_1_, f32[768,256]{1,0:T(8,128)S(1)} %get-tuple-element.38.refs_2_, ...), custom_call_target="tpu_custom_call" | custom-call | flops 2818572288 | bytes 2359296 | tf_op jit(solution)/shard_map/cross_near/pallas_call | solution.py:277
  72.2 0.5 collective-permute-done.7.refs_0_
  72.7 2.5 %collective-permute-done.9.refs_1_ = bf16[128,768]{1,0:T(8,128)(2,1)S(1)} collective-permute-done((bf16[128,768]{1,0:T(8,128)(2,1)S(1)}, bf16[128,768]{1,0:T(8,128)(2,1)S(1)}, u32[]{:S(2)}, u32[]{:S(2)}) %collective-permute-start.9) | collective-permute-done | bytes 196640 | tf_op jit(solution)/shard_map/ppermute | solution.py:374
  75.2 3.5 %cross_far.1 = f32[256,768]{1,0:T(8,128)} custom-call(bf16[128,768]{1,0:T(8,128)(2,1)S(1)} %collective-permute-done.7.refs_0_, bf16[128,768]{1,0:T(8,128)(2,1)S(1)} %collective-permute-done.9.refs_1_, f32[768,256]{1,0:T(8,128)S(1)} %camera_attention.1.refs_2_, bf16[256,768]{1,0:T(8,128)(2,1)S(1)} %get-tuple-element.37.q_ref.refs_1_.refs_5_.refs_3_, ...), custom_call_target="tpu_custom_call" | custom-call | flops 1711276032 | bytes 2359296 | tf_op jit(solution)/shard_map/cross_far/pallas_call | solution.py:290
  (53 shorter events, 0.5 us)
Async XLA Ops:
  0.0 14.1 %copy-start.4 = (bf16[256,768]{1,0:T(8,128)(2,1)S(1)}, bf16[256,768]{1,0:T(8,128)(2,1)}, u32[]{:S(2)}) copy-start(bf16[256,768]{1,0:T(8,128)(2,1)} %refs_9_.1) | copy-start | bytes 1179652
  0.0 14.1 %copy-start.9 = (f32[768]{0:T(1024)S(1)}, f32[768]{0:T(1024)}, u32[]{:S(2)}) copy-start(f32[768]{0:T(1024)} %gain.3) | copy-start | bytes 9220
  0.0 14.1 %copy-start.10 = (f32[768]{0:T(1024)S(1)}, f32[768]{0:T(1024)}, u32[]{:S(2)}) copy-start(f32[768]{0:T(1024)} %shift.3) | copy-start | bytes 9220
  0.0 17.8 %copy-start.19 = (s32[64]{0:T(128)S(1)}, s32[64]{0:T(128)}, u32[]{:S(2)}) copy-start(s32[64]{0:T(128)} %param.32) | copy-start | bytes 772
  2.4 16.0 %copy-start.5 = (bf16[768,768]{1,0:T(8,128)(2,1)S(1)}, bf16[768,768]{1,0:T(8,128)(2,1)}, u32[]{:S(2)}) copy-start(bf16[768,768]{1,0:T(8,128)(2,1)} %wc.1) | copy-start | bytes 3538948
  2.4 16.1 %copy-start.11 = (f32[768]{0:T(1024)S(1)}, f32[768]{0:T(1024)}, u32[]{:S(2)}) copy-start(f32[768]{0:T(1024)} %gain.4) | copy-start | bytes 9220
  2.4 16.1 %copy-start.12 = (f32[768]{0:T(1024)S(1)}, f32[768]{0:T(1024)}, u32[]{:S(2)}) copy-start(f32[768]{0:T(1024)} %shift.4) | copy-start | bytes 9220
  2.4 28.8 %all-to-all-start = ((bf16[64,32,128]{2,1,0:T(8,128)(2,1)}), bf16[64,32,128]{2,1,0:T(8,128)(2,1)S(1)}, u32[]{:S(2)}, u32[]{:S(2)}) async-start(bf16[64,32,128]{2,1,0:T(8,128)(2,1)} %bitcast.11), calls=%async_computation | async-start | bytes 1048576 | tf_op jit(solution)/shard_map/all_to_all | solution.py:340
  14.5 26.8 %collective-permute-start = (bf16[256,768]{1,0:T(8,128)(2,1)S(1)}, bf16[256,768]{1,0:T(8,128)(2,1)}, u32[]{:S(2)}, u32[]{:S(2)}) collective-permute-start(bf16[256,768]{1,0:T(8,128)(2,1)S(1)} %self_norm.1.h_ref.refs_0_), channel_id=1, source_target_pairs={{0,1},{1,2},{2,3},{3,0},{4,5},{5,6},{6,7},{7,4},{8,9},{9,10},{10,1... | collective-permute-start | bytes 1179656 | tf_op jit(solution)/shard_map/ppermute | solution.py:317
  14.8 27.7 %collective-permute-start.1 = (bf16[256,768]{1,0:T(8,128)(2,1)S(1)}, bf16[256,768]{1,0:T(8,128)(2,1)}, u32[]{:S(2)}, u32[]{:S(2)}) collective-permute-start(bf16[256,768]{1,0:T(8,128)(2,1)S(1)} %self_norm.1.h_ref.refs_0_), channel_id=1, source_target_pairs={{0,3},{1,0},{2,1},{3,2},{4,7},{5,4},{6,5},{7,6},{8,11},{9,8},{10,9... | collective-permute-start | bytes 1179656 | tf_op jit(solution)/shard_map/ppermute | solution.py:317
  16.6 26.0 %collective-permute-start.2 = (bf16[256,768]{1,0:T(8,128)(2,1)S(1)}, bf16[256,768]{1,0:T(8,128)(2,1)}, u32[]{:S(2)}, u32[]{:S(2)}) collective-permute-start(bf16[256,768]{1,0:T(8,128)(2,1)S(1)} %self_norm.1.h_ref.refs_0_), channel_id=1, source_target_pairs={{0,2},{1,3},{2,0},{3,1},{4,6},{5,7},{6,4},{7,5},{8,10},{9,11},{10,... | collective-permute-start | bytes 1179656 | tf_op jit(solution)/shard_map/ppermute | solution.py:317
  18.4 1.3 %copy-start.6 = (bf16[768,768]{1,0:T(8,128)(2,1)S(1)}, bf16[768,768]{1,0:T(8,128)(2,1)}, u32[]{:S(2)}) copy-start(bf16[768,768]{1,0:T(8,128)(2,1)} %ws.1) | copy-start | bytes 3538948
  19.7 1.7 %copy-start.13 = (bf16[768,768]{1,0:T(8,128)(2,1)S(1)}, bf16[768,768]{1,0:T(8,128)(2,1)}, u32[]{:S(2)}) copy-start(bf16[768,768]{1,0:T(8,128)(2,1)} %refs_3_.4) | copy-start | bytes 3538948
  19.7 1.8 %copy-start.14 = (bf16[768,768]{1,0:T(8,128)(2,1)S(1)}, bf16[768,768]{1,0:T(8,128)(2,1)}, u32[]{:S(2)}) copy-start(bf16[768,768]{1,0:T(8,128)(2,1)} %refs_5_.2) | copy-start | bytes 3538948
  21.5 2.5 %copy-start.15 = (bf16[256,768]{1,0:T(8,128)(2,1)}, bf16[256,768]{1,0:T(8,128)(2,1)S(1)}, u32[]{:S(2)}) copy-start(bf16[256,768]{1,0:T(8,128)(2,1)S(1)} %get-tuple-element.25.refs_1_.refs_4_) | copy-start | bytes 1179652
  23.9 18.6 %copy-start.16 = (f32[768,256]{1,0:T(8,128)}, f32[768,256]{1,0:T(8,128)S(1)}, u32[]{:S(2)}) copy-start(f32[768,256]{1,0:T(8,128)S(1)} %get-tuple-element.30.refs_6_) | copy-start | bytes 2359300
  23.9 18.6 %copy-start.17 = (f32[24,256]{1,0:T(8,128)}, f32[24,256]{1,0:T(8,128)S(1)}, u32[]{:S(2)}) copy-start(f32[24,256]{1,0:T(8,128)S(1)} %get-tuple-element.31.refs_7_) | copy-start | bytes 73732
  23.9 18.6 %copy-start.18 = (f32[24,256]{1,0:T(8,128)}, f32[24,256]{1,0:T(8,128)S(1)}, u32[]{:S(2)}) copy-start(f32[24,256]{1,0:T(8,128)S(1)} %get-tuple-element.32.refs_8_) | copy-start | bytes 73732
  32.7 21.1 %all-to-all-start.1 = ((bf16[64,24,128]{2,1,0:T(8,128)(2,1)}), bf16[64,24,128]{2,1,0:T(8,128)(2,1)}, u32[]{:S(2)}, u32[]{:S(2)}) async-start(bf16[64,24,128]{2,1,0:T(8,128)(2,1)} %bitcast.4), calls=%async_computation.1 | async-start | bytes 786432 | tf_op jit(solution)/shard_map/all_to_all | solution.py:367
  39.2 12.8 %collective-permute-start.3 = (bf16[64,8,128]{2,1,0:T(8,128)(2,1)S(1)}, bf16[64,8,128]{2,1,0:T(8,128)(2,1)S(1)}, u32[]{:S(2)}, u32[]{:S(2)}) collective-permute-start(bf16[64,8,128]{2,1,0:T(8,128)(2,1)S(1)} %slice.14.p0), channel_id=1, source_target_pairs={{0,1},{1,2},{2,3},{3,0},{4,5},{5,6},{6,7},{7,4},{8,9},{9,10},{10,1... | collective-permute-start | bytes 393224 | tf_op jit(solution)/shard_map/ppermute | solution.py:317
  39.5 12.5 %collective-permute-start.4 = (bf16[64,8,128]{2,1,0:T(8,128)(2,1)S(1)}, bf16[64,8,128]{2,1,0:T(8,128)(2,1)S(1)}, u32[]{:S(2)}, u32[]{:S(2)}) collective-permute-start(bf16[64,8,128]{2,1,0:T(8,128)(2,1)S(1)} %slice.14.p0), channel_id=1, source_target_pairs={{0,3},{1,0},{2,1},{3,2},{4,7},{5,4},{6,5},{7,6},{8,11},{9,8},{10,9... | collective-permute-start | bytes 393224 | tf_op jit(solution)/shard_map/ppermute | solution.py:317
  41.3 10.7 %collective-permute-start.5 = (bf16[64,8,128]{2,1,0:T(8,128)(2,1)S(1)}, bf16[64,8,128]{2,1,0:T(8,128)(2,1)S(1)}, u32[]{:S(2)}, u32[]{:S(2)}) collective-permute-start(bf16[64,8,128]{2,1,0:T(8,128)(2,1)S(1)} %slice.14.p0), channel_id=1, source_target_pairs={{0,2},{1,3},{2,0},{3,1},{4,6},{5,7},{6,4},{7,5},{8,10},{9,11},{10,... | collective-permute-start | bytes 393224 | tf_op jit(solution)/shard_map/ppermute | solution.py:317
  53.7 12.1 %collective-permute-start.6 = (bf16[256,768]{1,0:T(8,128)(2,1)}, bf16[256,768]{1,0:T(8,128)(2,1)S(1)}, u32[]{:S(2)}, u32[]{:S(2)}) collective-permute-start(bf16[256,768]{1,0:T(8,128)(2,1)} %bitcast.7.refs_0_), channel_id=1, source_target_pairs={{0,1},{1,2},{2,3},{3,0},{4,5},{5,6},{6,7},{7,4},{8,9},{9,10},{10,1... | collective-permute-start | bytes 1179656 | tf_op jit(solution)/shard_map/ppermute | solution.py:371
  54.2 13.2 %collective-permute-start.8 = (bf16[256,768]{1,0:T(8,128)(2,1)}, bf16[256,768]{1,0:T(8,128)(2,1)S(1)}, u32[]{:S(2)}, u32[]{:S(2)}) collective-permute-start(bf16[256,768]{1,0:T(8,128)(2,1)} %bitcast.7.refs_0_), channel_id=1, source_target_pairs={{0,3},{1,0},{2,1},{3,2},{4,7},{5,4},{6,5},{7,6},{8,11},{9,8},{10,9... | collective-permute-start | bytes 1179656 | tf_op jit(solution)/shard_map/ppermute | solution.py:372
  55.8 1.3 %copy-start = (bf16[768,768]{1,0:T(8,128)(2,1)S(1)}, bf16[768,768]{1,0:T(8,128)(2,1)}, u32[]{:S(2)}) copy-start(bf16[768,768]{1,0:T(8,128)(2,1)} %refs_4_.1) | copy-start | bytes 3538948
  57.0 1.3 %copy-start.2 = (bf16[768,768]{1,0:T(8,128)(2,1)S(1)}, bf16[768,768]{1,0:T(8,128)(2,1)}, u32[]{:S(2)}) copy-start(bf16[768,768]{1,0:T(8,128)(2,1)} %refs_5_.3) | copy-start | bytes 3538948
  58.3 2.1 %copy-start.1 = (bf16[768,768]{1,0:T(8,128)(2,1)S(1)}, bf16[768,768]{1,0:T(8,128)(2,1)}, u32[]{:S(2)}) copy-start(bf16[768,768]{1,0:T(8,128)(2,1)} %refs_4_.1) | copy-start | bytes 3538948
  58.3 2.1 %copy-start.3 = (bf16[768,768]{1,0:T(8,128)(2,1)S(1)}, bf16[768,768]{1,0:T(8,128)(2,1)}, u32[]{:S(2)}) copy-start(bf16[768,768]{1,0:T(8,128)(2,1)} %refs_5_.3) | copy-start | bytes 3538948
  65.8 6.9 %collective-permute-start.7 = (bf16[128,768]{1,0:T(8,128)(2,1)S(1)}, bf16[128,768]{1,0:T(8,128)(2,1)S(1)}, u32[]{:S(2)}, u32[]{:S(2)}) collective-permute-start(bf16[128,768]{1,0:T(8,128)(2,1)S(1)} %slice.15), channel_id=1, source_target_pairs={{0,1},{1,2},{2,3},{3,0},{4,5},{5,6},{6,7},{7,4},{8,9},{9,10},{10,1... | collective-permute-start | bytes 589832 | tf_op jit(solution)/shard_map/ppermute | solution.py:373
  67.4 7.8 %collective-permute-start.9 = (bf16[128,768]{1,0:T(8,128)(2,1)S(1)}, bf16[128,768]{1,0:T(8,128)(2,1)S(1)}, u32[]{:S(2)}, u32[]{:S(2)}) collective-permute-start(bf16[128,768]{1,0:T(8,128)(2,1)S(1)} %slice.16), channel_id=1, source_target_pairs={{0,3},{1,0},{2,1},{3,2},{4,7},{5,4},{6,5},{7,6},{8,11},{9,8},{10,9... | collective-permute-start | bytes 589832 | tf_op jit(solution)/shard_map/ppermute | solution.py:374
  68.3 7.0 %copy-start.7 = (bf16[768,768]{1,0:T(8,128)(2,1)S(1)}, bf16[768,768]{1,0:T(8,128)(2,1)}, u32[]{:S(2)}) copy-start(bf16[768,768]{1,0:T(8,128)(2,1)} %refs_6_.3) | copy-start | bytes 3538948
  68.3 7.0 %copy-start.8 = (f32[256,768]{1,0:T(8,128)S(1)}, f32[256,768]{1,0:T(8,128)}, u32[]{:S(2)}) copy-start(f32[256,768]{1,0:T(8,128)} %self_others.1.refs_10_) | copy-start | bytes 2359300
